TPU v7x, 32 devices: a whole 2x2x4 slice. The times are simulated.
32 devices in a mesh: depth: 4 (over y, x), gx: 8 (over z, core).
Axes of the slice: x: 2, y: 2, z: 4, core: 2. Of those that a mesh axis runs over, the one named last changes fastest.
Arguments:
- offset_image: bfloat16 [64, 64, 32, 256], P(None, 'depth', 'gx'), may hold values from -6 to 6
- dip_class: int32 [64, 32, 256], P('depth', 'gx'), may hold values from 0 to 7
- slant_taper: bfloat16 [64, 64, 33], replicated, may hold values from -0.3125 to 0.3125
- band_offsets: int32 [64], replicated, may hold values from -14 to 14
- coefficients: float32 [8, 27], replicated, may hold values from -1.25 to 1.25
Outputs:
- smoothed: bfloat16 [64, 64, 32, 256], P(None, 'depth', 'gx')
All inputs are finite; a program needn't handle non-finite values.
Results may differ from a plain program's by a relative error of at most 0.0049.
Values may be sent and summed in bfloat16 or wider, within the bound.
A program may use at most 64 MiB of HBM per device.

v0:
```python
import jax
import jax.numpy as jnp
from jax import lax
from jax.sharding import PartitionSpec as P

R = 16
BAND = 2
RX = 4
RY = 1


def with_halo(x, sides, width):
    for axis, dim in sides:
        count, length = (lax.axis_size(axis), x.shape[dim])
        up = [(i, (i + 1) % count) for i in range(count - 1)]
        down = [(j, i) for i, j in up]
        last = lax.slice_in_dim(x, length - width, length, axis=dim)
        leading = lax.slice_in_dim(x, 0, width, axis=dim)
        before = lax.ppermute(last, axis, up)
        after = lax.ppermute(leading, axis, down)
        x = jnp.concatenate([before, x, after], axis=dim)
    return x


def slant_matrix_of(slant_taper, band_offsets, offset_count):
    offset_index = jnp.arange(offset_count, dtype=jnp.int32)
    depth_shift = jnp.floor_divide(band_offsets[:, None] * offset_index[None, :], offset_count)
    reach_index = jnp.arange(slant_taper.shape[2], dtype=jnp.int32) - R
    inside_band = jnp.abs(reach_index[None, None, :] - depth_shift[:, :, None]) <= BAND
    return jnp.where(inside_band, slant_taper, jnp.zeros_like(slant_taper))


def slant_stack(slant_matrix, padded, depth_cells):

    def one_depth(depth_level):
        window = lax.dynamic_slice_in_dim(padded, depth_level, 2 * R + 1, 1)
        result = jnp.einsum(
            "ahd,hdxy->axy", slant_matrix, window, preferred_element_type=jnp.float32
        )
        return result.astype(jnp.bfloat16)

    return lax.map(one_depth, jnp.arange(depth_cells, dtype=jnp.int32))


def dip_weights(dip_class, coefficients):
    class_index = jnp.arange(coefficients.shape[0], dtype=jnp.int32)
    onehot = (dip_class[None] == class_index[:, None, None, None]).astype(jnp.float32)
    return jnp.einsum("qt,qzxy->tzxy", coefficients, onehot, precision=lax.Precision.HIGHEST)


def smooth_all(gathers, tap_weights, lateral_cells, cross_cells):
    padded_rows = jnp.pad(gathers, ((0, 0), (0, 0), (0, 0), (RY, RY)))
    running = jnp.zeros(
        (gathers.shape[0], gathers.shape[1], lateral_cells, cross_cells), jnp.float32
    )
    for column_step in range(2 * RX + 1):
        for row_step in range(2 * RY + 1):
            tap_index = column_step * (2 * RY + 1) + row_step
            shifted = padded_rows[
                :, :, column_step : column_step + lateral_cells, row_step : row_step + cross_cells
            ]
            running = running + tap_weights[tap_index][:, None] * shifted.astype(jnp.float32)
    return jnp.moveaxis(running.astype(jnp.bfloat16), 0, 1)


def depth_extend(offset_image, offset_count):
    group_size = offset_count // 4
    extended_groups = []
    for first_offset in range(0, offset_count, group_size):
        final_offset = first_offset + group_size - 1
        reach_rows = min(R, -(-(R - BAND) * final_offset // offset_count) + BAND)
        offset_group = offset_image[first_offset : first_offset + group_size]
        extended = with_halo(offset_group, (("depth", 1),), reach_rows)
        extended = jnp.pad(extended, ((0, 0), (R - reach_rows, R - reach_rows), (0, 0), (0, 0)))
        extended_groups.append(extended)
    return jnp.concatenate(extended_groups, axis=0)


def local(offset_image, dip_class, slant_taper, band_offsets, coefficients):
    offset_count, depth_cells, lateral_cells, cross_cells = offset_image.shape
    slant_matrix = slant_matrix_of(slant_taper, band_offsets, offset_count)
    padded = depth_extend(offset_image, offset_count)
    local_gathers = slant_stack(slant_matrix, padded, depth_cells)
    gathers = with_halo(local_gathers, (("gx", 2),), RX)
    tap_weights = dip_weights(dip_class, coefficients)
    return smooth_all(gathers, tap_weights, lateral_cells, cross_cells)


def solution(mesh):
    return jax.shard_map(
        local,
        mesh=mesh,
        in_specs=(P(None, "depth", "gx", None), P("depth", "gx", None), P(), P(), P()),
        out_specs=P(None, "depth", "gx", None),
        check_vma=False,
    )
```

profile of v0, /device:TPU:13, one launch (start us, length us, event | category | flops | bytes accessed | tf_op | source)
XLA Modules:
  0.0 273.9 jit_solution(16348860424145212145)
XLA Ops:
  0.0 1.3 fusion.50
  1.3 0.7 copy.55
  2.0 3.1 %collective-permute-start.1 = (bf16[16,6,4,256]{3,0,1,2:T(8,128)(2,1)}, bf16[16,6,4,256]{3,0,1,2:T(8,128)(2,1)}, u32[]{:S(2)}, u32[]{:S(2)}) collective-permute-start(bf16[16,6,4,256]{3,0,1,2:T(8,128)(2,1)} %copy.55), channel_id=1, source_target_pairs={{8,0},{16,8},{24,16},{9,1},{17,9},{25,17},{10,2},{18,10},{26,18},{... | collective-permute-start | bytes 589832 | tf_op jit(solution)/shard_map/ppermute | solution.py:20
  5.1 0.7 copy.53
  5.8 2.9 %collective-permute-start = (bf16[16,6,4,256]{3,0,1,2:T(8,128)(2,1)}, bf16[16,6,4,256]{3,0,1,2:T(8,128)(2,1)}, u32[]{:S(2)}, u32[]{:S(2)}) collective-permute-start(bf16[16,6,4,256]{3,0,1,2:T(8,128)(2,1)} %copy.53), channel_id=1, source_target_pairs={{0,8},{8,16},{16,24},{1,9},{9,17},{17,25},{2,10},{10,18},{18,26},{... | collective-permute-start | bytes 589832 | tf_op jit(solution)/shard_map/ppermute | solution.py:19
  8.7 1.3 fusion.52
  10.0 0.7 copy.58
  10.7 3.3 %collective-permute-start.3 = (bf16[16,9,4,256]{3,0,1,2:T(8,128)(2,1)}, bf16[16,9,4,256]{3,0,1,2:T(8,128)(2,1)}, u32[]{:S(2)}, u32[]{:S(2)}) collective-permute-start(bf16[16,9,4,256]{3,0,1,2:T(8,128)(2,1)} %copy.58), channel_id=1, source_target_pairs={{8,0},{16,8},{24,16},{9,1},{17,9},{25,17},{10,2},{18,10},{26,18},{... | collective-permute-start | bytes 884744 | tf_op jit(solution)/shard_map/ppermute | solution.py:20
  14.0 2.7 collective-permute-start.2
  16.8 1.0 fusion.53
  17.8 0.8 copy.61
  18.6 3.5 %collective-permute-start.5 = (bf16[16,13,4,256]{3,0,1,2:T(8,128)(2,1)}, bf16[16,13,4,256]{3,0,1,2:T(8,128)(2,1)}, u32[]{:S(2)}, u32[]{:S(2)}) collective-permute-start(bf16[16,13,4,256]{3,0,1,2:T(8,128)(2,1)} %copy.61), channel_id=1, source_target_pairs={{8,0},{16,8},{24,16},{9,1},{17,9},{25,17},{10,2},{18,10},{26,18},{... | collective-permute-start | bytes 1277960 | tf_op jit(solution)/shard_map/ppermute | solution.py:20
  22.1 1.0 convolution_bitcast_fusion
  23.2 1.0 fusion.49
  24.2 1.8 fusion.48
  26.0 1.8 fusion.51
  28.0 0.7 copy_bitcast_fusion.24
  28.6 0.7 copy_bitcast_fusion.18
  29.7 0.7 copy_bitcast_fusion.20
  30.4 1.1 copy.59
  31.4 1.3 copy.54
  32.8 1.3 copy.62
  34.1 1.3 copy.60
  35.7 2.5 collective-permute-start.4
  38.3 3.7 %collective-permute-start.7 = (bf16[16,16,4,256]{3,0,1,2:T(8,128)(2,1)S(1)}, bf16[16,16,4,256]{3,0,1,2:T(8,128)(2,1)S(1)}, u32[]{:S(2)}, u32[]{:S(2)}) collective-permute-start(bf16[16,16,4,256]{3,0,1,2:T(8,128)(2,1)S(1)} %copy.62), channel_id=1, source_target_pairs={{8,0},{16,8},{24,16},{9,1},{17,9},{25,17},{10,2},{18,10},{26,18},{... | collective-permute-start | bytes 1572872 | tf_op jit(solution)/shard_map/ppermute | solution.py:20
  42.0 1.2 fusion.37
  43.1 1.9 collective-permute-start.6
  45.1 1.2 fusion.39
  46.3 1.5 collective-permute-done.4
  47.8 1.1 fusion.41
  48.9 7.6 %collective-permute-done.7 = bf16[16,16,4,256]{3,0,1,2:T(8,128)(2,1)S(1)} collective-permute-done((bf16[16,16,4,256]{3,0,1,2:T(8,128)(2,1)S(1)}, bf16[16,16,4,256]{3,0,1,2:T(8,128)(2,1)S(1)}, u32[]{:S(2)}, u32[]{:S(2)}) %collective-permute-start.7) | collective-permute-done | bytes 524320 | tf_op jit(solution)/shard_map/ppermute | solution.py:20
  56.5 13.7 %collective-permute-done.6 = bf16[16,16,4,256]{3,0,1,2:T(8,128)(2,1)S(1)} collective-permute-done((bf16[16,16,4,256]{3,0,1,2:T(8,128)(2,1)S(1)}, bf16[16,16,4,256]{3,0,1,2:T(8,128)(2,1)S(1)}, u32[]{:S(2)}, u32[]{:S(2)}) %collective-permute-start.6) | collective-permute-done | bytes 524320 | tf_op jit(solution)/shard_map/ppermute | solution.py:19
  70.2 3.3 %maximum_maximum_fusion = bf16[64,48,4,256]{3,0,1,2:T(8,128)(2,1)} fusion(bf16[16,16,4,256]{3,0,1,2:T(8,128)(2,1)S(1)} %collective-permute-done.7, bf16[16,16,4,256]{3,0,1,2:T(8,128)(2,1)S(1)} %copy.62, bf16[16,16,4,256]{3,0,1,2:T(8,128)(2,1)S(1)} %collective-permute-done.6, bf16[16,48,4,256]{3,0,1,2:T(8,128)(2,1)S(1)} %fusion.41, ...), kind=kLoop, calls=%fused_computation.16 | loop fusion | flops 37748736 | bytes 12582912 | tf_op jit(solution)/shard_map/concatenate | solution.py:76
  73.6 93.4 %while.10 = (s32[]{:T(128)}, bf16[16,64,4,256]{3,2,0,1:T(4,128)(2,1)S(1)}, s32[16]{0:T(128)S(1)}, bf16[64,48,4,256]{3,0,1,2:T(8,128)(2,1)}, bf16[64,64,33]{1,0,2...) while((s32[]{:T(128)}, bf16[16,64,4,256]{3,2,0,1:T(4,128)(2,1)S(1)}, s32[16]{0:T(128)S(1)}, ...), condition=%wide.region_1.2_spmd, body=%wide.region_0.1_spmd.sunk | while | flops 276889600 | bytes 4989075 | solution.py:42
  76.1 3.1 %fusion.59 = bf16[1,64,4,256]{3,1,2,0:T(8,128)(2,1)S(1)} fusion(bf16[64,48,4,256]{3,0,1,2:T(8,128)(2,1)} %get-tuple-element.156, s32[]{:T(128)S(6)} %select_n.21, bf16[64,64,33]{1,0,2:T(8,128)(2,1)S(1)} %get-tuple-element.157), kind=kOutput, calls=%fused_computation.4.clone.1 | convolution fusion | flops 276889600 | bytes 4726788 | tf_op jit(solution)/shard_map/while/body/eval_jaxpr/ahd,hdxy->axy/dot_general | solution.py:37
  82.0 3.1 %fusion.59 = bf16[1,64,4,256]{3,1,2,0:T(8,128)(2,1)S(1)} fusion(bf16[64,48,4,256]{3,0,1,2:T(8,128)(2,1)} %get-tuple-element.156, s32[]{:T(128)S(6)} %select_n.21, bf16[64,64,33]{1,0,2:T(8,128)(2,1)S(1)} %get-tuple-element.157), kind=kOutput, calls=%fused_computation.4.clone.1 | convolution fusion | flops 276889600 | bytes 4726788 | tf_op jit(solution)/shard_map/while/body/eval_jaxpr/ahd,hdxy->axy/dot_general | solution.py:37
  87.8 3.1 %fusion.59 = bf16[1,64,4,256]{3,1,2,0:T(8,128)(2,1)S(1)} fusion(bf16[64,48,4,256]{3,0,1,2:T(8,128)(2,1)} %get-tuple-element.156, s32[]{:T(128)S(6)} %select_n.21, bf16[64,64,33]{1,0,2:T(8,128)(2,1)S(1)} %get-tuple-element.157), kind=kOutput, calls=%fused_computation.4.clone.1 | convolution fusion | flops 276889600 | bytes 4726788 | tf_op jit(solution)/shard_map/while/body/eval_jaxpr/ahd,hdxy->axy/dot_general | solution.py:37
  93.7 3.1 %fusion.59 = bf16[1,64,4,256]{3,1,2,0:T(8,128)(2,1)S(1)} fusion(bf16[64,48,4,256]{3,0,1,2:T(8,128)(2,1)} %get-tuple-element.156, s32[]{:T(128)S(6)} %select_n.21, bf16[64,64,33]{1,0,2:T(8,128)(2,1)S(1)} %get-tuple-element.157), kind=kOutput, calls=%fused_computation.4.clone.1 | convolution fusion | flops 276889600 | bytes 4726788 | tf_op jit(solution)/shard_map/while/body/eval_jaxpr/ahd,hdxy->axy/dot_general | solution.py:37
  99.5 3.1 %fusion.59 = bf16[1,64,4,256]{3,1,2,0:T(8,128)(2,1)S(1)} fusion(bf16[64,48,4,256]{3,0,1,2:T(8,128)(2,1)} %get-tuple-element.156, s32[]{:T(128)S(6)} %select_n.21, bf16[64,64,33]{1,0,2:T(8,128)(2,1)S(1)} %get-tuple-element.157), kind=kOutput, calls=%fused_computation.4.clone.1 | convolution fusion | flops 276889600 | bytes 4726788 | tf_op jit(solution)/shard_map/while/body/eval_jaxpr/ahd,hdxy->axy/dot_general | solution.py:37
  105.3 3.1 %fusion.59 = bf16[1,64,4,256]{3,1,2,0:T(8,128)(2,1)S(1)} fusion(bf16[64,48,4,256]{3,0,1,2:T(8,128)(2,1)} %get-tuple-element.156, s32[]{:T(128)S(6)} %select_n.21, bf16[64,64,33]{1,0,2:T(8,128)(2,1)S(1)} %get-tuple-element.157), kind=kOutput, calls=%fused_computation.4.clone.1 | convolution fusion | flops 276889600 | bytes 4726788 | tf_op jit(solution)/shard_map/while/body/eval_jaxpr/ahd,hdxy->axy/dot_general | solution.py:37
  111.2 3.1 %fusion.59 = bf16[1,64,4,256]{3,1,2,0:T(8,128)(2,1)S(1)} fusion(bf16[64,48,4,256]{3,0,1,2:T(8,128)(2,1)} %get-tuple-element.156, s32[]{:T(128)S(6)} %select_n.21, bf16[64,64,33]{1,0,2:T(8,128)(2,1)S(1)} %get-tuple-element.157), kind=kOutput, calls=%fused_computation.4.clone.1 | convolution fusion | flops 276889600 | bytes 4726788 | tf_op jit(solution)/shard_map/while/body/eval_jaxpr/ahd,hdxy->axy/dot_general | solution.py:37
  117.0 3.1 %fusion.59 = bf16[1,64,4,256]{3,1,2,0:T(8,128)(2,1)S(1)} fusion(bf16[64,48,4,256]{3,0,1,2:T(8,128)(2,1)} %get-tuple-element.156, s32[]{:T(128)S(6)} %select_n.21, bf16[64,64,33]{1,0,2:T(8,128)(2,1)S(1)} %get-tuple-element.157), kind=kOutput, calls=%fused_computation.4.clone.1 | convolution fusion | flops 276889600 | bytes 4726788 | tf_op jit(solution)/shard_map/while/body/eval_jaxpr/ahd,hdxy->axy/dot_general | solution.py:37
  122.9 3.1 %fusion.59 = bf16[1,64,4,256]{3,1,2,0:T(8,128)(2,1)S(1)} fusion(bf16[64,48,4,256]{3,0,1,2:T(8,128)(2,1)} %get-tuple-element.156, s32[]{:T(128)S(6)} %select_n.21, bf16[64,64,33]{1,0,2:T(8,128)(2,1)S(1)} %get-tuple-element.157), kind=kOutput, calls=%fused_computation.4.clone.1 | convolution fusion | flops 276889600 | bytes 4726788 | tf_op jit(solution)/shard_map/while/body/eval_jaxpr/ahd,hdxy->axy/dot_general | solution.py:37
  128.7 3.1 %fusion.59 = bf16[1,64,4,256]{3,1,2,0:T(8,128)(2,1)S(1)} fusion(bf16[64,48,4,256]{3,0,1,2:T(8,128)(2,1)} %get-tuple-element.156, s32[]{:T(128)S(6)} %select_n.21, bf16[64,64,33]{1,0,2:T(8,128)(2,1)S(1)} %get-tuple-element.157), kind=kOutput, calls=%fused_computation.4.clone.1 | convolution fusion | flops 276889600 | bytes 4726788 | tf_op jit(solution)/shard_map/while/body/eval_jaxpr/ahd,hdxy->axy/dot_general | solution.py:37
  134.5 3.1 %fusion.59 = bf16[1,64,4,256]{3,1,2,0:T(8,128)(2,1)S(1)} fusion(bf16[64,48,4,256]{3,0,1,2:T(8,128)(2,1)} %get-tuple-element.156, s32[]{:T(128)S(6)} %select_n.21, bf16[64,64,33]{1,0,2:T(8,128)(2,1)S(1)} %get-tuple-element.157), kind=kOutput, calls=%fused_computation.4.clone.1 | convolution fusion | flops 276889600 | bytes 4726788 | tf_op jit(solution)/shard_map/while/body/eval_jaxpr/ahd,hdxy->axy/dot_general | solution.py:37
  140.4 3.1 %fusion.59 = bf16[1,64,4,256]{3,1,2,0:T(8,128)(2,1)S(1)} fusion(bf16[64,48,4,256]{3,0,1,2:T(8,128)(2,1)} %get-tuple-element.156, s32[]{:T(128)S(6)} %select_n.21, bf16[64,64,33]{1,0,2:T(8,128)(2,1)S(1)} %get-tuple-element.157), kind=kOutput, calls=%fused_computation.4.clone.1 | convolution fusion | flops 276889600 | bytes 4726788 | tf_op jit(solution)/shard_map/while/body/eval_jaxpr/ahd,hdxy->axy/dot_general | solution.py:37
  146.2 3.1 %fusion.59 = bf16[1,64,4,256]{3,1,2,0:T(8,128)(2,1)S(1)} fusion(bf16[64,48,4,256]{3,0,1,2:T(8,128)(2,1)} %get-tuple-element.156, s32[]{:T(128)S(6)} %select_n.21, bf16[64,64,33]{1,0,2:T(8,128)(2,1)S(1)} %get-tuple-element.157), kind=kOutput, calls=%fused_computation.4.clone.1 | convolution fusion | flops 276889600 | bytes 4726788 | tf_op jit(solution)/shard_map/while/body/eval_jaxpr/ahd,hdxy->axy/dot_general | solution.py:37
  152.1 3.1 %fusion.59 = bf16[1,64,4,256]{3,1,2,0:T(8,128)(2,1)S(1)} fusion(bf16[64,48,4,256]{3,0,1,2:T(8,128)(2,1)} %get-tuple-element.156, s32[]{:T(128)S(6)} %select_n.21, bf16[64,64,33]{1,0,2:T(8,128)(2,1)S(1)} %get-tuple-element.157), kind=kOutput, calls=%fused_computation.4.clone.1 | convolution fusion | flops 276889600 | bytes 4726788 | tf_op jit(solution)/shard_map/while/body/eval_jaxpr/ahd,hdxy->axy/dot_general | solution.py:37
  157.9 3.1 %fusion.59 = bf16[1,64,4,256]{3,1,2,0:T(8,128)(2,1)S(1)} fusion(bf16[64,48,4,256]{3,0,1,2:T(8,128)(2,1)} %get-tuple-element.156, s32[]{:T(128)S(6)} %select_n.21, bf16[64,64,33]{1,0,2:T(8,128)(2,1)S(1)} %get-tuple-element.157), kind=kOutput, calls=%fused_computation.4.clone.1 | convolution fusion | flops 276889600 | bytes 4726788 | tf_op jit(solution)/shard_map/while/body/eval_jaxpr/ahd,hdxy->axy/dot_general | solution.py:37
  163.7 3.1 %fusion.59 = bf16[1,64,4,256]{3,1,2,0:T(8,128)(2,1)S(1)} fusion(bf16[64,48,4,256]{3,0,1,2:T(8,128)(2,1)} %get-tuple-element.156, s32[]{:T(128)S(6)} %select_n.21, bf16[64,64,33]{1,0,2:T(8,128)(2,1)S(1)} %get-tuple-element.157), kind=kOutput, calls=%fused_computation.4.clone.1 | convolution fusion | flops 276889600 | bytes 4726788 | tf_op jit(solution)/shard_map/while/body/eval_jaxpr/ahd,hdxy->axy/dot_general | solution.py:37
  167.0 6.1 %collective-permute-start.8 = (bf16[16,64,4,256]{3,2,0,1:T(4,128)(2,1)S(1)}, bf16[16,64,4,256]{3,2,0,1:T(4,128)(2,1)S(1)}, u32[]{:S(2)}, u32[]{:S(2)}) collective-permute-start(bf16[16,64,4,256]{3,2,0,1:T(4,128)(2,1)S(1)} %get-tuple-element.32), channel_id=1, source_target_pairs={{0,1},{1,2},{2,3},{3,4},{4,5},{5,6},{6,7},{8,9},{9,10},{10,11},{11... | collective-permute-start | bytes 6291464 | tf_op jit(solution)/shard_map/ppermute | solution.py:19
  173.2 2.1 collective-permute-start.9
  175.4 0.9 copy_bitcast_fusion.2
  176.3 1.6 copy_bitcast_fusion.4
  177.9 1.6 copy_bitcast_fusion.6
  179.5 1.6 copy_bitcast_fusion.8
  181.1 1.6 copy_bitcast_fusion.10
  182.6 1.5 copy_bitcast_fusion.12
  184.1 0.7 copy_bitcast_fusion.14
  184.9 0.7 copy_bitcast_fusion.16
  185.6 10.6 %collective-permute-done.8 = bf16[16,64,4,256]{3,2,0,1:T(4,128)(2,1)S(1)} collective-permute-done((bf16[16,64,4,256]{3,2,0,1:T(4,128)(2,1)S(1)}, bf16[16,64,4,256]{3,2,0,1:T(4,128)(2,1)S(1)}, u32[]{:S(2)}, u32[]{:S(2)}) %collective-permute-start.8) | collective-permute-done | bytes 2097184 | tf_op jit(solution)/shard_map/ppermute | solution.py:19
  196.1 4.4 %collective-permute-done.9 = bf16[16,64,4,256]{3,2,0,1:T(4,128)(2,1)S(1)} collective-permute-done((bf16[16,64,4,256]{3,2,0,1:T(4,128)(2,1)S(1)}, bf16[16,64,4,256]{3,2,0,1:T(4,128)(2,1)S(1)}, u32[]{:S(2)}, u32[]{:S(2)}) %collective-permute-start.9) | collective-permute-done | bytes 2097184 | tf_op jit(solution)/shard_map/ppermute | solution.py:20
  200.5 16.2 %fusion.18 = bf16[16,64,12,258]{3,2,0,1:T(8,128)(2,1)S(1)} fusion(bf16[16,64,4,256]{3,2,0,1:T(4,128)(2,1)S(1)} %collective-permute-done.9, bf16[16,64,4,256]{3,2,0,1:T(4,128)(2,1)} %copy-done.3, bf16[16,64,4,256]{3,2,0,1:T(4,128)(2,1)S(1)} %collective-permute-done.8), kind=kLoop, calls=%fused_computation.15 | loop fusion | flops 38043648 | bytes 12632064 | tf_op jit(solution)/shard_map/concatenate | solution.py:21
  216.8 56.9 %fusion.26 = bf16[64,16,4,256]{3,2,1,0:T(4,128)(2,1)} fusion(bf16[16,64,12,258]{3,2,0,1:T(8,128)(2,1)S(1)} %fusion.18, f32[16,4,256]{2,1,0:T(4,128)S(1)} %get-tuple-element.80, bf16[16,64,4,256]{3,2,0,1:T(4,128)(2,1)} %copy-done.2, f32[16,4,256]{2,1,0:T(4,128)S(1)} %get-tuple-element.81, f32[16,4,256]{2,1,0:T(4,128)S(1)} %get-tuple-element.82, ...), kind=kLoop, calls=%fused_computation.41 | loop fusion | flops 103809024 | bytes 47906816 | tf_op jit(solution)/shard_map/transpose | solution.py:63
  (97 shorter events, 12.5 us)
Async XLA Ops:
  0.0 22.1 %copy-start = (f32[8,27]{1,0:T(8,128)S(1)}, f32[8,27]{1,0:T(8,128)}, u32[]{:S(2)}) copy-start(f32[8,27]{1,0:T(8,128)} %param.11) | copy-start | bytes 2596
  0.0 16.7 %copy-start.4 = (bf16[64,16,4,256]{3,2,1,0:T(4,128)(2,1)S(1)}, bf16[64,16,4,256]{3,2,1,0:T(4,128)(2,1)}, u32[]{:S(2)}) copy-start(bf16[64,16,4,256]{3,2,1,0:T(4,128)(2,1)} %param.7) | copy-start | bytes 6291460
  0.0 22.1 %copy-start.23 = (s32[16,4,256]{2,1,0:T(4,128)S(1)}, s32[16,4,256]{2,1,0:T(4,128)}, u32[]{:S(2)}) copy-start(s32[16,4,256]{2,1,0:T(4,128)} %param.8) | copy-start | bytes 196612
  2.0 33.7 %collective-permute-start.1 = (bf16[16,6,4,256]{3,0,1,2:T(8,128)(2,1)}, bf16[16,6,4,256]{3,0,1,2:T(8,128)(2,1)}, u32[]{:S(2)}, u32[]{:S(2)}) collective-permute-start(bf16[16,6,4,256]{3,0,1,2:T(8,128)(2,1)} %copy.55), channel_id=1, source_target_pairs={{8,0},{16,8},{24,16},{9,1},{17,9},{25,17},{10,2},{18,10},{26,18},{... | collective-permute-start | bytes 589832 | tf_op jit(solution)/shard_map/ppermute | solution.py:20
  5.8 32.5 %collective-permute-start = (bf16[16,6,4,256]{3,0,1,2:T(8,128)(2,1)}, bf16[16,6,4,256]{3,0,1,2:T(8,128)(2,1)}, u32[]{:S(2)}, u32[]{:S(2)}) collective-permute-start(bf16[16,6,4,256]{3,0,1,2:T(8,128)(2,1)} %copy.53), channel_id=1, source_target_pairs={{0,8},{8,16},{16,24},{1,9},{9,17},{17,25},{2,10},{10,18},{18,26},{... | collective-permute-start | bytes 589832 | tf_op jit(solution)/shard_map/ppermute | solution.py:19
  10.7 32.4 %collective-permute-start.3 = (bf16[16,9,4,256]{3,0,1,2:T(8,128)(2,1)}, bf16[16,9,4,256]{3,0,1,2:T(8,128)(2,1)}, u32[]{:S(2)}, u32[]{:S(2)}) collective-permute-start(bf16[16,9,4,256]{3,0,1,2:T(8,128)(2,1)} %copy.58), channel_id=1, source_target_pairs={{8,0},{16,8},{24,16},{9,1},{17,9},{25,17},{10,2},{18,10},{26,18},{... | collective-permute-start | bytes 884744 | tf_op jit(solution)/shard_map/ppermute | solution.py:20
  14.0 31.0 %collective-permute-start.2 = (bf16[16,9,4,256]{3,0,1,2:T(8,128)(2,1)S(1)}, bf16[16,9,4,256]{3,0,1,2:T(8,128)(2,1)}, u32[]{:S(2)}, u32[]{:S(2)}) collective-permute-start(bf16[16,9,4,256]{3,0,1,2:T(8,128)(2,1)S(1)} %copy.56), channel_id=1, source_target_pairs={{0,8},{8,16},{16,24},{1,9},{9,17},{17,25},{2,10},{10,18},{18,26},{... | collective-permute-start | bytes 884744 | tf_op jit(solution)/shard_map/ppermute | solution.py:19
  18.6 27.6 %collective-permute-start.5 = (bf16[16,13,4,256]{3,0,1,2:T(8,128)(2,1)}, bf16[16,13,4,256]{3,0,1,2:T(8,128)(2,1)}, u32[]{:S(2)}, u32[]{:S(2)}) collective-permute-start(bf16[16,13,4,256]{3,0,1,2:T(8,128)(2,1)} %copy.61), channel_id=1, source_target_pairs={{8,0},{16,8},{24,16},{9,1},{17,9},{25,17},{10,2},{18,10},{26,18},{... | collective-permute-start | bytes 1277960 | tf_op jit(solution)/shard_map/ppermute | solution.py:20
  23.2 4.7 %copy-start.24 = (s32[64]{0:T(128)S(1)}, s32[64]{0:T(128)}, u32[]{:S(2)}) copy-start(s32[64]{0:T(128)} %param.10) | copy-start | bytes 772
  23.2 6.2 %copy-start.5 = (bf16[64,64,33]{1,0,2:T(8,128)(2,1)S(1)}, bf16[64,64,33]{1,0,2:T(8,128)(2,1)}, u32[]{:S(2)}) copy-start(bf16[64,64,33]{1,0,2:T(8,128)(2,1)} %param.9) | copy-start | bytes 811012
  35.7 12.0 %collective-permute-start.4 = (bf16[16,13,4,256]{3,0,1,2:T(8,128)(2,1)S(1)}, bf16[16,13,4,256]{3,0,1,2:T(8,128)(2,1)S(1)}, u32[]{:S(2)}, u32[]{:S(2)}) collective-permute-start(bf16[16,13,4,256]{3,0,1,2:T(8,128)(2,1)S(1)} %copy.59), channel_id=1, source_target_pairs={{0,8},{8,16},{16,24},{1,9},{9,17},{17,25},{2,10},{10,18},{18,26},{... | collective-permute-start | bytes 1277960 | tf_op jit(solution)/shard_map/ppermute | solution.py:19
  38.3 18.2 %collective-permute-start.7 = (bf16[16,16,4,256]{3,0,1,2:T(8,128)(2,1)S(1)}, bf16[16,16,4,256]{3,0,1,2:T(8,128)(2,1)S(1)}, u32[]{:S(2)}, u32[]{:S(2)}) collective-permute-start(bf16[16,16,4,256]{3,0,1,2:T(8,128)(2,1)S(1)} %copy.62), channel_id=1, source_target_pairs={{8,0},{16,8},{24,16},{9,1},{17,9},{25,17},{10,2},{18,10},{26,18},{... | collective-permute-start | bytes 1572872 | tf_op jit(solution)/shard_map/ppermute | solution.py:20
  43.1 27.1 %collective-permute-start.6 = (bf16[16,16,4,256]{3,0,1,2:T(8,128)(2,1)S(1)}, bf16[16,16,4,256]{3,0,1,2:T(8,128)(2,1)S(1)}, u32[]{:S(2)}, u32[]{:S(2)}) collective-permute-start(bf16[16,16,4,256]{3,0,1,2:T(8,128)(2,1)S(1)} %copy.62), channel_id=1, source_target_pairs={{0,8},{8,16},{16,24},{1,9},{9,17},{17,25},{2,10},{10,18},{18,26},{... | collective-permute-start | bytes 1572872 | tf_op jit(solution)/shard_map/ppermute | solution.py:19
  73.5 101.8 %copy-start.21 = (f32[1,16,4,256]{3,0,2,1:T(1,128)S(1)}, f32[1,16,4,256]{3,0,2,1:T(1,128)}, u32[]{:S(2)}) copy-start(f32[1,16,4,256]{3,0,2,1:T(1,128)} %get-tuple-element.67) | copy-start | bytes 196612
  73.5 101.8 %copy-start.22 = (f32[1,16,4,256]{3,0,2,1:T(1,128)S(1)}, f32[1,16,4,256]{3,0,2,1:T(1,128)}, u32[]{:S(2)}) copy-start(f32[1,16,4,256]{3,0,2,1:T(1,128)} %get-tuple-element.68) | copy-start | bytes 196612
  73.5 101.8 %copy-start.13 = (f32[1,16,4,256]{3,0,2,1:T(1,128)S(1)}, f32[1,16,4,256]{3,0,2,1:T(1,128)}, u32[]{:S(2)}) copy-start(f32[1,16,4,256]{3,0,2,1:T(1,128)} %get-tuple-element.43) | copy-start | bytes 196612
  73.5 101.8 %copy-start.19 = (f32[1,16,4,256]{3,0,2,1:T(1,128)S(1)}, f32[1,16,4,256]{3,0,2,1:T(1,128)}, u32[]{:S(2)}) copy-start(f32[1,16,4,256]{3,0,2,1:T(1,128)} %get-tuple-element.44) | copy-start | bytes 196612
  73.5 101.8 %copy-start.20 = (f32[1,16,4,256]{3,0,2,1:T(1,128)S(1)}, f32[1,16,4,256]{3,0,2,1:T(1,128)}, u32[]{:S(2)}) copy-start(f32[1,16,4,256]{3,0,2,1:T(1,128)} %get-tuple-element.45) | copy-start | bytes 196612
  73.5 109.1 %copy-start.18 = (f32[1,16,4,256]{3,0,2,1:T(1,128)S(1)}, f32[1,16,4,256]{3,0,2,1:T(1,128)}, u32[]{:S(2)}) copy-start(f32[1,16,4,256]{3,0,2,1:T(1,128)} %get-tuple-element.56) | copy-start | bytes 196612
  73.6 110.6 %copy-start.16 = (f32[1,16,4,256]{3,0,2,1:T(1,128)S(1)}, f32[1,16,4,256]{3,0,2,1:T(1,128)}, u32[]{:S(2)}) copy-start(f32[1,16,4,256]{3,0,2,1:T(1,128)} %get-tuple-element.58) | copy-start | bytes 196612
  73.6 110.6 %copy-start.17 = (f32[1,16,4,256]{3,0,2,1:T(1,128)S(1)}, f32[1,16,4,256]{3,0,2,1:T(1,128)}, u32[]{:S(2)}) copy-start(f32[1,16,4,256]{3,0,2,1:T(1,128)} %get-tuple-element.59) | copy-start | bytes 196612
  73.6 111.3 %copy-start.14 = (f32[1,16,4,256]{3,0,2,1:T(1,128)S(1)}, f32[1,16,4,256]{3,0,2,1:T(1,128)}, u32[]{:S(2)}) copy-start(f32[1,16,4,256]{3,0,2,1:T(1,128)} %get-tuple-element.60) | copy-start | bytes 196612
  73.6 111.3 %copy-start.15 = (f32[1,16,4,256]{3,0,2,1:T(1,128)S(1)}, f32[1,16,4,256]{3,0,2,1:T(1,128)}, u32[]{:S(2)}) copy-start(f32[1,16,4,256]{3,0,2,1:T(1,128)} %get-tuple-element.61) | copy-start | bytes 196612
  167.0 29.1 %copy-start.3 = (bf16[16,64,4,256]{3,2,0,1:T(4,128)(2,1)}, bf16[16,64,4,256]{3,2,0,1:T(4,128)(2,1)S(1)}, u32[]{:S(2)}) copy-start(bf16[16,64,4,256]{3,2,0,1:T(4,128)(2,1)S(1)} %get-tuple-element.32) | copy-start | bytes 6291460
  167.0 29.1 %collective-permute-start.8 = (bf16[16,64,4,256]{3,2,0,1:T(4,128)(2,1)S(1)}, bf16[16,64,4,256]{3,2,0,1:T(4,128)(2,1)S(1)}, u32[]{:S(2)}, u32[]{:S(2)}) collective-permute-start(bf16[16,64,4,256]{3,2,0,1:T(4,128)(2,1)S(1)} %get-tuple-element.32), channel_id=1, source_target_pairs={{0,1},{1,2},{2,3},{3,4},{4,5},{5,6},{6,7},{8,9},{9,10},{10,11},{11... | collective-permute-start | bytes 6291464 | tf_op jit(solution)/shard_map/ppermute | solution.py:19
  173.2 27.4 %collective-permute-start.9 = (bf16[16,64,4,256]{3,2,0,1:T(4,128)(2,1)S(1)}, bf16[16,64,4,256]{3,2,0,1:T(4,128)(2,1)S(1)}, u32[]{:S(2)}, u32[]{:S(2)}) collective-permute-start(bf16[16,64,4,256]{3,2,0,1:T(4,128)(2,1)S(1)} %get-tuple-element.32), channel_id=1, source_target_pairs={{1,0},{2,1},{3,2},{4,3},{5,4},{6,5},{7,6},{9,8},{10,9},{11,10},{12... | collective-permute-start | bytes 6291464 | tf_op jit(solution)/shard_map/ppermute | solution.py:20
  185.5 31.2 %copy-start.6 = (f32[16,4,256]{2,1,0:T(4,128)S(1)}, f32[16,4,256]{2,1,0:T(4,128)}, u32[]{:S(2)}) copy-start(f32[16,4,256]{2,1,0:T(4,128)} %get-tuple-element.105) | copy-start | bytes 196612
  185.5 31.2 %copy-start.7 = (f32[16,4,256]{2,1,0:T(4,128)S(1)}, f32[16,4,256]{2,1,0:T(4,128)}, u32[]{:S(2)}) copy-start(f32[16,4,256]{2,1,0:T(4,128)} %get-tuple-element.98) | copy-start | bytes 196612
  185.5 31.2 %copy-start.8 = (f32[16,4,256]{2,1,0:T(4,128)S(1)}, f32[16,4,256]{2,1,0:T(4,128)}, u32[]{:S(2)}) copy-start(f32[16,4,256]{2,1,0:T(4,128)} %get-tuple-element.99) | copy-start | bytes 196612
  185.5 31.2 %copy-start.9 = (f32[16,4,256]{2,1,0:T(4,128)S(1)}, f32[16,4,256]{2,1,0:T(4,128)}, u32[]{:S(2)}) copy-start(f32[16,4,256]{2,1,0:T(4,128)} %get-tuple-element.100) | copy-start | bytes 196612
  185.5 31.2 %copy-start.10 = (f32[16,4,256]{2,1,0:T(4,128)S(1)}, f32[16,4,256]{2,1,0:T(4,128)}, u32[]{:S(2)}) copy-start(f32[16,4,256]{2,1,0:T(4,128)} %get-tuple-element.101) | copy-start | bytes 196612
  196.1 20.6 %copy-start.1 = (bf16[16,64,4,256]{3,2,0,1:T(4,128)(2,1)}, bf16[16,64,4,256]{3,2,0,1:T(4,128)(2,1)S(1)}, u32[]{:S(2)}) copy-start(bf16[16,64,4,256]{3,2,0,1:T(4,128)(2,1)S(1)} %collective-permute-done.8) | copy-start | bytes 6291460
  200.5 16.2 %copy-start.2 = (bf16[16,64,4,256]{3,2,0,1:T(4,128)(2,1)}, bf16[16,64,4,256]{3,2,0,1:T(4,128)(2,1)S(1)}, u32[]{:S(2)}) copy-start(bf16[16,64,4,256]{3,2,0,1:T(4,128)(2,1)S(1)} %collective-permute-done.9) | copy-start | bytes 6291460
  200.5 16.2 %copy-start.11 = (f32[16,4,256]{2,1,0:T(4,128)S(1)}, f32[16,4,256]{2,1,0:T(4,128)}, u32[]{:S(2)}) copy-start(f32[16,4,256]{2,1,0:T(4,128)} %get-tuple-element.96) | copy-start | bytes 196612
  200.5 16.2 %copy-start.12 = (f32[16,4,256]{2,1,0:T(4,128)S(1)}, f32[16,4,256]{2,1,0:T(4,128)}, u32[]{:S(2)}) copy-start(f32[16,4,256]{2,1,0:T(4,128)} %get-tuple-element.97) | copy-start | bytes 196612
where the time goes:
time: 276 us; the launch traced here: 274 us
  other arithmetic  80.3 us (29%)
  matrix products  51.4 us (19%)
  local copies, waits for them, and re-layouts  40.5 us (15%)
  waiting for transfers between devices  37.8 us (14%)
  starting transfers between devices  31.7 us (11%)
  loops' own time  31.6 us (11%)
    transpose x1, other arithmetic, smooth_all(): return jnp.moveaxis(running.astype(jnp.bfloat16), 0, 1)  56.9 us
    dot_general x16, matrix products, one_depth(): jnp.einsum('ahd,hdxy->axy', slant_matrix, window, preferred_element_type=...  50.4 us
    another operation x1, loops' own time, slant_stack(): return lax.map(one_depth, jnp.arange(depth_cells, dtype=jnp.int32))  31.6 us
    ppermute x5, waiting for transfers between devices, with_halo(): before = lax.ppermute(last, axis, up)  25.8 us
    unnamed x74, local copies, waits for them, and re-layouts  20.7 us
    concatenate x4, other arithmetic, with_halo(): x = jnp.concatenate([before, x, after], axis=dim)  19.6 us
    ppermute x5, starting transfers between devices, with_halo(): before = lax.ppermute(last, axis, up)  16.1 us
    ppermute x5, starting transfers between devices, with_halo(): after = lax.ppermute(leading, axis, down)  15.6 us
  transfers between devices with their start and end apart: 10, of which 5 were waited for; matrix products, arithmetic and copies ran while one was open for 12% of the time, Pallas kernels for 0%

commit v1 on v0

v1 whole, which is shorter than its diff:
```python
import functools

import jax
import jax.numpy as jnp
from jax import lax
from jax.experimental import pallas as pl
from jax.experimental.pallas import tpu as pltpu
from jax.sharding import PartitionSpec as P

R = 16
BAND = 2
RX = 4
RY = 1
COLS = 2
ALIGN = 8


def first_offsets(offset_count):
    steep = R - BAND
    above, below = [], []
    for distance in range(1, R + 1):
        up = [h for h in range(offset_count) if -(-steep * h // offset_count) + BAND >= distance]
        down = [h for h in range(offset_count) if steep * h // offset_count + BAND >= distance]
        above.append((up[0] if up else offset_count) // ALIGN * ALIGN)
        below.append((down[0] if down else offset_count) // ALIGN * ALIGN)
    return above, below


def slant_matrix_of(slant_taper, band_offsets, offset_count):
    offset_index = jnp.arange(offset_count, dtype=jnp.int32)
    depth_shift = jnp.floor_divide(band_offsets[:, None] * offset_index[None, :], offset_count)
    reach_index = jnp.arange(slant_taper.shape[2], dtype=jnp.int32) - R
    inside_band = jnp.abs(reach_index[None, None, :] - depth_shift[:, :, None]) <= BAND
    return jnp.where(inside_band, slant_taper, jnp.zeros_like(slant_taper))


def stack_matrices(slant_matrix, depth_cells, above, below):
    angles, offset_count, reach = slant_matrix.shape
    flat = jnp.swapaxes(slant_matrix, 1, 2).reshape(angles, reach * offset_count)
    rows = [
        jnp.pad(flat, ((0, 0), (z * offset_count, (depth_cells - 1 - z) * offset_count)))
        for z in range(depth_cells)
    ]
    whole = jnp.concatenate(rows, axis=0)
    pieces = []
    for row in range(R):
        start = above[R - 1 - row]
        if start < offset_count:
            pieces.append(whole[:, row * offset_count + start : (row + 1) * offset_count])
    pieces.append(whole[:, R * offset_count : (R + depth_cells) * offset_count])
    for row in range(R):
        start = below[row]
        first = (R + depth_cells + row) * offset_count
        if start < offset_count:
            pieces.append(whole[:, first + start : first + offset_count])
    return jnp.concatenate(pieces, axis=1)


def stack_kernel(matrix_ref, above_ref, own_ref, below_ref, out_ref):
    na, no = above_ref.shape[1], own_ref.shape[1]
    total = jnp.dot(matrix_ref[:, :na], above_ref[0], preferred_element_type=jnp.float32)
    total += jnp.dot(matrix_ref[:, na : na + no], own_ref[0], preferred_element_type=jnp.float32)
    total += jnp.dot(matrix_ref[:, na + no :], below_ref[0], preferred_element_type=jnp.float32)
    out_ref[0] = total.astype(out_ref.dtype)


def slant_stack(matrix, above, own, below):
    columns, _, cross = own.shape
    rows, depth = matrix.shape
    tile = 256 if rows % 256 == 0 else rows
    return pl.pallas_call(
        stack_kernel,
        grid=(rows // tile, columns),
        in_specs=[
            pl.BlockSpec((tile, depth), lambda m, c: (m, 0)),
            pl.BlockSpec((1, above.shape[1], cross), lambda m, c: (c, 0, 0)),
            pl.BlockSpec((1, own.shape[1], cross), lambda m, c: (c, 0, 0)),
            pl.BlockSpec((1, below.shape[1], cross), lambda m, c: (c, 0, 0)),
        ],
        out_specs=pl.BlockSpec((1, tile, cross), lambda m, c: (c, m, 0)),
        out_shape=jax.ShapeDtypeStruct((columns, rows, cross), jnp.bfloat16),
        compiler_params=pltpu.CompilerParams(vmem_limit_bytes=32 * 1024 * 1024),
        cost_estimate=pl.CostEstimate(
            flops=2 * rows * depth * columns * cross,
            bytes_accessed=2 * (rows * depth + columns * (depth + rows) * cross),
            transcendentals=0,
        ),
        name="slant_stack",
    )(matrix, above, own, below)


def smooth_kernel(lateral, chunks, weight_ref, *refs):
    ins, out_ref = refs[:-1], refs[-1]
    angles, cross = out_ref.shape[2:]
    step = 32 if angles % 32 == 0 else angles
    for x in range(lateral):
        for first in range(0, angles, step):
            sums = [None] * (2 * RY + 1)
            for i in range(2 * RX + 1):
                chunk, column = chunks[x + i]
                plane = ins[chunk][column, 0, first : first + step, :].astype(jnp.float32)
                for j in range(2 * RY + 1):
                    tap = i * (2 * RY + 1) + j
                    term = weight_ref[0, x, tap : tap + 1, :] * plane
                    sums[j] = term if sums[j] is None else sums[j] + term
            total = sums[RY]
            for j in range(2 * RY + 1):
                if j != RY:
                    total = total + pltpu.roll(sums[j], (RY - j) % cross, 1)
            out_ref[x, 0, first : first + step, :] = total.astype(out_ref.dtype)


def smooth(weights, parts, chunks, lateral, depth_cells, angles):
    cross = weights.shape[-1]
    parts = [p.reshape(p.shape[0], depth_cells, angles, cross) for p in parts]
    return pl.pallas_call(
        functools.partial(smooth_kernel, lateral, chunks),
        grid=(depth_cells,),
        in_specs=[pl.BlockSpec((1,) + weights.shape[1:], lambda z: (z, 0, 0, 0))]
        + [pl.BlockSpec((p.shape[0], 1, angles, cross), lambda z: (0, z, 0, 0)) for p in parts],
        out_specs=pl.BlockSpec((lateral, 1, angles, cross), lambda z: (0, z, 0, 0)),
        out_shape=jax.ShapeDtypeStruct((lateral, depth_cells, angles, cross), jnp.bfloat16),
        compiler_params=pltpu.CompilerParams(vmem_limit_bytes=32 * 1024 * 1024),
        cost_estimate=pl.CostEstimate(
            flops=54 * lateral * depth_cells * angles * cross,
            bytes_accessed=8 * lateral * depth_cells * angles * cross,
            transcendentals=0,
        ),
        name="smooth",
    )(weights, *parts)


def dip_weights(dip_class, coefficients):
    classes, taps = coefficients.shape
    cross = dip_class.shape[-1]
    width = 2 * RY + 1
    padded = jnp.pad(dip_class, ((0, 0), (0, 0), (2 * RY, 2 * RY)), constant_values=-1)
    moved = jnp.stack(
        [padded[:, :, 3 * RY - j : 3 * RY - j + cross] for j in range(width)]
    )
    class_index = jnp.arange(classes, dtype=jnp.int32)
    onehot = (moved[:, :, :, None] == class_index[:, None]).astype(jnp.float32)
    weights = jnp.einsum(
        "qij,jzxqy->zxijy",
        coefficients.reshape(classes, taps // width, width),
        onehot,
        precision=lax.Precision.HIGHEST,
    )
    return weights.reshape(weights.shape[:2] + (taps, cross))


def neighbours(axis):
    count = lax.axis_size(axis)
    up = [(i, i + 1) for i in range(count - 1)]
    return up, [(j, i) for i, j in up]


def local(offset_image, dip_class, slant_taper, band_offsets, coefficients):
    offset_count, depth_cells, lateral, cross = offset_image.shape
    angles = slant_taper.shape[0]
    above, below = first_offsets(offset_count)
    up, down = neighbours("depth")
    right, left = neighbours("gx")
    cols = COLS if lateral % COLS == 0 else lateral

    by_column = jnp.transpose(offset_image, (2, 1, 0, 3))
    halos = []
    for first in range(0, lateral, cols):
        part = by_column[first : first + cols]
        last = [
            part[:, depth_cells - R + row, above[R - 1 - row] :]
            for row in range(R)
            if above[R - 1 - row] < offset_count
        ]
        leading = [part[:, row, below[row] :] for row in range(R) if below[row] < offset_count]
        halos.append(
            (
                lax.ppermute(jnp.concatenate(last, axis=1), "depth", up),
                lax.ppermute(jnp.concatenate(leading, axis=1), "depth", down),
            )
        )
    matrix = stack_matrices(
        slant_matrix_of(slant_taper, band_offsets, offset_count), depth_cells, above, below
    )
    weights = dip_weights(dip_class, coefficients)
    own = by_column.reshape(lateral, depth_cells * offset_count, cross)
    mine, before, after = [], [], []
    for index, (upper, lower) in enumerate(halos):
        first = index * cols
        part = slant_stack(matrix, upper, own[first : first + cols], lower)
        mine.append(part)
        before.append(lax.ppermute(part, "gx", right))
        after.append(lax.ppermute(part, "gx", left))
    parts = before + mine + after
    chunks = [(p, c) for p in range(len(parts)) for c in range(cols)]
    chunks = chunks[lateral - RX : 2 * lateral + RX]
    out = smooth(weights, parts, chunks, lateral, depth_cells, angles)
    return jnp.transpose(out, (2, 1, 0, 3))


def solution(mesh):
    return jax.shard_map(
        local,
        mesh=mesh,
        in_specs=(P(None, "depth", "gx", None), P("depth", "gx", None), P(), P(), P()),
        out_specs=P(None, "depth", "gx", None),
        check_vma=False,
    )
```

time: 276 us -> 142 us (0.51)
  the two profiles are of different devices: /device:TPU:13 before, /device:TPU:1 now
where the time goes in v1:
time: 142 us; the launch traced here: 140 us
  local copies, waits for them, and re-layouts  63.5 us (45%)
  waiting for transfers between devices  27 us (19%)
  starting transfers between devices  23.8 us (17%)
  Pallas kernels  23.7 us (17%)
    unnamed x69, local copies, waits for them, and re-layouts  29.8 us
    ppermute x2, waiting for transfers between devices, local(): after.append(lax.ppermute(part, 'gx', left))  15.7 us
    concatenate x1, local copies, waits for them, and re-layouts, stack_matrices(): return jnp.concatenate(pieces, axis=1)  13.2 us
    pallas_call x1, Pallas kernels, smooth(): pl.pallas_call(functools.partial(smooth_kernel, lateral, chunks), grid=(d...  12.7 us
    pallas_call x2, Pallas kernels, slant_stack(): pl.pallas_call(stack_kernel, grid=(rows // tile, columns), in_specs=[pl.B...  11 us
    ppermute x2, starting transfers between devices, local(): before.append(lax.ppermute(part, 'gx', right))  9.24 us
    slice x7, local copies, waits for them, and re-layouts, stack_matrices(): pieces.append(whole[:, first + start:first + offset_count])  8.45 us
    ppermute x2, starting transfers between devices, local(): lax.ppermute(jnp.concatenate(last, axis=1), 'depth', up)  8 us
  transfers between devices with their start and end apart: 8, of which 4 were waited for; matrix products, arithmetic and copies ran while one was open for 23% of the time, Pallas kernels for 8%

profile of v1, /device:TPU:1, one launch (start us, length us, event | category | flops | bytes accessed | tf_op | source)
XLA Modules:
  0.0 140.3 jit_solution(17068828787236694407)
XLA Ops:
  0.0 2.8 %copy.26 = bf16[64,16,4,256]{3,0,2,1:T(8,128)(2,1)S(1)} copy(bf16[64,16,4,256]{3,2,1,0:T(4,128)(2,1)} %param.5) | data formatting | bytes 4194304 | tf_op args[0]
  2.8 0.7 constant_dynamic-update-slice_fusion.61
  3.5 0.7 constant_dynamic-update-slice_fusion.60
  4.2 0.7 constant_dynamic-update-slice_fusion.59
  4.9 0.7 constant_dynamic-update-slice_fusion.58
  5.5 0.6 constant_dynamic-update-slice_fusion.57
  6.2 0.7 constant_dynamic-update-slice_fusion.56
  6.9 0.6 constant_dynamic-update-slice_fusion.55
  7.5 0.7 constant_dynamic-update-slice_fusion.54
  8.2 0.6 constant_dynamic-update-slice_fusion.53
  8.8 0.6 constant_dynamic-update-slice_fusion.52
  9.5 0.6 constant_dynamic-update-slice_fusion.51
  10.1 0.6 constant_dynamic-update-slice_fusion.50
  10.7 0.6 constant_dynamic-update-slice_fusion.49
  11.3 0.6 constant_dynamic-update-slice_fusion.48
  13.2 0.6 constant_dynamic-update-slice_fusion.44
  13.8 0.7 constant_dynamic-update-slice_fusion.43
  14.5 0.6 constant_dynamic-update-slice_fusion.42
  15.1 0.6 constant_dynamic-update-slice_fusion.41
  15.7 0.6 constant_dynamic-update-slice_fusion.40
  16.4 0.7 constant_dynamic-update-slice_fusion.39
  17.0 0.7 constant_dynamic-update-slice_fusion.38
  17.7 0.7 constant_dynamic-update-slice_fusion.37
  18.4 0.7 constant_dynamic-update-slice_fusion.36
  19.0 0.7 constant_dynamic-update-slice_fusion.35
  19.7 0.7 constant_dynamic-update-slice_fusion.34
  20.4 0.7 constant_dynamic-update-slice_fusion.33
  21.0 0.7 constant_dynamic-update-slice_fusion.32
  21.7 0.7 constant_dynamic-update-slice_fusion.31
  22.4 4.0 %collective-permute-start = (bf16[2,656,256]{2,1,0:T(8,128)(2,1)}, bf16[2,656,256]{2,1,0:T(8,128)(2,1)S(1)}, u32[]{:S(2)}, u32[]{:S(2)}) collective-permute-start(bf16[2,656,256]{2,1,0:T(8,128)(2,1)} %get-tuple-element.63), channel_id=1, source_target_pairs={{0,8},{8,16},{16,24},{1,9},{9,17},{17,25},{2,10},{10,18},{18,26},{... | collective-permute-start | bytes 2015240 | tf_op jit(solution)/shard_map/ppermute | solution.py:178
  26.4 1.3 collective-permute-start.1
  27.7 4.0 %collective-permute-start.3 = (bf16[2,656,256]{2,1,0:T(8,128)(2,1)}, bf16[2,656,256]{2,1,0:T(8,128)(2,1)S(1)}, u32[]{:S(2)}, u32[]{:S(2)}) collective-permute-start(bf16[2,656,256]{2,1,0:T(8,128)(2,1)} %get-tuple-element.62), channel_id=1, source_target_pairs={{0,8},{8,16},{16,24},{1,9},{9,17},{17,25},{2,10},{10,18},{18,26},{... | collective-permute-start | bytes 2015240 | tf_op jit(solution)/shard_map/ppermute | solution.py:178
  31.7 1.3 collective-permute-start.4
  35.7 1.4 fusion.10
  37.1 1.3 fusion.11
  38.4 1.3 fusion.12
  39.7 1.1 fusion.15
  40.9 1.0 fusion.9
  41.9 3.4 %slice.445 = bf16[1024,1528]{1,0:T(8,128)(2,1)} slice(bf16[1024,3072]{1,0:T(8,128)(2,1)S(1)} %pad_dynamic-update-slice_fusion), slice={[0:1024], [712:2240]} | slice | bytes 6258688 | tf_op jit(solution)/shard_map/slice | solution.py:49
  45.5 1.0 copy.17
  46.5 1.0 fusion.13
  47.5 1.3 fusion.14
  48.9 13.2 %concatenate.19.matrix_ref = bf16[1024,2272]{1,0:T(8,128)(2,1)} concatenate(bf16[1024,8]{1,0:T(8,128)(2,1)} %get-tuple-element.6, bf16[1024,16]{1,0:T(8,128)(2,1)} %get-tuple-element.10, bf16[1024,16]{1,0:T(8,128)(2,1)} %get-tuple-element.9, bf16[1024,24]{1,0:T(8,128)(2,1)} %get-tuple-element.14, bf16[1024,24]{1,0:T(8,128)(2,1)} %get-tuple-element.13, ...), dimensions={1} | concatenate | bytes 9306112 | tf_op jit(solution)/shard_map/concatenate | solution.py:56
  62.1 0.8 copy-done.4
  62.9 2.3 %copy-done = bf16[1024,2272]{1,0:T(8,128)(2,1)S(1)} copy-done((bf16[1024,2272]{1,0:T(8,128)(2,1)S(1)}, bf16[1024,2272]{1,0:T(8,128)(2,1)}, u32[]{:S(2)}) %copy-start) | copy-done | bytes 4653080
  65.3 1.1 copy-done.5
  66.4 4.4 %slant_stack.2 = bf16[2,1024,256]{2,1,0:T(8,128)(2,1)S(1)} custom-call(bf16[1024,2272]{1,0:T(8,128)(2,1)S(1)} %copy-done, bf16[2,656,256]{2,1,0:T(8,128)(2,1)S(1)} %collective-permute-done.above_ref, bf16[2,1024,256]{2,1,0:T(8,128)(2,1)S(1)} %bitcast.274, bf16[2,592,256]{2,1,0:T(8,128)(2,1)S(1)} %copy-done.5), custom_call_target="tpu_custom_call" | custom-call | flops 2382364672 | bytes 8028160 | tf_op jit(solution)/shard_map/slant_stack/pallas_call | solution.py:71
  70.7 4.6 %collective-permute-start.2 = (bf16[2,1024,256]{2,1,0:T(8,128)(2,1)S(1)}, bf16[2,1024,256]{2,1,0:T(8,128)(2,1)S(1)}, u32[]{:S(2)}, u32[]{:S(2)}) collective-permute-start(bf16[2,1024,256]{2,1,0:T(8,128)(2,1)S(1)} %slant_stack.2), channel_id=1, source_target_pairs={{0,1},{1,2},{2,3},{3,4},{4,5},{5,6},{6,7},{8,9},{9,10},{10,11},{11... | collective-permute-start | bytes 3145736 | tf_op jit(solution)/shard_map/ppermute | solution.py:192
  75.3 7.4 %collective-permute-done.4.below_ref = bf16[2,592,256]{2,1,0:T(8,128)(2,1)} collective-permute-done((bf16[2,592,256]{2,1,0:T(8,128)(2,1)}, bf16[2,592,256]{2,1,0:T(8,128)(2,1)}, u32[]{:S(2)}, u32[]{:S(2)}) %collective-permute-start.4) | collective-permute-done | bytes 606240 | tf_op jit(solution)/shard_map/ppermute | solution.py:179
  82.7 0.9 copy-done.2
  83.5 1.2 copy-done.1
  84.8 1.1 copy-done.3
  85.9 6.7 %slant_stack.3 = bf16[2,1024,256]{2,1,0:T(8,128)(2,1)S(1)} custom-call(bf16[1024,2272]{1,0:T(8,128)(2,1)S(1)} %copy-done, bf16[2,656,256]{2,1,0:T(8,128)(2,1)S(1)} %copy-done.3, bf16[2,1024,256]{2,1,0:T(8,128)(2,1)S(1)} %bitcast.273, bf16[2,592,256]{2,1,0:T(8,128)(2,1)} %collective-permute-done.4.below_ref), custom_call_target="tpu_custom_call" | custom-call | flops 2382364672 | bytes 8028160 | tf_op jit(solution)/shard_map/slant_stack/pallas_call | solution.py:71
  92.5 4.6 %collective-permute-start.5 = (bf16[2,1024,256]{2,1,0:T(8,128)(2,1)S(1)}, bf16[2,1024,256]{2,1,0:T(8,128)(2,1)}, u32[]{:S(2)}, u32[]{:S(2)}) collective-permute-start(bf16[2,1024,256]{2,1,0:T(8,128)(2,1)S(1)} %slant_stack.3), channel_id=1, source_target_pairs={{0,1},{1,2},{2,3},{3,4},{4,5},{5,6},{6,7},{8,9},{9,10},{10,11},{11... | collective-permute-start | bytes 3145736 | tf_op jit(solution)/shard_map/ppermute | solution.py:192
  97.2 1.9 %collective-permute-start.6 = (bf16[2,1024,256]{2,1,0:T(8,128)(2,1)S(1)}, bf16[2,1024,256]{2,1,0:T(8,128)(2,1)}, u32[]{:S(2)}, u32[]{:S(2)}) collective-permute-start(bf16[2,1024,256]{2,1,0:T(8,128)(2,1)S(1)} %slant_stack.2), channel_id=1, source_target_pairs={{1,0},{2,1},{3,2},{4,3},{5,4},{6,5},{7,6},{9,8},{10,9},{11,10},{12... | collective-permute-start | bytes 3145736 | tf_op jit(solution)/shard_map/ppermute | solution.py:193
  99.1 2.1 %collective-permute-start.7 = (bf16[2,1024,256]{2,1,0:T(8,128)(2,1)S(1)}, bf16[2,1024,256]{2,1,0:T(8,128)(2,1)}, u32[]{:S(2)}, u32[]{:S(2)}) collective-permute-start(bf16[2,1024,256]{2,1,0:T(8,128)(2,1)S(1)} %slant_stack.3), channel_id=1, source_target_pairs={{1,0},{2,1},{3,2},{4,3},{5,4},{6,5},{7,6},{9,8},{10,9},{11,10},{12... | collective-permute-start | bytes 3145736 | tf_op jit(solution)/shard_map/ppermute | solution.py:193
  101.5 1.4 convolution_bitcast_fusion
  102.9 1.0 copy.13
  103.9 1.0 copy.18.weight_ref
  105.0 3.9 %collective-permute-done.5 = bf16[2,1024,256]{2,1,0:T(8,128)(2,1)} collective-permute-done((bf16[2,1024,256]{2,1,0:T(8,128)(2,1)S(1)}, bf16[2,1024,256]{2,1,0:T(8,128)(2,1)}, u32[]{:S(2)}, u32[]{:S(2)}) %collective-permute-start.5) | collective-permute-done | bytes 1048608 | tf_op jit(solution)/shard_map/ppermute | solution.py:192
  108.9 4.5 %collective-permute-done.6 = bf16[2,1024,256]{2,1,0:T(8,128)(2,1)} collective-permute-done((bf16[2,1024,256]{2,1,0:T(8,128)(2,1)S(1)}, bf16[2,1024,256]{2,1,0:T(8,128)(2,1)}, u32[]{:S(2)}, u32[]{:S(2)}) %collective-permute-start.6) | collective-permute-done | bytes 1048608 | tf_op jit(solution)/shard_map/ppermute | solution.py:193
  113.4 11.2 %collective-permute-done.7 = bf16[2,1024,256]{2,1,0:T(8,128)(2,1)} collective-permute-done((bf16[2,1024,256]{2,1,0:T(8,128)(2,1)S(1)}, bf16[2,1024,256]{2,1,0:T(8,128)(2,1)}, u32[]{:S(2)}, u32[]{:S(2)}) %collective-permute-start.7) | collective-permute-done | bytes 1048608 | tf_op jit(solution)/shard_map/ppermute | solution.py:193
  124.6 12.7 %smooth.1 = bf16[4,16,64,256]{3,2,1,0:T(8,128)(2,1)S(1)} custom-call(f32[16,4,27,256]{3,2,1,0:T(8,128)S(1)} %copy.18.weight_ref, bf16[2,16,64,256]{3,2,1,0:T(8,128)(2,1)S(1)} %bitcast.271, bf16[2,16,64,256]{3,2,1,0:T(8,128)(2,1)} %bitcast.71.refs_1_, bf16[2,16,64,256]{3,2,1,0:T(8,128)(2,1)S(1)} %bitcast.270, bf16[2,16,64,256]{3,2,1,0:T(8,128)(2,1)S(1)} %bitcast.272, ...), custom_call_target="tpu_custom_call" | custom-call | flops 56623104 | bytes 8388608 | tf_op jit(solution)/shard_map/smooth/pallas_call | solution.py:116
  137.4 2.9 %copy.19 = bf16[64,16,4,256]{3,2,1,0:T(4,128)(2,1)} copy(bf16[64,16,4,256]{3,0,1,2:T(8,128)(2,1)S(1)} %bitcast.269) | data formatting | bytes 4194304 | tf_op jit(solution)/shard_map/transpose | solution.py:198
  (51 shorter events, 4.3 us)
Async XLA Ops:
  0.0 33.0 %copy-start.11 = (s32[64]{0:T(128)S(1)}, s32[64]{0:T(128)}, u32[]{:S(2)}) copy-start(s32[64]{0:T(128)} %param.8) | copy-start | bytes 772
  0.0 33.1 %copy-start.8 = (bf16[64,64,33]{1,0,2:T(8,128)(2,1)S(1)}, bf16[64,64,33]{1,0,2:T(8,128)(2,1)}, u32[]{:S(2)}) copy-start(bf16[64,64,33]{1,0,2:T(8,128)(2,1)} %param.7) | copy-start | bytes 811012
  2.8 30.6 %copy-start.6 = (bf16[64,16,4,256]{3,0,2,1:T(8,128)(2,1)}, bf16[64,16,4,256]{3,0,2,1:T(8,128)(2,1)S(1)}, u32[]{:S(2)}) copy-start(bf16[64,16,4,256]{3,0,2,1:T(8,128)(2,1)S(1)} %copy.26) | copy-start | bytes 6291460
  22.4 40.6 %collective-permute-start = (bf16[2,656,256]{2,1,0:T(8,128)(2,1)}, bf16[2,656,256]{2,1,0:T(8,128)(2,1)S(1)}, u32[]{:S(2)}, u32[]{:S(2)}) collective-permute-start(bf16[2,656,256]{2,1,0:T(8,128)(2,1)} %get-tuple-element.63), channel_id=1, source_target_pairs={{0,8},{8,16},{16,24},{1,9},{9,17},{17,25},{2,10},{10,18},{18,26},{... | collective-permute-start | bytes 2015240 | tf_op jit(solution)/shard_map/ppermute | solution.py:178
  26.4 35.7 %collective-permute-start.1 = (bf16[2,592,256]{2,1,0:T(8,128)(2,1)}, bf16[2,592,256]{2,1,0:T(8,128)(2,1)S(1)}, u32[]{:S(2)}, u32[]{:S(2)}) collective-permute-start(bf16[2,592,256]{2,1,0:T(8,128)(2,1)} %get-tuple-element.30), channel_id=1, source_target_pairs={{8,0},{16,8},{24,16},{9,1},{17,9},{25,17},{10,2},{18,10},{26,18},{... | collective-permute-start | bytes 1818632 | tf_op jit(solution)/shard_map/ppermute | solution.py:179
  27.7 55.0 %collective-permute-start.3 = (bf16[2,656,256]{2,1,0:T(8,128)(2,1)}, bf16[2,656,256]{2,1,0:T(8,128)(2,1)S(1)}, u32[]{:S(2)}, u32[]{:S(2)}) collective-permute-start(bf16[2,656,256]{2,1,0:T(8,128)(2,1)} %get-tuple-element.62), channel_id=1, source_target_pairs={{0,8},{8,16},{16,24},{1,9},{9,17},{17,25},{2,10},{10,18},{18,26},{... | collective-permute-start | bytes 2015240 | tf_op jit(solution)/shard_map/ppermute | solution.py:178
  31.7 51.0 %collective-permute-start.4 = (bf16[2,592,256]{2,1,0:T(8,128)(2,1)}, bf16[2,592,256]{2,1,0:T(8,128)(2,1)}, u32[]{:S(2)}, u32[]{:S(2)}) collective-permute-start(bf16[2,592,256]{2,1,0:T(8,128)(2,1)} %get-tuple-element.28), channel_id=1, source_target_pairs={{8,0},{16,8},{24,16},{9,1},{17,9},{25,17},{10,2},{18,10},{26,18},{... | collective-permute-start | bytes 1818632 | tf_op jit(solution)/shard_map/ppermute | solution.py:179
  35.0 5.8 %copy-start.7 = (bf16[64,16,4,256]{3,0,2,1:T(8,128)(2,1)S(1)}, bf16[64,16,4,256]{3,0,2,1:T(8,128)(2,1)}, u32[]{:S(2)}) copy-start(bf16[64,16,4,256]{3,0,2,1:T(8,128)(2,1)} %copy-done.6) | copy-start | bytes 6291460
  62.1 0.8 copy-start.4
  62.9 2.3 %copy-start = (bf16[1024,2272]{1,0:T(8,128)(2,1)S(1)}, bf16[1024,2272]{1,0:T(8,128)(2,1)}, u32[]{:S(2)}) copy-start(bf16[1024,2272]{1,0:T(8,128)(2,1)} %concatenate.19.matrix_ref) | copy-start | bytes 13959172
  65.3 1.1 copy-start.5
  66.4 34.9 %copy-start.10 = (f32[8,27]{1,0:T(8,128)S(1)}, f32[8,27]{1,0:T(8,128)}, u32[]{:S(2)}) copy-start(f32[8,27]{1,0:T(8,128)} %param.9) | copy-start | bytes 2596
  66.4 35.0 %copy-start.9 = (s32[16,4,256]{2,1,0:T(4,128)S(1)}, s32[16,4,256]{2,1,0:T(4,128)}, u32[]{:S(2)}) copy-start(s32[16,4,256]{2,1,0:T(4,128)} %param.6) | copy-start | bytes 196612
  70.7 34.2 %collective-permute-start.2 = (bf16[2,1024,256]{2,1,0:T(8,128)(2,1)S(1)}, bf16[2,1024,256]{2,1,0:T(8,128)(2,1)S(1)}, u32[]{:S(2)}, u32[]{:S(2)}) collective-permute-start(bf16[2,1024,256]{2,1,0:T(8,128)(2,1)S(1)} %slant_stack.2), channel_id=1, source_target_pairs={{0,1},{1,2},{2,3},{3,4},{4,5},{5,6},{6,7},{8,9},{9,10},{10,11},{11... | collective-permute-start | bytes 3145736 | tf_op jit(solution)/shard_map/ppermute | solution.py:192
  82.7 0.9 copy-start.2
  83.5 1.2 copy-start.1
  84.8 1.1 copy-start.3
  92.5 16.4 %collective-permute-start.5 = (bf16[2,1024,256]{2,1,0:T(8,128)(2,1)S(1)}, bf16[2,1024,256]{2,1,0:T(8,128)(2,1)}, u32[]{:S(2)}, u32[]{:S(2)}) collective-permute-start(bf16[2,1024,256]{2,1,0:T(8,128)(2,1)S(1)} %slant_stack.3), channel_id=1, source_target_pairs={{0,1},{1,2},{2,3},{3,4},{4,5},{5,6},{6,7},{8,9},{9,10},{10,11},{11... | collective-permute-start | bytes 3145736 | tf_op jit(solution)/shard_map/ppermute | solution.py:192
  97.2 16.2 %collective-permute-start.6 = (bf16[2,1024,256]{2,1,0:T(8,128)(2,1)S(1)}, bf16[2,1024,256]{2,1,0:T(8,128)(2,1)}, u32[]{:S(2)}, u32[]{:S(2)}) collective-permute-start(bf16[2,1024,256]{2,1,0:T(8,128)(2,1)S(1)} %slant_stack.2), channel_id=1, source_target_pairs={{1,0},{2,1},{3,2},{4,3},{5,4},{6,5},{7,6},{9,8},{10,9},{11,10},{12... | collective-permute-start | bytes 3145736 | tf_op jit(solution)/shard_map/ppermute | solution.py:193
  99.1 25.5 %collective-permute-start.7 = (bf16[2,1024,256]{2,1,0:T(8,128)(2,1)S(1)}, bf16[2,1024,256]{2,1,0:T(8,128)(2,1)}, u32[]{:S(2)}, u32[]{:S(2)}) collective-permute-start(bf16[2,1024,256]{2,1,0:T(8,128)(2,1)S(1)} %slant_stack.3), channel_id=1, source_target_pairs={{1,0},{2,1},{3,2},{4,3},{5,4},{6,5},{7,6},{9,8},{10,9},{11,10},{12... | collective-permute-start | bytes 3145736 | tf_op jit(solution)/shard_map/ppermute | solution.py:193

commit v2 on v1

v2 whole, which is shorter than its diff:
```python
import functools

import jax
import jax.numpy as jnp
from jax import lax
from jax.experimental import pallas as pl
from jax.experimental.pallas import tpu as pltpu
from jax.sharding import PartitionSpec as P

R = 16
BAND = 2
RX = 4
RY = 1
COLS = 2
GROUP = 4
ALIGN = 8


def first_offsets(offset_count):
    steep = R - BAND
    above, below = [], []
    for distance in range(1, R + 1):
        up = [h for h in range(offset_count) if -(-steep * h // offset_count) + BAND >= distance]
        down = [h for h in range(offset_count) if steep * h // offset_count + BAND >= distance]
        above.append((up[0] if up else offset_count) // ALIGN * ALIGN)
        below.append((down[0] if down else offset_count) // ALIGN * ALIGN)
    return above, below


def slant_matrix_of(slant_taper, band_offsets, offset_count):
    offset_index = jnp.arange(offset_count, dtype=jnp.int32)
    depth_shift = jnp.floor_divide(band_offsets[:, None] * offset_index[None, :], offset_count)
    reach_index = jnp.arange(slant_taper.shape[2], dtype=jnp.int32) - R
    inside_band = jnp.abs(reach_index[None, None, :] - depth_shift[:, :, None]) <= BAND
    return jnp.where(inside_band, slant_taper, jnp.zeros_like(slant_taper))


def stack_matrix(slant_matrix, group):
    angles, offset_count, reach = slant_matrix.shape
    flat = jnp.swapaxes(slant_matrix, 1, 2).reshape(angles, reach * offset_count)
    rows = [
        jnp.pad(flat, ((0, 0), (z * offset_count, (group - 1 - z) * offset_count)))
        for z in range(group)
    ]
    return jnp.concatenate(rows, axis=0)


def packed_rows(starts, offset_count):
    rows, place = [], 0
    for row, start in enumerate(starts):
        if start < offset_count:
            rows.append((row, start, place))
            place += offset_count - start
    return rows, place


def pack_kernel(upper, lower, image_ref, last_ref, leading_ref):
    depth_cells, offset_count = image_ref.shape[1:3]
    for row, start, place in upper:
        last_ref[0, place : place + offset_count - start, :] = image_ref[
            0, depth_cells - R + row, start:, :
        ]
    for row, start, place in lower:
        leading_ref[0, place : place + offset_count - start, :] = image_ref[0, row, start:, :]


def pack(by_column, upper, lower):
    columns, depth_cells, offset_count, cross = by_column.shape
    sizes = [upper[1], lower[1]]
    return pl.pallas_call(
        functools.partial(pack_kernel, upper[0], lower[0]),
        grid=(columns,),
        in_specs=[pl.BlockSpec((1, depth_cells, offset_count, cross), lambda c: (c, 0, 0, 0))],
        out_specs=[pl.BlockSpec((1, n, cross), lambda c: (c, 0, 0)) for n in sizes],
        out_shape=[jax.ShapeDtypeStruct((columns, n, cross), jnp.bfloat16) for n in sizes],
        compiler_params=pltpu.CompilerParams(vmem_limit_bytes=32 * 1024 * 1024),
        cost_estimate=pl.CostEstimate(
            flops=0, bytes_accessed=4 * columns * sum(sizes) * cross, transcendentals=0
        ),
        name="pack",
    )(by_column)


def stack_kernel(upper, lower, group, matrix_ref, above_ref, own_ref, below_ref, out_ref, planes):
    depth_cells, offset_count, cross = own_ref.shape[1:]
    below_row = R + depth_cells

    @pl.when(pl.program_id(0) == 0)
    def _():
        planes[: R * offset_count, :] = jnp.zeros((R * offset_count, cross), planes.dtype)
        planes[below_row * offset_count :, :] = jnp.zeros((R * offset_count, cross), planes.dtype)

    for row, start, place in upper:
        planes[row * offset_count + start : (row + 1) * offset_count, :] = above_ref[
            0, place : place + offset_count - start, :
        ]
    for row in range(depth_cells):
        planes[(R + row) * offset_count : (R + row + 1) * offset_count, :] = own_ref[0, row]
    for row, start, place in lower:
        first = (below_row + row) * offset_count
        planes[first + start : first + offset_count, :] = below_ref[
            0, place : place + offset_count - start, :
        ]
    tile, depth = matrix_ref.shape
    for z in range(0, depth_cells, group):
        total = jnp.dot(
            matrix_ref[...],
            planes[z * offset_count : z * offset_count + depth, :],
            preferred_element_type=jnp.float32,
        )
        out_ref[0, z // group * tile : (z // group + 1) * tile, :] = total.astype(out_ref.dtype)


def slant_stack(matrix, group, above, by_column, below, upper, lower, first, columns):
    _, depth_cells, offset_count, cross = by_column.shape
    tile, depth = matrix.shape
    rows = depth_cells // group * tile
    return pl.pallas_call(
        functools.partial(stack_kernel, upper[0], lower[0], group),
        grid=(columns,),
        in_specs=[
            pl.BlockSpec((tile, depth), lambda c: (0, 0)),
            pl.BlockSpec((1, upper[1], cross), lambda c: (c, 0, 0)),
            pl.BlockSpec((1, depth_cells, offset_count, cross), lambda c: (c + first, 0, 0, 0)),
            pl.BlockSpec((1, lower[1], cross), lambda c: (c, 0, 0)),
        ],
        out_specs=pl.BlockSpec((1, rows, cross), lambda c: (c, 0, 0)),
        out_shape=jax.ShapeDtypeStruct((columns, rows, cross), jnp.bfloat16),
        scratch_shapes=[pltpu.VMEM(((2 * R + depth_cells) * offset_count, cross), jnp.bfloat16)],
        compiler_params=pltpu.CompilerParams(vmem_limit_bytes=32 * 1024 * 1024),
        cost_estimate=pl.CostEstimate(
            flops=2 * rows * depth * columns * cross,
            bytes_accessed=2 * (tile * depth + columns * (depth + rows) * cross),
            transcendentals=0,
        ),
        name="slant_stack",
    )(matrix, above, by_column, below)


def smooth_kernel(sources, weight_ref, *refs):
    out_ref = refs[-1]
    lateral, _, angles, cross = out_ref.shape
    step = 32 if angles % 32 == 0 else angles
    count = 1 + max(which for planes in sources for _, which, _ in planes)
    for x in range(lateral):
        for first in range(0, angles, step):
            sums = [None] * (2 * RY + 1)
            for i, which, column in sources[x]:
                plane = refs[which][column, 0, first : first + step, :].astype(jnp.float32)
                for j in range(2 * RY + 1):
                    tap = i * (2 * RY + 1) + j
                    term = weight_ref[0, x, tap : tap + 1, :] * plane
                    sums[j] = term if sums[j] is None else sums[j] + term
            total = sums[RY]
            for j in range(2 * RY + 1):
                if j != RY:
                    total = total + pltpu.roll(sums[j], (RY - j) % cross, 1)
            if len(refs) > count + 1:
                total = total + refs[count][x, 0, first : first + step, :]
            out_ref[x, 0, first : first + step, :] = total.astype(out_ref.dtype)


def smooth(weights, parts, sources, partial, lateral, depth_cells, angles, kind):
    cross = weights.shape[-1]
    used = sorted({which for planes in sources for _, which, _ in planes})
    sources = [[(i, used.index(which), column) for i, which, column in planes] for planes in sources]
    ins = [parts[which] for which in used]
    ins = [p.reshape(p.shape[0], depth_cells, angles, cross) for p in ins]
    if partial is not None:
        ins.append(partial)
    planes = sum(len(s) for s in sources)
    return pl.pallas_call(
        functools.partial(smooth_kernel, sources),
        grid=(depth_cells,),
        in_specs=[pl.BlockSpec((1,) + weights.shape[1:], lambda z: (z, 0, 0, 0))]
        + [pl.BlockSpec((p.shape[0], 1, angles, cross), lambda z: (0, z, 0, 0)) for p in ins],
        out_specs=pl.BlockSpec((lateral, 1, angles, cross), lambda z: (0, z, 0, 0)),
        out_shape=jax.ShapeDtypeStruct((lateral, depth_cells, angles, cross), kind),
        compiler_params=pltpu.CompilerParams(vmem_limit_bytes=32 * 1024 * 1024),
        cost_estimate=pl.CostEstimate(
            flops=200 * planes * depth_cells * angles * cross,
            bytes_accessed=8 * lateral * depth_cells * angles * cross,
            transcendentals=0,
        ),
        name="smooth",
    )(weights, *ins)


def dip_weights(dip_class, coefficients):
    classes, taps = coefficients.shape
    cross = dip_class.shape[-1]
    width = 2 * RY + 1
    padded = jnp.pad(dip_class, ((0, 0), (0, 0), (2 * RY, 2 * RY)), constant_values=-1)
    moved = jnp.stack(
        [padded[:, :, 3 * RY - j : 3 * RY - j + cross] for j in range(width)]
    )
    class_index = jnp.arange(classes, dtype=jnp.int32)
    onehot = (moved[:, :, :, None] == class_index[:, None]).astype(jnp.float32)
    weights = jnp.einsum(
        "qij,jzxqy->zxijy",
        coefficients.reshape(classes, taps // width, width),
        onehot,
        precision=lax.Precision.HIGHEST,
    )
    return weights.reshape(weights.shape[:2] + (taps, cross))


def neighbours(axis):
    count = lax.axis_size(axis)
    up = [(i, i + 1) for i in range(count - 1)]
    return up, [(j, i) for i, j in up]


def halo_of(last, leading):
    up, down = neighbours("depth")
    return lax.ppermute(last, "depth", up), lax.ppermute(leading, "depth", down)


def local(offset_image, dip_class, slant_taper, band_offsets, coefficients):
    offset_count, depth_cells, lateral, cross = offset_image.shape
    angles = slant_taper.shape[0]
    above, below = first_offsets(offset_count)
    right, left = neighbours("gx")
    cols = COLS if lateral % COLS == 0 else lateral

    upper = packed_rows(above[::-1], offset_count)
    lower = packed_rows(below, offset_count)
    group = GROUP if depth_cells % GROUP == 0 else depth_cells
    by_column = jnp.transpose(offset_image, (2, 1, 0, 3))
    last, leading = pack(by_column, upper, lower)
    halos = [
        halo_of(last[first : first + cols], leading[first : first + cols])
        for first in range(0, lateral, cols)
    ]
    matrix = stack_matrix(slant_matrix_of(slant_taper, band_offsets, offset_count), group)
    weights = dip_weights(dip_class, coefficients)
    mine, before, after = [], [], []
    for index, (from_above, from_below) in enumerate(halos):
        part = slant_stack(
            matrix, group, from_above, by_column, from_below, upper, lower, index * cols, cols
        )
        mine.append(part)
        before.append(lax.ppermute(part, "gx", right))
        after.append(lax.ppermute(part, "gx", left))
    parts = before + mine + after
    chunks = [(p, c) for p in range(len(parts)) for c in range(cols)]
    chunks = chunks[lateral - RX : 2 * lateral + RX]
    count = len(mine)
    final = {count - 1, 3 * count - 1} if count > 1 else set()
    early, late = [], []
    for x in range(lateral):
        planes = [(i,) + chunks[x + i] for i in range(2 * RX + 1)]
        early.append([p for p in planes if p[1] not in final])
        late.append([p for p in planes if p[1] in final])
    sizes = (lateral, depth_cells, angles)
    if all(late):
        out = smooth(weights, parts, early, None, *sizes, jnp.float32)
        out = smooth(weights, parts, late, out, *sizes, jnp.bfloat16)
    else:
        out = smooth(weights, parts, [e + l for e, l in zip(early, late)], None, *sizes, jnp.bfloat16)
    return jnp.transpose(out, (2, 1, 0, 3))


def solution(mesh):
    return jax.shard_map(
        local,
        mesh=mesh,
        in_specs=(P(None, "depth", "gx", None), P("depth", "gx", None), P(), P(), P()),
        out_specs=P(None, "depth", "gx", None),
        check_vma=False,
    )
```

time: 142 us -> 99.3 us (0.70)
  local copies, waits for them, and re-layouts: 63.5 us -> 17.6 us
  starting transfers between devices: 23.8 us -> 25.9 us
  other arithmetic: 0.45 us -> 2.07 us
    unnamed x69 -> x18, local copies, waits for them, and re-layouts: 29.8 us -> 6.71 us
    ppermute x4, waiting for transfers between devices: 7.36 us -> 27.7 us  [the longest x2 27.7 us: halo_of(): lax.ppermute(leading, 'depth', down)]
    ppermute x2, waiting for transfers between devices: 15.7 us -> 0.01 us  [local(): after.append(lax.ppermute(part, 'gx', left))]
    concatenate x4 -> x0, local copies, waits for them, and re-layouts: 14.6 us -> none  [the longest x1 13.2 us: stack_matrices(): return jnp.concatenate(pieces, axis=1)]
    slice x11 -> x2, local copies, waits for them, and re-layouts: 13.1 us -> 2.33 us  [the longest x1 1.16 us: local(): last[first:first + cols]]
    ppermute x2, waiting for transfers between devices: 3.92 us -> 0.01 us  [local(): before.append(lax.ppermute(part, 'gx', right))]
    reshape x1, local copies, waits for them, and re-layouts: 0.33 us -> 2.16 us  [stack_matrix(): jnp.swapaxes(slant_matrix, 1, 2).reshape(angles, reach * offset_count)]
    concatenate x0 -> x1, other arithmetic: none -> 1.62 us  [stack_matrix(): return jnp.concatenate(rows, axis=0)]
  transfers between devices with their start and end apart: 8 -> 8, of which waited for: 4 -> 2; matrix products, arithmetic and copies ran while one was open for 23% -> 10% of each run, Pallas kernels for 8% -> 19%
where the time goes in v2:
time: 99.3 us; the launch traced here: 98.2 us
  waiting for transfers between devices  27.7 us (28%)
  starting transfers between devices  25.9 us (26%)
  Pallas kernels  23.3 us (23%)
  local copies, waits for them, and re-layouts  17.6 us (18%)
  other arithmetic  2.07 us (2%)
  matrix products  1.38 us (1%)
    ppermute x2, waiting for transfers between devices, halo_of(): lax.ppermute(leading, 'depth', down)  27.7 us
    pallas_call x2, Pallas kernels, smooth(): pl.pallas_call(functools.partial(smooth_kernel, sources), grid=(depth_cel...  15.4 us
    ppermute x2, starting transfers between devices, local(): before.append(lax.ppermute(part, 'gx', right))  10.5 us
    ppermute x2, starting transfers between devices, halo_of(): lax.ppermute(last, 'depth', up)  8.81 us
    pallas_call x2, Pallas kernels, slant_stack(): pl.pallas_call(functools.partial(stack_kernel, upper[0], lower[0], group)...  7.57 us
    unnamed x18, local copies, waits for them, and re-layouts  6.71 us
    ppermute x2, starting transfers between devices, local(): after.append(lax.ppermute(part, 'gx', left))  4.02 us
    transpose x1, local copies, waits for them, and re-layouts, local(): return jnp.transpose(out, (2, 1, 0, 3))  2.94 us
  transfers between devices with their start and end apart: 8, of which 2 were waited for; matrix products, arithmetic and copies ran while one was open for 10% of the time, Pallas kernels for 19%

profile of v2, /device:TPU:1, one launch (start us, length us, event | category | flops | bytes accessed | tf_op | source)
XLA Modules:
  0.0 98.2 jit_solution(6330327210361409338)
XLA Ops:
  0.0 2.8 %copy.25 = bf16[64,16,4,256]{3,0,1,2:T(8,128)(2,1)S(1)} copy(bf16[64,16,4,256]{3,2,1,0:T(4,128)(2,1)} %param.5) | data formatting | bytes 4194304 | tf_op args[0]
  2.8 0.2 pack.1
  3.0 0.0 copy-start.7
  3.0 0.0 copy-start.4
  3.0 1.2 %fusion.18 = (bf16[2,656,256]{2,1,0:T(8,128)(2,1)}, bf16[2,656,256]{2,1,0:T(8,128)(2,1)}) fusion(bf16[4,656,256]{2,1,0:T(8,128)(2,1)S(1)} %get-tuple-element.7), kind=kLoop, calls=%fused_computation.38 | loop fusion | bytes 2686976 | tf_op jit(solution)/shard_map/slice | solution.py:232
  4.2 4.0 %collective-permute-start.4 = (bf16[2,656,256]{2,1,0:T(8,128)(2,1)}, bf16[2,656,256]{2,1,0:T(8,128)(2,1)S(1)}, u32[]{:S(2)}, u32[]{:S(2)}) collective-permute-start(bf16[2,656,256]{2,1,0:T(8,128)(2,1)} %get-tuple-element.9), channel_id=1, source_target_pairs={{0,8},{8,16},{16,24},{1,9},{9,17},{17,25},{2,10},{10,18},{18,26},{... | collective-permute-start | bytes 2015240 | tf_op jit(solution)/shard_map/ppermute | solution.py:216
  8.2 1.2 %fusion.19 = (bf16[2,592,256]{2,1,0:T(8,128)(2,1)}, bf16[2,592,256]{2,1,0:T(8,128)(2,1)}) fusion(bf16[4,592,256]{2,1,0:T(8,128)(2,1)S(1)} %get-tuple-element.8), kind=kLoop, calls=%fused_computation.39 | loop fusion | bytes 2424832 | tf_op jit(solution)/shard_map/slice | solution.py:232
  9.3 1.3 %collective-permute-start.5 = (bf16[2,592,256]{2,1,0:T(8,128)(2,1)}, bf16[2,592,256]{2,1,0:T(8,128)(2,1)S(1)}, u32[]{:S(2)}, u32[]{:S(2)}) collective-permute-start(bf16[2,592,256]{2,1,0:T(8,128)(2,1)} %get-tuple-element.11), channel_id=1, source_target_pairs={{8,0},{16,8},{24,16},{9,1},{17,9},{25,17},{10,2},{18,10},{26,18},{... | collective-permute-start | bytes 1818632 | tf_op jit(solution)/shard_map/ppermute | solution.py:216
  10.6 4.8 %collective-permute-start = (bf16[2,656,256]{2,1,0:T(8,128)(2,1)}, bf16[2,656,256]{2,1,0:T(8,128)(2,1)}, u32[]{:S(2)}, u32[]{:S(2)}) collective-permute-start(bf16[2,656,256]{2,1,0:T(8,128)(2,1)} %get-tuple-element.10), channel_id=1, source_target_pairs={{0,8},{8,16},{16,24},{1,9},{9,17},{17,25},{2,10},{10,18},{18,26},{... | collective-permute-start | bytes 2015240 | tf_op jit(solution)/shard_map/ppermute | solution.py:216
  15.5 1.3 %collective-permute-start.1 = (bf16[2,592,256]{2,1,0:T(8,128)(2,1)}, bf16[2,592,256]{2,1,0:T(8,128)(2,1)}, u32[]{:S(2)}, u32[]{:S(2)}) collective-permute-start(bf16[2,592,256]{2,1,0:T(8,128)(2,1)} %get-tuple-element.12), channel_id=1, source_target_pairs={{8,0},{16,8},{24,16},{9,1},{17,9},{25,17},{10,2},{18,10},{26,18},{... | collective-permute-start | bytes 1818632 | tf_op jit(solution)/shard_map/ppermute | solution.py:216
  16.8 0.0 copy-done.7
  16.8 0.1 add_select_fusion
  16.9 0.0 copy-done.4
  16.9 0.3 fusion.11
  17.2 1.2 %copy.14 = bf16[64,33,64]{2,1,0:T(8,128)(2,1)} copy(bf16[64,33,64]{2,0,1:T(8,128)(2,1)S(1)} %fusion.11) | data formatting | bytes 540672 | tf_op jit(solution)/shard_map/transpose | solution.py:40
  18.5 2.2 %reshape.70 = bf16[64,2112]{1,0:T(8,128)(2,1)} reshape(bf16[64,33,64]{2,1,0:T(8,128)(2,1)} %copy.14) | data formatting | bytes 540672 | tf_op jit(solution)/shard_map/reshape | solution.py:40
  20.6 1.6 %fusion.7.matrix_ref = bf16[256,2304]{1,0:T(8,128)(2,1)S(1)} fusion(bf16[64,2112]{1,0:T(8,128)(2,1)} %reshape.70), kind=kLoop, calls=%fused_computation.16 | loop fusion | flops 11796480 | bytes 1449984 | tf_op jit(solution)/shard_map/concatenate | solution.py:45
  22.2 14.8 %collective-permute-done.5.below_ref = bf16[2,592,256]{2,1,0:T(8,128)(2,1)S(1)} collective-permute-done((bf16[2,592,256]{2,1,0:T(8,128)(2,1)}, bf16[2,592,256]{2,1,0:T(8,128)(2,1)S(1)}, u32[]{:S(2)}, u32[]{:S(2)}) %collective-permute-start.5) | collective-permute-done | bytes 606240 | tf_op jit(solution)/shard_map/ppermute | solution.py:216
  37.0 0.0 copy-start.2
  37.0 0.8 copy-done.2
  37.9 0.0 collective-permute-done.4.above_ref
  37.9 0.0 copy-start
  37.9 0.8 copy-done
  38.7 0.0 copy-start.1
  38.7 1.1 %copy-done.1 = bf16[2,656,256]{2,1,0:T(8,128)(2,1)S(1)} copy-done((bf16[2,656,256]{2,1,0:T(8,128)(2,1)S(1)}, bf16[2,656,256]{2,1,0:T(8,128)(2,1)}, u32[]{:S(2)}) %copy-start.1) | copy-done | bytes 671768
  39.8 0.0 copy-start.3
  39.8 1.1 %copy-done.3 = bf16[2,592,256]{2,1,0:T(8,128)(2,1)S(1)} copy-done((bf16[2,592,256]{2,1,0:T(8,128)(2,1)S(1)}, bf16[2,592,256]{2,1,0:T(8,128)(2,1)}, u32[]{:S(2)}) %copy-start.3) | copy-done | bytes 606232
  40.9 2.9 %slant_stack.3 = bf16[2,1024,256]{2,1,0:T(8,128)(2,1)S(1)} custom-call(bf16[256,2304]{1,0:T(8,128)(2,1)S(1)} %fusion.7.matrix_ref, bf16[2,656,256]{2,1,0:T(8,128)(2,1)S(1)} %copy-done.1, bf16[4,16,64,256]{3,2,1,0:T(8,128)(2,1)S(1)} %bitcast.25, bf16[2,592,256]{2,1,0:T(8,128)(2,1)S(1)} %copy-done.3), custom_call_target="tpu_custom_call" | custom-call | flops 2415919104 | bytes 4587520 | tf_op jit(solution)/shard_map/slant_stack/pallas_call | solution.py:118
  43.7 0.0 copy-start.6
  43.7 0.0 copy-start.5
  43.8 5.9 %collective-permute-start.6 = (bf16[2,1024,256]{2,1,0:T(8,128)(2,1)S(1)}, bf16[2,1024,256]{2,1,0:T(8,128)(2,1)}, u32[]{:S(2)}, u32[]{:S(2)}) collective-permute-start(bf16[2,1024,256]{2,1,0:T(8,128)(2,1)S(1)} %slant_stack.3), channel_id=1, source_target_pairs={{0,1},{1,2},{2,3},{3,4},{4,5},{5,6},{6,7},{8,9},{9,10},{10,11},{11... | collective-permute-start | bytes 3145736 | tf_op jit(solution)/shard_map/ppermute | solution.py:243
  49.7 1.9 %collective-permute-start.7 = (bf16[2,1024,256]{2,1,0:T(8,128)(2,1)S(1)}, bf16[2,1024,256]{2,1,0:T(8,128)(2,1)}, u32[]{:S(2)}, u32[]{:S(2)}) collective-permute-start(bf16[2,1024,256]{2,1,0:T(8,128)(2,1)S(1)} %slant_stack.3), channel_id=1, source_target_pairs={{1,0},{2,1},{3,2},{4,3},{5,4},{6,5},{7,6},{9,8},{10,9},{11,10},{12... | collective-permute-start | bytes 3145736 | tf_op jit(solution)/shard_map/ppermute | solution.py:244
  51.6 12.9 %collective-permute-done.1.below_ref = bf16[2,592,256]{2,1,0:T(8,128)(2,1)} collective-permute-done((bf16[2,592,256]{2,1,0:T(8,128)(2,1)}, bf16[2,592,256]{2,1,0:T(8,128)(2,1)}, u32[]{:S(2)}, u32[]{:S(2)}) %collective-permute-start.1) | collective-permute-done | bytes 606240 | tf_op jit(solution)/shard_map/ppermute | solution.py:216
  64.5 0.0 collective-permute-done.above_ref
  64.5 4.7 %slant_stack.2 = bf16[2,1024,256]{2,1,0:T(8,128)(2,1)} custom-call(bf16[256,2304]{1,0:T(8,128)(2,1)S(1)} %fusion.7.matrix_ref, bf16[2,656,256]{2,1,0:T(8,128)(2,1)} %collective-permute-done.above_ref, bf16[4,16,64,256]{3,2,1,0:T(8,128)(2,1)S(1)} %bitcast.26, bf16[2,592,256]{2,1,0:T(8,128)(2,1)} %collective-permute-done.1.below_ref), custom_call_target="tpu_custom_call" | custom-call | flops 2415919104 | bytes 4587520 | tf_op jit(solution)/shard_map/slant_stack/pallas_call | solution.py:118
  69.2 4.6 %collective-permute-start.2 = (bf16[2,1024,256]{2,1,0:T(8,128)(2,1)}, bf16[2,1024,256]{2,1,0:T(8,128)(2,1)S(1)}, u32[]{:S(2)}, u32[]{:S(2)}) collective-permute-start(bf16[2,1024,256]{2,1,0:T(8,128)(2,1)} %slant_stack.2), channel_id=1, source_target_pairs={{0,1},{1,2},{2,3},{3,4},{4,5},{5,6},{6,7},{8,9},{9,10},{10,11},{11... | collective-permute-start | bytes 3145736 | tf_op jit(solution)/shard_map/ppermute | solution.py:243
  73.9 2.1 %collective-permute-start.3 = (bf16[2,1024,256]{2,1,0:T(8,128)(2,1)}, bf16[2,1024,256]{2,1,0:T(8,128)(2,1)S(1)}, u32[]{:S(2)}, u32[]{:S(2)}) collective-permute-start(bf16[2,1024,256]{2,1,0:T(8,128)(2,1)} %slant_stack.2), channel_id=1, source_target_pairs={{1,0},{2,1},{3,2},{4,3},{5,4},{6,5},{7,6},{9,8},{10,9},{11,10},{12... | collective-permute-start | bytes 3145736 | tf_op jit(solution)/shard_map/ppermute | solution.py:244
  76.0 0.0 copy-done.6
  76.0 0.1 copy.11
  76.1 0.0 copy-done.5
  76.1 0.1 fusion.12
  76.2 1.4 %convolution_bitcast_fusion = f32[16,4,9,3,256]{4,2,1,0,3:T(8,128)S(1)} fusion(s32[3,16,4,256]{3,2,1,0:T(4,128)S(1)} %pad_add_fusion, f32[8,9,3,1,1]{0,2,1,4,3:T(4,128)S(1)} %bitcast.32), kind=kOutput, calls=%fused_computation.13 | convolution fusion | flops 42860544 | bytes 1966944 | tf_op jit(solution)/shard_map/qij,jzxqy->zxijy/dot_general | solution.py:199
  77.6 1.0 %copy.13 = f32[16,4,9,3,256]{4,0,3,2,1:T(8,128)S(1)} copy(f32[16,4,9,3,256]{4,2,1,0,3:T(8,128)S(1)} %convolution_bitcast_fusion) | data formatting | bytes 3538944 | tf_op jit(solution)/shard_map/qij,jzxqy->zxijy/transpose | solution.py:199
  78.7 1.0 %copy.17.weight_ref = f32[16,4,27,256]{3,2,1,0:T(8,128)S(1)} copy(f32[16,4,27,256]{3,0,2,1:T(8,128)S(1)} %bitcast.30) | data formatting | bytes 3538944 | tf_op jit(solution)/shard_map/reshape | solution.py:205
  79.7 0.0 collective-permute-done.6
  79.7 0.0 collective-permute-done.7
  79.7 11.3 %smooth.2.refs_2_ = f32[4,16,64,256]{3,2,1,0:T(8,128)S(1)} custom-call(f32[16,4,27,256]{3,2,1,0:T(8,128)S(1)} %copy.17.weight_ref, bf16[2,16,64,256]{3,2,1,0:T(8,128)(2,1)} %bitcast.10.refs_0_, bf16[2,16,64,256]{3,2,1,0:T(8,128)(2,1)S(1)} %bitcast.27, bf16[2,16,64,256]{3,2,1,0:T(8,128)(2,1)} %bitcast.12.refs_2_, bf16[2,16,64,256]{3,2,1,0:T(8,128)(2,1)} %bitcast.13.refs_3_), custom_call_target="tpu_custom_call" | custom-call | flops 1363148800 | bytes 8388608 | tf_op jit(solution)/shard_map/smooth/pallas_call | solution.py:172
  91.1 0.0 collective-permute-done.2
  91.1 0.0 collective-permute-done.3
  91.1 4.1 %smooth.3 = bf16[4,16,64,256]{3,2,1,0:T(8,128)(2,1)S(1)} custom-call(f32[16,4,27,256]{3,2,1,0:T(8,128)S(1)} %copy.17.weight_ref, bf16[2,16,64,256]{3,2,1,0:T(8,128)(2,1)S(1)} %bitcast.28, bf16[2,16,64,256]{3,2,1,0:T(8,128)(2,1)S(1)} %bitcast.29, f32[4,16,64,256]{3,2,1,0:T(8,128)S(1)} %smooth.2.refs_2_), custom_call_target="tpu_custom_call" | custom-call | flops 524288000 | bytes 8388608 | tf_op jit(solution)/shard_map/smooth/pallas_call | solution.py:172
  95.2 2.9 %copy.18 = bf16[64,16,4,256]{3,2,1,0:T(4,128)(2,1)} copy(bf16[64,16,4,256]{3,0,1,2:T(8,128)(2,1)S(1)} %bitcast.23) | data formatting | bytes 4194304 | tf_op jit(solution)/shard_map/transpose | solution.py:261
  (3 shorter events, 0.0 us)
Async XLA Ops:
  3.0 13.8 %copy-start.7 = (s32[64]{0:T(128)S(1)}, s32[64]{0:T(128)}, u32[]{:S(2)}) copy-start(s32[64]{0:T(128)} %param.8) | copy-start | bytes 772
  3.0 13.9 %copy-start.4 = (bf16[64,64,33]{1,0,2:T(8,128)(2,1)S(1)}, bf16[64,64,33]{1,0,2:T(8,128)(2,1)}, u32[]{:S(2)}) copy-start(bf16[64,64,33]{1,0,2:T(8,128)(2,1)} %param.7) | copy-start | bytes 811012
  4.2 33.7 %collective-permute-start.4 = (bf16[2,656,256]{2,1,0:T(8,128)(2,1)}, bf16[2,656,256]{2,1,0:T(8,128)(2,1)S(1)}, u32[]{:S(2)}, u32[]{:S(2)}) collective-permute-start(bf16[2,656,256]{2,1,0:T(8,128)(2,1)} %get-tuple-element.9), channel_id=1, source_target_pairs={{0,8},{8,16},{16,24},{1,9},{9,17},{17,25},{2,10},{10,18},{18,26},{... | collective-permute-start | bytes 2015240 | tf_op jit(solution)/shard_map/ppermute | solution.py:216
  9.3 27.7 %collective-permute-start.5 = (bf16[2,592,256]{2,1,0:T(8,128)(2,1)}, bf16[2,592,256]{2,1,0:T(8,128)(2,1)S(1)}, u32[]{:S(2)}, u32[]{:S(2)}) collective-permute-start(bf16[2,592,256]{2,1,0:T(8,128)(2,1)} %get-tuple-element.11), channel_id=1, source_target_pairs={{8,0},{16,8},{24,16},{9,1},{17,9},{25,17},{10,2},{18,10},{26,18},{... | collective-permute-start | bytes 1818632 | tf_op jit(solution)/shard_map/ppermute | solution.py:216
  10.6 53.9 %collective-permute-start = (bf16[2,656,256]{2,1,0:T(8,128)(2,1)}, bf16[2,656,256]{2,1,0:T(8,128)(2,1)}, u32[]{:S(2)}, u32[]{:S(2)}) collective-permute-start(bf16[2,656,256]{2,1,0:T(8,128)(2,1)} %get-tuple-element.10), channel_id=1, source_target_pairs={{0,8},{8,16},{16,24},{1,9},{9,17},{17,25},{2,10},{10,18},{18,26},{... | collective-permute-start | bytes 2015240 | tf_op jit(solution)/shard_map/ppermute | solution.py:216
  15.5 49.0 %collective-permute-start.1 = (bf16[2,592,256]{2,1,0:T(8,128)(2,1)}, bf16[2,592,256]{2,1,0:T(8,128)(2,1)}, u32[]{:S(2)}, u32[]{:S(2)}) collective-permute-start(bf16[2,592,256]{2,1,0:T(8,128)(2,1)} %get-tuple-element.12), channel_id=1, source_target_pairs={{8,0},{16,8},{24,16},{9,1},{17,9},{25,17},{10,2},{18,10},{26,18},{... | collective-permute-start | bytes 1818632 | tf_op jit(solution)/shard_map/ppermute | solution.py:216
  37.0 0.8 copy-start.2
  37.9 0.8 copy-start
  38.7 1.1 %copy-start.1 = (bf16[2,656,256]{2,1,0:T(8,128)(2,1)S(1)}, bf16[2,656,256]{2,1,0:T(8,128)(2,1)}, u32[]{:S(2)}) copy-start(bf16[2,656,256]{2,1,0:T(8,128)(2,1)} %copy-done) | copy-start | bytes 2015236
  39.8 1.1 %copy-start.3 = (bf16[2,592,256]{2,1,0:T(8,128)(2,1)S(1)}, bf16[2,592,256]{2,1,0:T(8,128)(2,1)}, u32[]{:S(2)}) copy-start(bf16[2,592,256]{2,1,0:T(8,128)(2,1)} %copy-done.2) | copy-start | bytes 1818628
  43.7 32.2 %copy-start.6 = (f32[8,27]{1,0:T(8,128)S(1)}, f32[8,27]{1,0:T(8,128)}, u32[]{:S(2)}) copy-start(f32[8,27]{1,0:T(8,128)} %param.9) | copy-start | bytes 2596
  43.7 32.3 %copy-start.5 = (s32[16,4,256]{2,1,0:T(4,128)S(1)}, s32[16,4,256]{2,1,0:T(4,128)}, u32[]{:S(2)}) copy-start(s32[16,4,256]{2,1,0:T(4,128)} %param.6) | copy-start | bytes 196612
  43.8 36.0 %collective-permute-start.6 = (bf16[2,1024,256]{2,1,0:T(8,128)(2,1)S(1)}, bf16[2,1024,256]{2,1,0:T(8,128)(2,1)}, u32[]{:S(2)}, u32[]{:S(2)}) collective-permute-start(bf16[2,1024,256]{2,1,0:T(8,128)(2,1)S(1)} %slant_stack.3), channel_id=1, source_target_pairs={{0,1},{1,2},{2,3},{3,4},{4,5},{5,6},{6,7},{8,9},{9,10},{10,11},{11... | collective-permute-start | bytes 3145736 | tf_op jit(solution)/shard_map/ppermute | solution.py:243
  49.7 30.1 %collective-permute-start.7 = (bf16[2,1024,256]{2,1,0:T(8,128)(2,1)S(1)}, bf16[2,1024,256]{2,1,0:T(8,128)(2,1)}, u32[]{:S(2)}, u32[]{:S(2)}) collective-permute-start(bf16[2,1024,256]{2,1,0:T(8,128)(2,1)S(1)} %slant_stack.3), channel_id=1, source_target_pairs={{1,0},{2,1},{3,2},{4,3},{5,4},{6,5},{7,6},{9,8},{10,9},{11,10},{12... | collective-permute-start | bytes 3145736 | tf_op jit(solution)/shard_map/ppermute | solution.py:244
  69.2 21.8 %collective-permute-start.2 = (bf16[2,1024,256]{2,1,0:T(8,128)(2,1)}, bf16[2,1024,256]{2,1,0:T(8,128)(2,1)S(1)}, u32[]{:S(2)}, u32[]{:S(2)}) collective-permute-start(bf16[2,1024,256]{2,1,0:T(8,128)(2,1)} %slant_stack.2), channel_id=1, source_target_pairs={{0,1},{1,2},{2,3},{3,4},{4,5},{5,6},{6,7},{8,9},{9,10},{10,11},{11... | collective-permute-start | bytes 3145736 | tf_op jit(solution)/shard_map/ppermute | solution.py:243
  73.9 17.2 %collective-permute-start.3 = (bf16[2,1024,256]{2,1,0:T(8,128)(2,1)}, bf16[2,1024,256]{2,1,0:T(8,128)(2,1)S(1)}, u32[]{:S(2)}, u32[]{:S(2)}) collective-permute-start(bf16[2,1024,256]{2,1,0:T(8,128)(2,1)} %slant_stack.2), channel_id=1, source_target_pairs={{1,0},{2,1},{3,2},{4,3},{5,4},{6,5},{7,6},{9,8},{10,9},{11,10},{12... | collective-permute-start | bytes 3145736 | tf_op jit(solution)/shard_map/ppermute | solution.py:244

commit v3 on v2

--- a/solution.py
+++ b/solution.py
@@ -151,9 +151,9 @@
                     tap = i * (2 * RY + 1) + j
                     term = weight_ref[0, x, tap : tap + 1, :] * plane
                     sums[j] = term if sums[j] is None else sums[j] + term
-            total = sums[RY]
+            total = sums[RY] if sources[x] else jnp.zeros((step, cross), jnp.float32)
             for j in range(2 * RY + 1):
-                if j != RY:
+                if j != RY and sources[x]:
                     total = total + pltpu.roll(sums[j], (RY - j) % cross, 1)
             if len(refs) > count + 1:
                 total = total + refs[count][x, 0, first : first + step, :]
@@ -211,9 +211,31 @@
     return up, [(j, i) for i, j in up]
 
 
-def halo_of(last, leading):
-    up, down = neighbours("depth")
-    return lax.ppermute(last, "depth", up), lax.ppermute(leading, "depth", down)
+def halos_of(last, leading, cols):
+    lateral = last.shape[0]
+    chunks = [(last[c : c + cols], leading[c : c + cols]) for c in range(0, lateral, cols)]
+    if lax.axis_size("depth") != 4 or last.shape[1] < leading.shape[1]:
+        up, down = neighbours("depth")
+        return [
+            (lax.ppermute(upper, "depth", up), lax.ppermute(lower, "depth", down))
+            for upper, lower in chunks
+        ]
+    place = lax.axis_index("depth")
+    rows, columns = ([(1, 0), (2, 3)], [(1, 3), (2, 0)])
+    next_rows, next_columns = ([(0, 1), (3, 2)], [(0, 2), (3, 1)])
+    pad = last.shape[1] - leading.shape[1]
+    relays, results = [], []
+    for index, (upper, lower) in enumerate(chunks):
+        crossing = jnp.where(place == 1, upper, jnp.pad(lower, ((0, 0), (0, pad), (0, 0))))
+        relays.append(lax.ppermute(crossing, "depth", columns if index % 2 else rows))
+    for index, (upper, lower) in enumerate(chunks):
+        from_above = lax.ppermute(upper, "depth", [(0, 1), (2, 3)])
+        from_below = lax.ppermute(lower, "depth", [(1, 0), (3, 2)])
+        crossed = lax.ppermute(relays[index], "depth", next_rows if index % 2 else next_columns)
+        from_above = jnp.where(place == 2, crossed, from_above)
+        from_below = jnp.where(place == 1, crossed[:, : lower.shape[1]], from_below)
+        results.append((from_above, from_below))
+    return results
 
 
 def local(offset_image, dip_class, slant_taper, band_offsets, coefficients):
@@ -228,14 +250,32 @@
     group = GROUP if depth_cells % GROUP == 0 else depth_cells
     by_column = jnp.transpose(offset_image, (2, 1, 0, 3))
     last, leading = pack(by_column, upper, lower)
-    halos = [
-        halo_of(last[first : first + cols], leading[first : first + cols])
-        for first in range(0, lateral, cols)
-    ]
+    halos = halos_of(last, leading, cols)
     matrix = stack_matrix(slant_matrix_of(slant_taper, band_offsets, offset_count), group)
     weights = dip_weights(dip_class, coefficients)
+    matrix, weights = lax.optimization_barrier((matrix, weights))
     mine, before, after = [], [], []
+    count = len(halos)
+    chunks = [(p, c) for p in range(3 * count) for c in range(cols)]
+    chunks = chunks[lateral - RX : 2 * lateral + RX]
+
+    def add_planes(stage, parts, out, kind):
+        sources = [
+            [(i,) + chunks[x + i] for i in range(2 * RX + 1) if chunks[x + i][0] in stage]
+            for x in range(lateral)
+        ]
+        if not any(sources):
+            return out
+        return smooth(weights, parts, sources, out, lateral, depth_cells, angles, kind)
+
+    own = set(range(count, 2 * count - 1))
+    final = {count - 1, 3 * count - 1}
+    out = None
     for index, (from_above, from_below) in enumerate(halos):
+        if index == count - 1:
+            out = add_planes(own, [None] * count + mine, None, jnp.float32)
+            if out is not None:
+                out, by_column = lax.optimization_barrier((out, by_column))
         part = slant_stack(
             matrix, group, from_above, by_column, from_below, upper, lower, index * cols, cols
         )
@@ -243,21 +283,8 @@
         before.append(lax.ppermute(part, "gx", right))
         after.append(lax.ppermute(part, "gx", left))
     parts = before + mine + after
-    chunks = [(p, c) for p in range(len(parts)) for c in range(cols)]
-    chunks = chunks[lateral - RX : 2 * lateral + RX]
-    count = len(mine)
-    final = {count - 1, 3 * count - 1} if count > 1 else set()
-    early, late = [], []
-    for x in range(lateral):
-        planes = [(i,) + chunks[x + i] for i in range(2 * RX + 1)]
-        early.append([p for p in planes if p[1] not in final])
-        late.append([p for p in planes if p[1] in final])
-    sizes = (lateral, depth_cells, angles)
-    if all(late):
-        out = smooth(weights, parts, early, None, *sizes, jnp.float32)
-        out = smooth(weights, parts, late, out, *sizes, jnp.bfloat16)
-    else:
-        out = smooth(weights, parts, [e + l for e, l in zip(early, late)], None, *sizes, jnp.bfloat16)
+    out = add_planes(set(range(3 * count)) - own - final, parts, out, jnp.float32)
+    out = add_planes(final, parts, out, jnp.bfloat16)
     return jnp.transpose(out, (2, 1, 0, 3))
 
 

time: 99.3 us -> 116 us (1.17)
  waiting for transfers between devices: 27.7 us -> 40.9 us
  other arithmetic: 2.07 us -> 8.62 us
  starting transfers between devices: 25.9 us -> 31.1 us
  local copies, waits for them, and re-layouts: 17.6 us -> 13.3 us
  Pallas kernels: 23.3 us -> 19.8 us
    ppermute x4 -> x8, waiting for transfers between devices: 27.7 us -> 35 us  [the longest x2 24.9 us: halos_of(): lax.ppermute(crossing, 'depth', columns if index % 2 else rows)]
    ppermute x4 -> x8, starting transfers between devices: 11.4 us -> 16.4 us  [the longest x2 8.63 us: halos_of(): from_above = lax.ppermute(upper, 'depth', [(0, 1), (2, 3)])]
    ppermute x2, waiting for transfers between devices: 0.01 us -> 4.67 us  [local(): after.append(lax.ppermute(part, 'gx', left))]
    unnamed x18 -> x12, local copies, waits for them, and re-layouts: 6.71 us -> 2.88 us
    select_n x0 -> x4, other arithmetic: none -> 3.52 us  [the longest x2 2.29 us: halos_of(): from_below = jnp.where(place == 1, crossed[:, :lower.shape[1]], from_below)]
    slice x0 -> x1, other arithmetic: none -> 3.06 us  [halos_of(): last[c:c + cols]]
    optimization_barrier x0 -> x1, local copies, waits for them, and re-layouts: none -> 2.59 us  [local(): matrix, weights = lax.optimization_barrier((matrix, weights))]
    pallas_call x2, Pallas kernels: 7.57 us -> 5.76 us  [slant_stack(): pl.pallas_call(functools.partial(stack_kernel, upper[0], lower[0], group)...]
  transfers between devices with their start and end apart: 8 -> 12, of which waited for: 2 -> 5; matrix products, arithmetic and copies ran while one was open for 10% -> 14% of each run, Pallas kernels for 19% -> 13%
where the time goes in v3:
time: 116 us; the launch traced here: 115 us
  waiting for transfers between devices  40.9 us (35%)
  starting transfers between devices  31.1 us (27%)
  Pallas kernels  19.8 us (17%)
  local copies, waits for them, and re-layouts  13.3 us (11%)
  other arithmetic  8.62 us (7%)
  matrix products  1.38 us (1%)
    ppermute x2, waiting for transfers between devices, halos_of(): lax.ppermute(crossing, 'depth', columns if index % 2 else rows)  24.9 us
    pallas_call x3, Pallas kernels, smooth(): pl.pallas_call(functools.partial(smooth_kernel, sources), grid=(depth_cel...  13.8 us
    ppermute x2, waiting for transfers between devices, halos_of(): lax.ppermute(relays[index], 'depth', next_rows if index % 2 else next_col...  10.1 us
    ppermute x2, starting transfers between devices, local(): before.append(lax.ppermute(part, 'gx', right))  8.95 us
    ppermute x2, starting transfers between devices, halos_of(): from_above = lax.ppermute(upper, 'depth', [(0, 1), (2, 3)])  8.63 us
    ppermute x2, starting transfers between devices, local(): after.append(lax.ppermute(part, 'gx', left))  5.77 us
    pallas_call x2, Pallas kernels, slant_stack(): pl.pallas_call(functools.partial(stack_kernel, upper[0], lower[0], group)...  5.76 us
    ppermute x2, waiting for transfers between devices, local(): after.append(lax.ppermute(part, 'gx', left))  4.67 us
  transfers between devices with their start and end apart: 12, of which 5 were waited for; matrix products, arithmetic and copies ran while one was open for 14% of the time, Pallas kernels for 13%

profile of v3, /device:TPU:1, one launch (start us, length us, event | category | flops | bytes accessed | tf_op | source)
XLA Modules:
  0.0 115.5 jit_solution(6348547219896382881)
XLA Ops:
  0.0 2.8 %copy.26 = bf16[64,16,4,256]{3,0,1,2:T(8,128)(2,1)S(1)} copy(bf16[64,16,4,256]{3,2,1,0:T(4,128)(2,1)} %param.5) | data formatting | bytes 4194304 | tf_op args[0]
  2.8 0.2 pack.1
  3.0 1.1 fusion.19
  4.1 1.3 %collective-permute-start.6 = (bf16[2,592,256]{2,1,0:T(8,128)(2,1)}, bf16[2,592,256]{2,1,0:T(8,128)(2,1)}, u32[]{:S(2)}, u32[]{:S(2)}) collective-permute-start(bf16[2,592,256]{2,1,0:T(8,128)(2,1)} %get-tuple-element.21), channel_id=1, source_target_pairs={{8,0},{24,16},{9,1},{25,17},{10,2},{26,18},{11,3},{27,19},{12,4},{... | collective-permute-start | bytes 1818632 | tf_op jit(solution)/shard_map/ppermute | solution.py:233
  5.4 1.3 %collective-permute-start.7 = (bf16[2,592,256]{2,1,0:T(8,128)(2,1)}, bf16[2,592,256]{2,1,0:T(8,128)(2,1)}, u32[]{:S(2)}, u32[]{:S(2)}) collective-permute-start(bf16[2,592,256]{2,1,0:T(8,128)(2,1)} %get-tuple-element.22), channel_id=1, source_target_pairs={{8,0},{24,16},{9,1},{25,17},{10,2},{26,18},{11,3},{27,19},{12,4},{... | collective-permute-start | bytes 1818632 | tf_op jit(solution)/shard_map/ppermute | solution.py:233
  6.7 0.0 copy-start.2
  6.7 0.0 copy-start.3
  6.8 3.1 %fusion.18 = (bf16[2,656,256]{2,1,0:T(8,128)(2,1)}, bf16[2,656,256]{2,1,0:T(8,128)(2,1)}, bf16[2,656,256]{2,1,0:T(8,128)(2,1)}, bf16[2,656,256]{2,1,0:T(8,128)(2,1)}) fusion(bf16[4,656,256]{2,1,0:T(8,128)(2,1)S(1)} %get-tuple-element.13, bf16[2,592,256]{2,1,0:T(8,128)(2,1)} %get-tuple-element.22, pred[]{:T(512)S(6)} %eq.27, ...), kind=kLoop, calls=%fused_computation.44 | loop fusion | flops 671744 | bytes 5242881 | tf_op jit(solution)/shard_map/slice | solution.py:216
  9.8 1.3 %collective-permute-start.3 = (bf16[2,656,256]{2,1,0:T(8,128)(2,1)}, bf16[2,656,256]{2,1,0:T(8,128)(2,1)}, u32[]{:S(2)}, u32[]{:S(2)}) collective-permute-start(bf16[2,656,256]{2,1,0:T(8,128)(2,1)} %get-tuple-element.19), channel_id=1, source_target_pairs={{8,0},{16,24},{9,1},{17,25},{10,2},{18,26},{11,3},{19,27},{12,4},{... | collective-permute-start | bytes 2015240 | tf_op jit(solution)/shard_map/ppermute | solution.py:230
  11.1 7.3 %collective-permute-start.5 = (bf16[2,656,256]{2,1,0:T(8,128)(2,1)}, bf16[2,656,256]{2,1,0:T(8,128)(2,1)}, u32[]{:S(2)}, u32[]{:S(2)}) collective-permute-start(bf16[2,656,256]{2,1,0:T(8,128)(2,1)} %get-tuple-element.17), channel_id=1, source_target_pairs={{0,8},{16,24},{1,9},{17,25},{2,10},{18,26},{3,11},{19,27},{4,12},{... | collective-permute-start | bytes 2015240 | tf_op jit(solution)/shard_map/ppermute | solution.py:232
  18.4 1.3 %collective-permute-start = (bf16[2,656,256]{2,1,0:T(8,128)(2,1)}, bf16[2,656,256]{2,1,0:T(8,128)(2,1)}, u32[]{:S(2)}, u32[]{:S(2)}) collective-permute-start(bf16[2,656,256]{2,1,0:T(8,128)(2,1)} %get-tuple-element.18), channel_id=1, source_target_pairs={{8,24},{16,0},{9,25},{17,1},{10,26},{18,2},{11,27},{19,3},{12,28},... | collective-permute-start | bytes 2015240 | tf_op jit(solution)/shard_map/ppermute | solution.py:230
  19.7 0.0 copy-done.2
  19.7 0.1 fusion.12
  19.9 0.0 copy-done.3
  19.9 0.1 copy.12
  20.0 1.4 %convolution_bitcast_fusion = f32[16,4,9,3,256]{4,2,1,0,3:T(8,128)S(1)} fusion(s32[3,16,4,256]{3,2,1,0:T(4,128)S(1)} %pad_add_fusion, f32[8,9,3,1,1]{0,2,1,4,3:T(4,128)S(1)} %bitcast.35), kind=kOutput, calls=%fused_computation.13 | convolution fusion | flops 42860544 | bytes 1966944 | tf_op jit(solution)/shard_map/qij,jzxqy->zxijy/dot_general | solution.py:199
  21.4 0.0 copy-start.4
  21.4 0.0 copy-start.1
  21.4 2.2 %copy.14 = f32[16,4,9,3,256]{4,0,3,2,1:T(8,128)} copy(f32[16,4,9,3,256]{4,2,1,0,3:T(8,128)S(1)} %convolution_bitcast_fusion) | data formatting | bytes 3538944 | tf_op jit(solution)/shard_map/qij,jzxqy->zxijy/transpose | solution.py:199
  23.6 0.0 copy-done.4
  23.6 0.1 add_select_fusion
  23.7 24.9 %collective-permute-done.3 = bf16[2,656,256]{2,1,0:T(8,128)(2,1)} collective-permute-done((bf16[2,656,256]{2,1,0:T(8,128)(2,1)}, bf16[2,656,256]{2,1,0:T(8,128)(2,1)}, u32[]{:S(2)}, u32[]{:S(2)}) %collective-permute-start.3) | collective-permute-done | bytes 671776 | tf_op jit(solution)/shard_map/ppermute | solution.py:230
  48.6 1.3 %collective-permute-start.4 = (bf16[2,656,256]{2,1,0:T(8,128)(2,1)}, bf16[2,656,256]{2,1,0:T(8,128)(2,1)S(1)}, u32[]{:S(2)}, u32[]{:S(2)}) collective-permute-start(bf16[2,656,256]{2,1,0:T(8,128)(2,1)} %collective-permute-done.3), channel_id=1, source_target_pairs={{0,16},{24,8},{1,17},{25,9},{2,18},{26,10},{3,19},{27,11},{4,20},{... | collective-permute-start | bytes 2015240 | tf_op jit(solution)/shard_map/ppermute | solution.py:234
  50.0 0.0 copy-done.1
  50.0 0.3 fusion.11
  50.3 0.4 copy.11
  50.7 1.1 reshape.68
  51.8 1.6 %fusion.7.matrix_ref = bf16[256,2304]{1,0:T(8,128)(2,1)S(1)} fusion(bf16[64,2112]{1,0:T(8,128)(2,1)} %reshape.68), kind=kLoop, calls=%fused_computation.16 | loop fusion | flops 11796480 | bytes 1449984 | tf_op jit(solution)/shard_map/concatenate | solution.py:45
  53.3 0.0 copy-start
  53.3 2.6 %copy.18.weight_ref = f32[16,4,27,256]{3,2,1,0:T(8,128)S(1)} copy(f32[16,4,27,256]{3,0,2,1:T(8,128)} %bitcast.33) | data formatting | bytes 3538944 | tf_op jit(solution)/shard_map/optimization_barrier | solution.py:256
  55.9 0.0 collective-permute-done.5
  56.0 0.0 copy-done
  56.0 1.3 %collective-permute-start.2 = (bf16[2,656,256]{2,1,0:T(8,128)(2,1)S(1)}, bf16[2,656,256]{2,1,0:T(8,128)(2,1)S(1)}, u32[]{:S(2)}, u32[]{:S(2)}) collective-permute-start(bf16[2,656,256]{2,1,0:T(8,128)(2,1)S(1)} %copy-done), channel_id=1, source_target_pairs={{0,8},{16,24},{1,9},{17,25},{2,10},{18,26},{3,11},{19,27},{4,12},{... | collective-permute-start | bytes 2015240 | tf_op jit(solution)/shard_map/ppermute | solution.py:232
  57.3 0.0 collective-permute-done
  57.3 1.3 %collective-permute-start.1 = (bf16[2,656,256]{2,1,0:T(8,128)(2,1)}, bf16[2,656,256]{2,1,0:T(8,128)(2,1)S(1)}, u32[]{:S(2)}, u32[]{:S(2)}) collective-permute-start(bf16[2,656,256]{2,1,0:T(8,128)(2,1)} %collective-permute-done), channel_id=1, source_target_pairs={{0,8},{24,16},{1,9},{25,17},{2,10},{26,18},{3,11},{27,19},{4,12},{... | collective-permute-start | bytes 2015240 | tf_op jit(solution)/shard_map/ppermute | solution.py:234
  58.7 5.0 %collective-permute-done.4 = bf16[2,656,256]{2,1,0:T(8,128)(2,1)S(1)} collective-permute-done((bf16[2,656,256]{2,1,0:T(8,128)(2,1)}, bf16[2,656,256]{2,1,0:T(8,128)(2,1)S(1)}, u32[]{:S(2)}, u32[]{:S(2)}) %collective-permute-start.4) | collective-permute-done | bytes 671776 | tf_op jit(solution)/shard_map/ppermute | solution.py:234
  63.7 1.2 %broadcast_select_fusion.above_ref = bf16[2,656,256]{2,1,0:T(8,128)(2,1)S(1)} fusion(bf16[2,656,256]{2,1,0:T(8,128)(2,1)S(1)} %collective-permute-done.4, bf16[2,656,256]{2,1,0:T(8,128)(2,1)} %collective-permute-done.5, pred[]{:T(512)S(6)} %eq.26), kind=kLoop, calls=%fused_computation.23 | loop fusion | flops 335872 | bytes 2015233 | tf_op jit(solution)/shard_map/jit(_where)/select_n | solution.py:235
  64.9 0.0 collective-permute-done.6
  64.9 1.1 slice_select_fusion.1.below_ref
  66.0 2.9 %slant_stack.2 = bf16[2,1024,256]{2,1,0:T(8,128)(2,1)S(1)} custom-call(bf16[256,2304]{1,0:T(8,128)(2,1)S(1)} %fusion.7.matrix_ref, bf16[2,656,256]{2,1,0:T(8,128)(2,1)S(1)} %broadcast_select_fusion.above_ref, bf16[4,16,64,256]{3,2,1,0:T(8,128)(2,1)S(1)} %bitcast.25, bf16[2,592,256]{2,1,0:T(8,128)(2,1)S(1)} %slice_select_fusion.1.below_ref), custom_call_target="tpu_custom_call" | custom-call | flops 2415919104 | bytes 4587520 | tf_op jit(solution)/shard_map/slant_stack/pallas_call | solution.py:118
  68.9 5.4 %collective-permute-start.10 = (bf16[2,1024,256]{2,1,0:T(8,128)(2,1)S(1)}, bf16[2,1024,256]{2,1,0:T(8,128)(2,1)S(1)}, u32[]{:S(2)}, u32[]{:S(2)}) collective-permute-start(bf16[2,1024,256]{2,1,0:T(8,128)(2,1)S(1)} %slant_stack.2), channel_id=1, source_target_pairs={{0,1},{1,2},{2,3},{3,4},{4,5},{5,6},{6,7},{8,9},{9,10},{10,11},{11... | collective-permute-start | bytes 3145736 | tf_op jit(solution)/shard_map/ppermute | solution.py:283
  74.3 1.9 %collective-permute-start.11 = (bf16[2,1024,256]{2,1,0:T(8,128)(2,1)S(1)}, bf16[2,1024,256]{2,1,0:T(8,128)(2,1)S(1)}, u32[]{:S(2)}, u32[]{:S(2)}) collective-permute-start(bf16[2,1024,256]{2,1,0:T(8,128)(2,1)S(1)} %slant_stack.2), channel_id=1, source_target_pairs={{1,0},{2,1},{3,2},{4,3},{5,4},{6,5},{7,6},{9,8},{10,9},{11,10},{12... | collective-permute-start | bytes 3145736 | tf_op jit(solution)/shard_map/ppermute | solution.py:284
  76.2 3.8 %smooth.3.refs_3_ = f32[4,16,64,256]{3,2,1,0:T(8,128)S(1)} custom-call(f32[16,4,27,256]{3,2,1,0:T(8,128)S(1)} %copy.18.weight_ref, bf16[2,16,64,256]{3,2,1,0:T(8,128)(2,1)S(1)} %bitcast.27), custom_call_target="tpu_custom_call" | custom-call | flops 419430400 | bytes 8388608 | tf_op jit(solution)/shard_map/smooth/pallas_call | solution.py:172
  80.0 0.0 collective-permute-done.2
  80.1 5.0 %collective-permute-done.1 = bf16[2,656,256]{2,1,0:T(8,128)(2,1)S(1)} collective-permute-done((bf16[2,656,256]{2,1,0:T(8,128)(2,1)}, bf16[2,656,256]{2,1,0:T(8,128)(2,1)S(1)}, u32[]{:S(2)}, u32[]{:S(2)}) %collective-permute-start.1) | collective-permute-done | bytes 671776 | tf_op jit(solution)/shard_map/ppermute | solution.py:234
  85.1 0.1 broadcast_select_fusion.1.above_ref
  85.2 0.0 collective-permute-done.7
  85.2 1.1 slice_select_fusion.below_ref
  86.3 2.9 %slant_stack.3 = bf16[2,1024,256]{2,1,0:T(8,128)(2,1)S(1)} custom-call(bf16[256,2304]{1,0:T(8,128)(2,1)S(1)} %fusion.7.matrix_ref, bf16[2,656,256]{2,1,0:T(8,128)(2,1)S(1)} %broadcast_select_fusion.1.above_ref, bf16[4,16,64,256]{3,2,1,0:T(8,128)(2,1)S(1)} %bitcast.26, bf16[2,592,256]{2,1,0:T(8,128)(2,1)S(1)} %slice_select_fusion.below_ref), custom_call_target="tpu_custom_call" | custom-call | flops 2415919104 | bytes 4587520 | tf_op jit(solution)/shard_map/slant_stack/pallas_call | solution.py:118
  89.2 3.8 %collective-permute-start.9 = (bf16[2,1024,256]{2,1,0:T(8,128)(2,1)S(1)}, bf16[2,1024,256]{2,1,0:T(8,128)(2,1)S(1)}, u32[]{:S(2)}, u32[]{:S(2)}) collective-permute-start(bf16[2,1024,256]{2,1,0:T(8,128)(2,1)S(1)} %slant_stack.3), channel_id=1, source_target_pairs={{1,0},{2,1},{3,2},{4,3},{5,4},{6,5},{7,6},{9,8},{10,9},{11,10},{12... | collective-permute-start | bytes 3145736 | tf_op jit(solution)/shard_map/ppermute | solution.py:284
  93.1 3.6 %collective-permute-start.8 = (bf16[2,1024,256]{2,1,0:T(8,128)(2,1)S(1)}, bf16[2,1024,256]{2,1,0:T(8,128)(2,1)S(1)}, u32[]{:S(2)}, u32[]{:S(2)}) collective-permute-start(bf16[2,1024,256]{2,1,0:T(8,128)(2,1)S(1)} %slant_stack.3), channel_id=1, source_target_pairs={{0,1},{1,2},{2,3},{3,4},{4,5},{5,6},{6,7},{8,9},{9,10},{10,11},{11... | collective-permute-start | bytes 3145736 | tf_op jit(solution)/shard_map/ppermute | solution.py:283
  96.7 0.0 collective-permute-done.10
  96.7 0.0 collective-permute-done.11
  96.7 5.8 %smooth.4.refs_2_ = f32[4,16,64,256]{3,2,1,0:T(8,128)S(1)} custom-call(f32[16,4,27,256]{3,2,1,0:T(8,128)S(1)} %copy.18.weight_ref, bf16[2,16,64,256]{3,2,1,0:T(8,128)(2,1)S(1)} %bitcast.30, bf16[2,16,64,256]{3,2,1,0:T(8,128)(2,1)S(1)} %bitcast.32, bf16[2,16,64,256]{3,2,1,0:T(8,128)(2,1)S(1)} %bitcast.31, f32[4,16,64,256]{3,2,1,0:T(8,128)S(1)} %smooth.3.refs_3_), custom_call_target="tpu_custom_call" | custom-call | flops 943718400 | bytes 8388608 | tf_op jit(solution)/shard_map/smooth/pallas_call | solution.py:172
  102.5 4.7 %collective-permute-done.9 = bf16[2,1024,256]{2,1,0:T(8,128)(2,1)S(1)} collective-permute-done((bf16[2,1024,256]{2,1,0:T(8,128)(2,1)S(1)}, bf16[2,1024,256]{2,1,0:T(8,128)(2,1)S(1)}, u32[]{:S(2)}, u32[]{:S(2)}) %collective-permute-start.9) | collective-permute-done | bytes 1048608 | tf_op jit(solution)/shard_map/ppermute | solution.py:284
  107.2 1.2 %collective-permute-done.8 = bf16[2,1024,256]{2,1,0:T(8,128)(2,1)S(1)} collective-permute-done((bf16[2,1024,256]{2,1,0:T(8,128)(2,1)S(1)}, bf16[2,1024,256]{2,1,0:T(8,128)(2,1)S(1)}, u32[]{:S(2)}, u32[]{:S(2)}) %collective-permute-start.8) | collective-permute-done | bytes 1048608 | tf_op jit(solution)/shard_map/ppermute | solution.py:283
  108.4 4.1 %smooth.5 = bf16[4,16,64,256]{3,2,1,0:T(8,128)(2,1)S(1)} custom-call(f32[16,4,27,256]{3,2,1,0:T(8,128)S(1)} %copy.18.weight_ref, bf16[2,16,64,256]{3,2,1,0:T(8,128)(2,1)S(1)} %bitcast.29, bf16[2,16,64,256]{3,2,1,0:T(8,128)(2,1)S(1)} %bitcast.28, f32[4,16,64,256]{3,2,1,0:T(8,128)S(1)} %smooth.4.refs_2_), custom_call_target="tpu_custom_call" | custom-call | flops 524288000 | bytes 8388608 | tf_op jit(solution)/shard_map/smooth/pallas_call | solution.py:172
  112.5 2.9 %copy.19 = bf16[64,16,4,256]{3,2,1,0:T(4,128)(2,1)} copy(bf16[64,16,4,256]{3,0,1,2:T(8,128)(2,1)S(1)} %bitcast.23) | data formatting | bytes 4194304 | tf_op jit(solution)/shard_map/transpose | solution.py:288
  (3 shorter events, 0.0 us)
Async XLA Ops:
  4.1 60.7 %collective-permute-start.6 = (bf16[2,592,256]{2,1,0:T(8,128)(2,1)}, bf16[2,592,256]{2,1,0:T(8,128)(2,1)}, u32[]{:S(2)}, u32[]{:S(2)}) collective-permute-start(bf16[2,592,256]{2,1,0:T(8,128)(2,1)} %get-tuple-element.21), channel_id=1, source_target_pairs={{8,0},{24,16},{9,1},{25,17},{10,2},{26,18},{11,3},{27,19},{12,4},{... | collective-permute-start | bytes 1818632 | tf_op jit(solution)/shard_map/ppermute | solution.py:233
  5.4 79.7 %collective-permute-start.7 = (bf16[2,592,256]{2,1,0:T(8,128)(2,1)}, bf16[2,592,256]{2,1,0:T(8,128)(2,1)}, u32[]{:S(2)}, u32[]{:S(2)}) collective-permute-start(bf16[2,592,256]{2,1,0:T(8,128)(2,1)} %get-tuple-element.22), channel_id=1, source_target_pairs={{8,0},{24,16},{9,1},{25,17},{10,2},{26,18},{11,3},{27,19},{12,4},{... | collective-permute-start | bytes 1818632 | tf_op jit(solution)/shard_map/ppermute | solution.py:233
  6.7 13.0 %copy-start.2 = (s32[16,4,256]{2,1,0:T(4,128)S(1)}, s32[16,4,256]{2,1,0:T(4,128)}, u32[]{:S(2)}) copy-start(s32[16,4,256]{2,1,0:T(4,128)} %param.6) | copy-start | bytes 196612
  6.7 13.1 %copy-start.3 = (f32[8,27]{1,0:T(8,128)S(1)}, f32[8,27]{1,0:T(8,128)}, u32[]{:S(2)}) copy-start(f32[8,27]{1,0:T(8,128)} %param.9) | copy-start | bytes 2596
  9.8 38.8 %collective-permute-start.3 = (bf16[2,656,256]{2,1,0:T(8,128)(2,1)}, bf16[2,656,256]{2,1,0:T(8,128)(2,1)}, u32[]{:S(2)}, u32[]{:S(2)}) collective-permute-start(bf16[2,656,256]{2,1,0:T(8,128)(2,1)} %get-tuple-element.19), channel_id=1, source_target_pairs={{8,0},{16,24},{9,1},{17,25},{10,2},{18,26},{11,3},{19,27},{12,4},{... | collective-permute-start | bytes 2015240 | tf_op jit(solution)/shard_map/ppermute | solution.py:230
  11.1 44.8 %collective-permute-start.5 = (bf16[2,656,256]{2,1,0:T(8,128)(2,1)}, bf16[2,656,256]{2,1,0:T(8,128)(2,1)}, u32[]{:S(2)}, u32[]{:S(2)}) collective-permute-start(bf16[2,656,256]{2,1,0:T(8,128)(2,1)} %get-tuple-element.17), channel_id=1, source_target_pairs={{0,8},{16,24},{1,9},{17,25},{2,10},{18,26},{3,11},{19,27},{4,12},{... | collective-permute-start | bytes 2015240 | tf_op jit(solution)/shard_map/ppermute | solution.py:232
  18.4 38.9 %collective-permute-start = (bf16[2,656,256]{2,1,0:T(8,128)(2,1)}, bf16[2,656,256]{2,1,0:T(8,128)(2,1)}, u32[]{:S(2)}, u32[]{:S(2)}) collective-permute-start(bf16[2,656,256]{2,1,0:T(8,128)(2,1)} %get-tuple-element.18), channel_id=1, source_target_pairs={{8,24},{16,0},{9,25},{17,1},{10,26},{18,2},{11,27},{19,3},{12,28},... | collective-permute-start | bytes 2015240 | tf_op jit(solution)/shard_map/ppermute | solution.py:230
  21.4 2.3 %copy-start.4 = (s32[64]{0:T(128)S(1)}, s32[64]{0:T(128)}, u32[]{:S(2)}) copy-start(s32[64]{0:T(128)} %param.8) | copy-start | bytes 772
  21.4 28.6 %copy-start.1 = (bf16[64,64,33]{1,0,2:T(8,128)(2,1)S(1)}, bf16[64,64,33]{1,0,2:T(8,128)(2,1)}, u32[]{:S(2)}) copy-start(bf16[64,64,33]{1,0,2:T(8,128)(2,1)} %param.7) | copy-start | bytes 811012
  48.6 15.1 %collective-permute-start.4 = (bf16[2,656,256]{2,1,0:T(8,128)(2,1)}, bf16[2,656,256]{2,1,0:T(8,128)(2,1)S(1)}, u32[]{:S(2)}, u32[]{:S(2)}) collective-permute-start(bf16[2,656,256]{2,1,0:T(8,128)(2,1)} %collective-permute-done.3), channel_id=1, source_target_pairs={{0,16},{24,8},{1,17},{25,9},{2,18},{26,10},{3,19},{27,11},{4,20},{... | collective-permute-start | bytes 2015240 | tf_op jit(solution)/shard_map/ppermute | solution.py:234
  53.3 2.6 %copy-start = (bf16[2,656,256]{2,1,0:T(8,128)(2,1)S(1)}, bf16[2,656,256]{2,1,0:T(8,128)(2,1)}, u32[]{:S(2)}) copy-start(bf16[2,656,256]{2,1,0:T(8,128)(2,1)} %get-tuple-element.20) | copy-start | bytes 2015236
  56.0 24.1 %collective-permute-start.2 = (bf16[2,656,256]{2,1,0:T(8,128)(2,1)S(1)}, bf16[2,656,256]{2,1,0:T(8,128)(2,1)S(1)}, u32[]{:S(2)}, u32[]{:S(2)}) collective-permute-start(bf16[2,656,256]{2,1,0:T(8,128)(2,1)S(1)} %copy-done), channel_id=1, source_target_pairs={{0,8},{16,24},{1,9},{17,25},{2,10},{18,26},{3,11},{19,27},{4,12},{... | collective-permute-start | bytes 2015240 | tf_op jit(solution)/shard_map/ppermute | solution.py:232
  57.3 27.8 %collective-permute-start.1 = (bf16[2,656,256]{2,1,0:T(8,128)(2,1)}, bf16[2,656,256]{2,1,0:T(8,128)(2,1)S(1)}, u32[]{:S(2)}, u32[]{:S(2)}) collective-permute-start(bf16[2,656,256]{2,1,0:T(8,128)(2,1)} %collective-permute-done), channel_id=1, source_target_pairs={{0,8},{24,16},{1,9},{25,17},{2,10},{26,18},{3,11},{27,19},{4,12},{... | collective-permute-start | bytes 2015240 | tf_op jit(solution)/shard_map/ppermute | solution.py:234
  68.9 27.7 %collective-permute-start.10 = (bf16[2,1024,256]{2,1,0:T(8,128)(2,1)S(1)}, bf16[2,1024,256]{2,1,0:T(8,128)(2,1)S(1)}, u32[]{:S(2)}, u32[]{:S(2)}) collective-permute-start(bf16[2,1024,256]{2,1,0:T(8,128)(2,1)S(1)} %slant_stack.2), channel_id=1, source_target_pairs={{0,1},{1,2},{2,3},{3,4},{4,5},{5,6},{6,7},{8,9},{9,10},{10,11},{11... | collective-permute-start | bytes 3145736 | tf_op jit(solution)/shard_map/ppermute | solution.py:283
  74.3 22.4 %collective-permute-start.11 = (bf16[2,1024,256]{2,1,0:T(8,128)(2,1)S(1)}, bf16[2,1024,256]{2,1,0:T(8,128)(2,1)S(1)}, u32[]{:S(2)}, u32[]{:S(2)}) collective-permute-start(bf16[2,1024,256]{2,1,0:T(8,128)(2,1)S(1)} %slant_stack.2), channel_id=1, source_target_pairs={{1,0},{2,1},{3,2},{4,3},{5,4},{6,5},{7,6},{9,8},{10,9},{11,10},{12... | collective-permute-start | bytes 3145736 | tf_op jit(solution)/shard_map/ppermute | solution.py:284
  89.2 18.0 %collective-permute-start.9 = (bf16[2,1024,256]{2,1,0:T(8,128)(2,1)S(1)}, bf16[2,1024,256]{2,1,0:T(8,128)(2,1)S(1)}, u32[]{:S(2)}, u32[]{:S(2)}) collective-permute-start(bf16[2,1024,256]{2,1,0:T(8,128)(2,1)S(1)} %slant_stack.3), channel_id=1, source_target_pairs={{1,0},{2,1},{3,2},{4,3},{5,4},{6,5},{7,6},{9,8},{10,9},{11,10},{12... | collective-permute-start | bytes 3145736 | tf_op jit(solution)/shard_map/ppermute | solution.py:284
  93.1 15.3 %collective-permute-start.8 = (bf16[2,1024,256]{2,1,0:T(8,128)(2,1)S(1)}, bf16[2,1024,256]{2,1,0:T(8,128)(2,1)S(1)}, u32[]{:S(2)}, u32[]{:S(2)}) collective-permute-start(bf16[2,1024,256]{2,1,0:T(8,128)(2,1)S(1)} %slant_stack.3), channel_id=1, source_target_pairs={{0,1},{1,2},{2,3},{3,4},{4,5},{5,6},{6,7},{8,9},{9,10},{10,11},{11... | collective-permute-start | bytes 3145736 | tf_op jit(solution)/shard_map/ppermute | solution.py:283

commit v4 on v3

--- a/solution.py
+++ b/solution.py
@@ -221,17 +221,21 @@
             for upper, lower in chunks
         ]
     place = lax.axis_index("depth")
-    rows, columns = ([(1, 0), (2, 3)], [(1, 3), (2, 0)])
-    next_rows, next_columns = ([(0, 1), (3, 2)], [(0, 2), (3, 1)])
+    up, down = neighbours("depth")
     pad = last.shape[1] - leading.shape[1]
-    relays, results = [], []
+    results, relays = [], {}
     for index, (upper, lower) in enumerate(chunks):
-        crossing = jnp.where(place == 1, upper, jnp.pad(lower, ((0, 0), (0, pad), (0, 0))))
-        relays.append(lax.ppermute(crossing, "depth", columns if index % 2 else rows))
+        if index % 2:
+            crossing = jnp.where(place == 1, upper, jnp.pad(lower, ((0, 0), (0, pad), (0, 0))))
+            relays[index] = lax.ppermute(crossing, "depth", [(1, 3), (2, 0)])
     for index, (upper, lower) in enumerate(chunks):
+        if index % 2 == 0:
+            results.append((lax.ppermute(upper, "depth", up), lax.ppermute(lower, "depth", down)))
+            continue
+        relayed, upper, lower = lax.optimization_barrier((relays[index], upper, lower))
+        crossed = lax.ppermute(relayed, "depth", [(0, 1), (3, 2)])
         from_above = lax.ppermute(upper, "depth", [(0, 1), (2, 3)])
         from_below = lax.ppermute(lower, "depth", [(1, 0), (3, 2)])
-        crossed = lax.ppermute(relays[index], "depth", next_rows if index % 2 else next_columns)
         from_above = jnp.where(place == 2, crossed, from_above)
         from_below = jnp.where(place == 1, crossed[:, : lower.shape[1]], from_below)
         results.append((from_above, from_below))

time: 116 us -> 90 us (0.78)
  waiting for transfers between devices: 40.9 us -> 11.8 us
  starting transfers between devices: 31.1 us -> 33.5 us
  other arithmetic: 8.62 us -> 6.6 us
  matrix products: 1.38 us -> 3.02 us
    ppermute x4, waiting for transfers between devices: 35 us -> 5.95 us  [the longest x1 5.94 us: halos_of(): relays[index] = lax.ppermute(crossing, 'depth', [(1, 3), (2, 0)])]
    ppermute x4, starting transfers between devices: 5.21 us -> 13.5 us  [the longest x1 7.49 us: halos_of(): lax.ppermute(upper, 'depth', up)]
    ppermute x2 -> x1, starting transfers between devices: 8.63 us -> 5.76 us  [halos_of(): from_above = lax.ppermute(upper, 'depth', [(0, 1), (2, 3)])]
    ppermute x2, starting transfers between devices: 5.77 us -> 3.84 us  [local(): after.append(lax.ppermute(part, 'gx', left))]
    dot_general x1, matrix products: 1.38 us -> 3.02 us  [dip_weights(): jnp.einsum('qij,jzxqy->zxijy', coefficients.reshape(classes, taps // widt...]
    optimization_barrier x1, local copies, waits for them, and re-layouts: 2.59 us -> 1.04 us  [local(): matrix, weights = lax.optimization_barrier((matrix, weights))]
    concatenate x1, other arithmetic: 1.58 us -> 0.23 us  [stack_matrix(): return jnp.concatenate(rows, axis=0)]
    ppermute x2 -> x1, starting transfers between devices: 2.57 us -> 1.28 us  [halos_of(): from_below = lax.ppermute(lower, 'depth', [(1, 0), (3, 2)])]
  transfers between devices with their start and end apart: 12 -> 10, of which waited for: 5 -> 3; matrix products, arithmetic and copies ran while one was open for 14% -> 15% of each run, Pallas kernels for 13% -> 18%
where the time goes in v4:
time: 90 us; the launch traced here: 89.4 us
  starting transfers between devices  33.5 us (37%)
  Pallas kernels  20.8 us (23%)
  local copies, waits for them, and re-layouts  13.3 us (15%)
  waiting for transfers between devices  11.8 us (13%)
  other arithmetic  6.6 us (7%)
  matrix products  3.02 us (3%)
    pallas_call x3, Pallas kernels, smooth(): pl.pallas_call(functools.partial(smooth_kernel, sources), grid=(depth_cel...  13.8 us
    ppermute x2, starting transfers between devices, local(): before.append(lax.ppermute(part, 'gx', right))  9.12 us
    ppermute x1, starting transfers between devices, halos_of(): lax.ppermute(upper, 'depth', up)  7.49 us
    pallas_call x2, Pallas kernels, slant_stack(): pl.pallas_call(functools.partial(stack_kernel, upper[0], lower[0], group)...  6.82 us
    ppermute x1, waiting for transfers between devices, halos_of(): relays[index] = lax.ppermute(crossing, 'depth', [(1, 3), (2, 0)])  5.94 us
    ppermute x1, starting transfers between devices, halos_of(): from_above = lax.ppermute(upper, 'depth', [(0, 1), (2, 3)])  5.76 us
    ppermute x2, waiting for transfers between devices, local(): after.append(lax.ppermute(part, 'gx', left))  4.71 us
    ppermute x2, starting transfers between devices, local(): after.append(lax.ppermute(part, 'gx', left))  3.84 us
  transfers between devices with their start and end apart: 10, of which 3 were waited for; matrix products, arithmetic and copies ran while one was open for 15% of the time, Pallas kernels for 18%

profile of v4, /device:TPU:1, one launch (start us, length us, event | category | flops | bytes accessed | tf_op | source)
XLA Modules:
  0.0 89.4 jit_solution(6624897483054093843)
XLA Ops:
  0.0 2.8 %copy.26 = bf16[64,16,4,256]{3,0,1,2:T(8,128)(2,1)S(1)} copy(bf16[64,16,4,256]{3,2,1,0:T(4,128)(2,1)} %param.5) | data formatting | bytes 4194304 | tf_op args[0]
  2.8 0.2 pack.1
  3.0 1.1 %fusion.19 = (bf16[2,592,256]{2,1,0:T(8,128)(2,1)}, bf16[2,592,256]{2,1,0:T(8,128)(2,1)}) fusion(bf16[4,592,256]{2,1,0:T(8,128)(2,1)S(1)} %get-tuple-element.17), kind=kLoop, calls=%fused_computation.42 | loop fusion | bytes 2424832 | tf_op jit(solution)/shard_map/slice | solution.py:216
  4.1 0.0 copy-start.1
  4.1 0.0 copy-start
  4.1 2.6 %fusion.18 = (bf16[2,656,256]{2,1,0:T(8,128)(2,1)}, bf16[2,656,256]{2,1,0:T(8,128)(2,1)}, bf16[2,656,256]{2,1,0:T(8,128)(2,1)}) fusion(bf16[4,656,256]{2,1,0:T(8,128)(2,1)S(1)} %get-tuple-element.16, bf16[2,592,256]{2,1,0:T(8,128)(2,1)} %get-tuple-element.21, pred[]{:T(512)S(6)} %eq.24), kind=kLoop, calls=%fused_computation.41 | loop fusion | flops 335872 | bytes 3964929 | tf_op jit(solution)/shard_map/slice | solution.py:216
  6.7 1.3 %collective-permute-start = (bf16[2,656,256]{2,1,0:T(8,128)(2,1)}, bf16[2,656,256]{2,1,0:T(8,128)(2,1)}, u32[]{:S(2)}, u32[]{:S(2)}) collective-permute-start(bf16[2,656,256]{2,1,0:T(8,128)(2,1)} %get-tuple-element.24), channel_id=1, source_target_pairs={{8,24},{16,0},{9,25},{17,1},{10,26},{18,2},{11,27},{19,3},{12,28},... | collective-permute-start | bytes 2015240 | tf_op jit(solution)/shard_map/ppermute | solution.py:230
  8.0 7.5 %collective-permute-start.3 = (bf16[2,656,256]{2,1,0:T(8,128)(2,1)}, bf16[2,656,256]{2,1,0:T(8,128)(2,1)}, u32[]{:S(2)}, u32[]{:S(2)}) collective-permute-start(bf16[2,656,256]{2,1,0:T(8,128)(2,1)} %get-tuple-element.23), channel_id=1, source_target_pairs={{0,8},{8,16},{16,24},{1,9},{9,17},{17,25},{2,10},{10,18},{18,26},{... | collective-permute-start | bytes 2015240 | tf_op jit(solution)/shard_map/ppermute | solution.py:233
  15.5 1.3 %collective-permute-start.4 = (bf16[2,592,256]{2,1,0:T(8,128)(2,1)}, bf16[2,592,256]{2,1,0:T(8,128)(2,1)}, u32[]{:S(2)}, u32[]{:S(2)}) collective-permute-start(bf16[2,592,256]{2,1,0:T(8,128)(2,1)} %get-tuple-element.26), channel_id=1, source_target_pairs={{8,0},{16,8},{24,16},{9,1},{17,9},{25,17},{10,2},{18,10},{26,18},{... | collective-permute-start | bytes 1818632 | tf_op jit(solution)/shard_map/ppermute | solution.py:233
  16.8 0.0 copy-done.1
  16.8 0.1 add_select_fusion
  16.9 0.0 copy-done
  16.9 0.3 fusion.11
  17.2 0.4 copy.11
  17.6 0.3 reshape.68
  18.0 0.2 fusion.7.matrix_ref
  18.2 1.0 %fusion.12 = (s32[1,16,4,256]{3,2,1,0:T(4,128)S(1)}, s32[1,16,4,256]{3,2,1,0:T(4,128)S(1)}) fusion(s32[16,4,256]{2,1,0:T(4,128)} %param.6), kind=kLoop, calls=%fused_computation.28 | loop fusion | bytes 196608 | tf_op jit(solution)/shard_map/stack | solution.py:194
  19.2 5.9 %collective-permute-done = bf16[2,656,256]{2,1,0:T(8,128)(2,1)} collective-permute-done((bf16[2,656,256]{2,1,0:T(8,128)(2,1)}, bf16[2,656,256]{2,1,0:T(8,128)(2,1)}, u32[]{:S(2)}, u32[]{:S(2)}) %collective-permute-start) | collective-permute-done | bytes 671776 | tf_op jit(solution)/shard_map/ppermute | solution.py:230
  25.2 3.5 %collective-permute-start.1 = (bf16[2,656,256]{2,1,0:T(8,128)(2,1)}, bf16[2,656,256]{2,1,0:T(8,128)(2,1)}, u32[]{:S(2)}, u32[]{:S(2)}) collective-permute-start(bf16[2,656,256]{2,1,0:T(8,128)(2,1)} %collective-permute-done), channel_id=1, source_target_pairs={{0,8},{24,16},{1,9},{25,17},{2,10},{26,18},{3,11},{27,19},{4,12},{... | collective-permute-start | bytes 2015240 | tf_op jit(solution)/shard_map/ppermute | solution.py:236
  28.7 1.3 %collective-permute-start.5 = (bf16[2,592,256]{2,1,0:T(8,128)(2,1)}, bf16[2,592,256]{2,1,0:T(8,128)(2,1)}, u32[]{:S(2)}, u32[]{:S(2)}) collective-permute-start(bf16[2,592,256]{2,1,0:T(8,128)(2,1)} %get-tuple-element.21), channel_id=1, source_target_pairs={{8,0},{24,16},{9,1},{25,17},{10,2},{26,18},{11,3},{27,19},{12,4},{... | collective-permute-start | bytes 1818632 | tf_op jit(solution)/shard_map/ppermute | solution.py:238
  30.0 0.9 pad_add_fusion
  30.8 0.8 copy.12
  31.6 5.8 %collective-permute-start.2 = (bf16[2,656,256]{2,1,0:T(8,128)(2,1)}, bf16[2,656,256]{2,1,0:T(8,128)(2,1)}, u32[]{:S(2)}, u32[]{:S(2)}) collective-permute-start(bf16[2,656,256]{2,1,0:T(8,128)(2,1)} %get-tuple-element.19), channel_id=1, source_target_pairs={{0,8},{16,24},{1,9},{17,25},{2,10},{18,26},{3,11},{19,27},{4,12},{... | collective-permute-start | bytes 2015240 | tf_op jit(solution)/shard_map/ppermute | solution.py:237
  37.4 3.0 %convolution_bitcast_fusion = f32[16,4,9,3,256]{4,2,1,0,3:T(8,128)} fusion(s32[3,16,4,256]{3,2,1,0:T(4,128)S(1)} %pad_add_fusion, f32[8,9,3,1,1]{0,2,1,4,3:T(4,128)S(1)} %bitcast.35), kind=kOutput, calls=%fused_computation.13 | convolution fusion | flops 42860544 | bytes 1966944 | tf_op jit(solution)/shard_map/qij,jzxqy->zxijy/dot_general | solution.py:199
  40.4 2.9 %copy.14 = f32[16,4,9,3,256]{4,0,3,2,1:T(8,128)S(1)} copy(f32[16,4,9,3,256]{4,2,1,0,3:T(8,128)} %convolution_bitcast_fusion) | data formatting | bytes 3538944 | tf_op jit(solution)/shard_map/qij,jzxqy->zxijy/transpose | solution.py:199
  43.3 1.0 %copy.18.weight_ref = f32[16,4,27,256]{3,2,1,0:T(8,128)S(1)} copy(f32[16,4,27,256]{3,0,2,1:T(8,128)S(1)} %bitcast.33) | data formatting | bytes 3538944 | tf_op jit(solution)/shard_map/optimization_barrier | solution.py:260
  44.4 0.0 collective-permute-done.4.below_ref
  44.4 0.0 collective-permute-done.3.above_ref
  44.4 3.9 %slant_stack.2 = bf16[2,1024,256]{2,1,0:T(8,128)(2,1)S(1)} custom-call(bf16[256,2304]{1,0:T(8,128)(2,1)S(1)} %fusion.7.matrix_ref, bf16[2,656,256]{2,1,0:T(8,128)(2,1)} %collective-permute-done.3.above_ref, bf16[4,16,64,256]{3,2,1,0:T(8,128)(2,1)S(1)} %bitcast.25, bf16[2,592,256]{2,1,0:T(8,128)(2,1)} %collective-permute-done.4.below_ref), custom_call_target="tpu_custom_call" | custom-call | flops 2415919104 | bytes 4587520 | tf_op jit(solution)/shard_map/slant_stack/pallas_call | solution.py:118
  48.3 5.5 %collective-permute-start.8 = (bf16[2,1024,256]{2,1,0:T(8,128)(2,1)S(1)}, bf16[2,1024,256]{2,1,0:T(8,128)(2,1)S(1)}, u32[]{:S(2)}, u32[]{:S(2)}) collective-permute-start(bf16[2,1024,256]{2,1,0:T(8,128)(2,1)S(1)} %slant_stack.2), channel_id=1, source_target_pairs={{0,1},{1,2},{2,3},{3,4},{4,5},{5,6},{6,7},{8,9},{9,10},{10,11},{11... | collective-permute-start | bytes 3145736 | tf_op jit(solution)/shard_map/ppermute | solution.py:287
  53.8 1.9 %collective-permute-start.9 = (bf16[2,1024,256]{2,1,0:T(8,128)(2,1)S(1)}, bf16[2,1024,256]{2,1,0:T(8,128)(2,1)S(1)}, u32[]{:S(2)}, u32[]{:S(2)}) collective-permute-start(bf16[2,1024,256]{2,1,0:T(8,128)(2,1)S(1)} %slant_stack.2), channel_id=1, source_target_pairs={{1,0},{2,1},{3,2},{4,3},{5,4},{6,5},{7,6},{9,8},{10,9},{11,10},{12... | collective-permute-start | bytes 3145736 | tf_op jit(solution)/shard_map/ppermute | solution.py:288
  55.7 3.8 %smooth.3.refs_3_ = f32[4,16,64,256]{3,2,1,0:T(8,128)S(1)} custom-call(f32[16,4,27,256]{3,2,1,0:T(8,128)S(1)} %copy.18.weight_ref, bf16[2,16,64,256]{3,2,1,0:T(8,128)(2,1)S(1)} %bitcast.27), custom_call_target="tpu_custom_call" | custom-call | flops 419430400 | bytes 8388608 | tf_op jit(solution)/shard_map/smooth/pallas_call | solution.py:172
  59.6 0.0 collective-permute-done.5
  59.6 0.0 collective-permute-done.1
  59.6 1.3 %slice_select_fusion.below_ref = bf16[2,592,256]{2,1,0:T(8,128)(2,1)S(1)} fusion(bf16[2,592,256]{2,1,0:T(8,128)(2,1)} %collective-permute-done.5, bf16[2,656,256]{2,1,0:T(8,128)(2,1)} %collective-permute-done.1, pred[]{:T(512)S(6)} %eq.24), kind=kLoop, calls=%fused_computation.23 | loop fusion | flops 303104 | bytes 1818625 | tf_op jit(solution)/shard_map/jit(_where)/select_n | solution.py:240
  60.9 0.0 collective-permute-done.2
  60.9 1.2 %broadcast_select_fusion.above_ref = bf16[2,656,256]{2,1,0:T(8,128)(2,1)S(1)} fusion(bf16[2,656,256]{2,1,0:T(8,128)(2,1)} %collective-permute-done.1, bf16[2,656,256]{2,1,0:T(8,128)(2,1)} %collective-permute-done.2, pred[]{:T(512)S(6)} %eq.23), kind=kLoop, calls=%fused_computation.22 | loop fusion | flops 335872 | bytes 2015233 | tf_op jit(solution)/shard_map/jit(_where)/select_n | solution.py:239
  62.1 2.9 %slant_stack.3 = bf16[2,1024,256]{2,1,0:T(8,128)(2,1)S(1)} custom-call(bf16[256,2304]{1,0:T(8,128)(2,1)S(1)} %fusion.7.matrix_ref, bf16[2,656,256]{2,1,0:T(8,128)(2,1)S(1)} %broadcast_select_fusion.above_ref, bf16[4,16,64,256]{3,2,1,0:T(8,128)(2,1)S(1)} %bitcast.26, bf16[2,592,256]{2,1,0:T(8,128)(2,1)S(1)} %slice_select_fusion.below_ref), custom_call_target="tpu_custom_call" | custom-call | flops 2415919104 | bytes 4587520 | tf_op jit(solution)/shard_map/slant_stack/pallas_call | solution.py:118
  65.0 1.9 %collective-permute-start.7 = (bf16[2,1024,256]{2,1,0:T(8,128)(2,1)S(1)}, bf16[2,1024,256]{2,1,0:T(8,128)(2,1)S(1)}, u32[]{:S(2)}, u32[]{:S(2)}) collective-permute-start(bf16[2,1024,256]{2,1,0:T(8,128)(2,1)S(1)} %slant_stack.3), channel_id=1, source_target_pairs={{1,0},{2,1},{3,2},{4,3},{5,4},{6,5},{7,6},{9,8},{10,9},{11,10},{12... | collective-permute-start | bytes 3145736 | tf_op jit(solution)/shard_map/ppermute | solution.py:288
  66.9 3.6 %collective-permute-start.6 = (bf16[2,1024,256]{2,1,0:T(8,128)(2,1)S(1)}, bf16[2,1024,256]{2,1,0:T(8,128)(2,1)S(1)}, u32[]{:S(2)}, u32[]{:S(2)}) collective-permute-start(bf16[2,1024,256]{2,1,0:T(8,128)(2,1)S(1)} %slant_stack.3), channel_id=1, source_target_pairs={{0,1},{1,2},{2,3},{3,4},{4,5},{5,6},{6,7},{8,9},{9,10},{10,11},{11... | collective-permute-start | bytes 3145736 | tf_op jit(solution)/shard_map/ppermute | solution.py:287
  70.6 0.0 collective-permute-done.8
  70.6 0.0 collective-permute-done.9
  70.6 5.8 %smooth.4.refs_2_ = f32[4,16,64,256]{3,2,1,0:T(8,128)S(1)} custom-call(f32[16,4,27,256]{3,2,1,0:T(8,128)S(1)} %copy.18.weight_ref, bf16[2,16,64,256]{3,2,1,0:T(8,128)(2,1)S(1)} %bitcast.30, bf16[2,16,64,256]{3,2,1,0:T(8,128)(2,1)S(1)} %bitcast.32, bf16[2,16,64,256]{3,2,1,0:T(8,128)(2,1)S(1)} %bitcast.31, f32[4,16,64,256]{3,2,1,0:T(8,128)S(1)} %smooth.3.refs_3_), custom_call_target="tpu_custom_call" | custom-call | flops 943718400 | bytes 8388608 | tf_op jit(solution)/shard_map/smooth/pallas_call | solution.py:172
  76.5 4.7 %collective-permute-done.7 = bf16[2,1024,256]{2,1,0:T(8,128)(2,1)S(1)} collective-permute-done((bf16[2,1024,256]{2,1,0:T(8,128)(2,1)S(1)}, bf16[2,1024,256]{2,1,0:T(8,128)(2,1)S(1)}, u32[]{:S(2)}, u32[]{:S(2)}) %collective-permute-start.7) | collective-permute-done | bytes 1048608 | tf_op jit(solution)/shard_map/ppermute | solution.py:288
  81.2 1.1 %collective-permute-done.6 = bf16[2,1024,256]{2,1,0:T(8,128)(2,1)S(1)} collective-permute-done((bf16[2,1024,256]{2,1,0:T(8,128)(2,1)S(1)}, bf16[2,1024,256]{2,1,0:T(8,128)(2,1)S(1)}, u32[]{:S(2)}, u32[]{:S(2)}) %collective-permute-start.6) | collective-permute-done | bytes 1048608 | tf_op jit(solution)/shard_map/ppermute | solution.py:287
  82.3 4.1 %smooth.5 = bf16[4,16,64,256]{3,2,1,0:T(8,128)(2,1)S(1)} custom-call(f32[16,4,27,256]{3,2,1,0:T(8,128)S(1)} %copy.18.weight_ref, bf16[2,16,64,256]{3,2,1,0:T(8,128)(2,1)S(1)} %bitcast.29, bf16[2,16,64,256]{3,2,1,0:T(8,128)(2,1)S(1)} %bitcast.28, f32[4,16,64,256]{3,2,1,0:T(8,128)S(1)} %smooth.4.refs_2_), custom_call_target="tpu_custom_call" | custom-call | flops 524288000 | bytes 8388608 | tf_op jit(solution)/shard_map/smooth/pallas_call | solution.py:172
  86.4 2.9 %copy.19 = bf16[64,16,4,256]{3,2,1,0:T(4,128)(2,1)} copy(bf16[64,16,4,256]{3,0,1,2:T(8,128)(2,1)S(1)} %bitcast.23) | data formatting | bytes 4194304 | tf_op jit(solution)/shard_map/transpose | solution.py:292
  (2 shorter events, 0.0 us)
Async XLA Ops:
  4.1 12.7 %copy-start.1 = (s32[64]{0:T(128)S(1)}, s32[64]{0:T(128)}, u32[]{:S(2)}) copy-start(s32[64]{0:T(128)} %param.8) | copy-start | bytes 772
  4.1 12.8 %copy-start = (bf16[64,64,33]{1,0,2:T(8,128)(2,1)S(1)}, bf16[64,64,33]{1,0,2:T(8,128)(2,1)}, u32[]{:S(2)}) copy-start(bf16[64,64,33]{1,0,2:T(8,128)(2,1)} %param.7) | copy-start | bytes 811012
  6.7 18.5 %collective-permute-start = (bf16[2,656,256]{2,1,0:T(8,128)(2,1)}, bf16[2,656,256]{2,1,0:T(8,128)(2,1)}, u32[]{:S(2)}, u32[]{:S(2)}) collective-permute-start(bf16[2,656,256]{2,1,0:T(8,128)(2,1)} %get-tuple-element.24), channel_id=1, source_target_pairs={{8,24},{16,0},{9,25},{17,1},{10,26},{18,2},{11,27},{19,3},{12,28},... | collective-permute-start | bytes 2015240 | tf_op jit(solution)/shard_map/ppermute | solution.py:230
  8.0 36.4 %collective-permute-start.3 = (bf16[2,656,256]{2,1,0:T(8,128)(2,1)}, bf16[2,656,256]{2,1,0:T(8,128)(2,1)}, u32[]{:S(2)}, u32[]{:S(2)}) collective-permute-start(bf16[2,656,256]{2,1,0:T(8,128)(2,1)} %get-tuple-element.23), channel_id=1, source_target_pairs={{0,8},{8,16},{16,24},{1,9},{9,17},{17,25},{2,10},{10,18},{18,26},{... | collective-permute-start | bytes 2015240 | tf_op jit(solution)/shard_map/ppermute | solution.py:233
  15.5 28.9 %collective-permute-start.4 = (bf16[2,592,256]{2,1,0:T(8,128)(2,1)}, bf16[2,592,256]{2,1,0:T(8,128)(2,1)}, u32[]{:S(2)}, u32[]{:S(2)}) collective-permute-start(bf16[2,592,256]{2,1,0:T(8,128)(2,1)} %get-tuple-element.26), channel_id=1, source_target_pairs={{8,0},{16,8},{24,16},{9,1},{17,9},{25,17},{10,2},{18,10},{26,18},{... | collective-permute-start | bytes 1818632 | tf_op jit(solution)/shard_map/ppermute | solution.py:233
  25.2 34.4 %collective-permute-start.1 = (bf16[2,656,256]{2,1,0:T(8,128)(2,1)}, bf16[2,656,256]{2,1,0:T(8,128)(2,1)}, u32[]{:S(2)}, u32[]{:S(2)}) collective-permute-start(bf16[2,656,256]{2,1,0:T(8,128)(2,1)} %collective-permute-done), channel_id=1, source_target_pairs={{0,8},{24,16},{1,9},{25,17},{2,10},{26,18},{3,11},{27,19},{4,12},{... | collective-permute-start | bytes 2015240 | tf_op jit(solution)/shard_map/ppermute | solution.py:236
  28.7 30.9 %collective-permute-start.5 = (bf16[2,592,256]{2,1,0:T(8,128)(2,1)}, bf16[2,592,256]{2,1,0:T(8,128)(2,1)}, u32[]{:S(2)}, u32[]{:S(2)}) collective-permute-start(bf16[2,592,256]{2,1,0:T(8,128)(2,1)} %get-tuple-element.21), channel_id=1, source_target_pairs={{8,0},{24,16},{9,1},{25,17},{10,2},{26,18},{11,3},{27,19},{12,4},{... | collective-permute-start | bytes 1818632 | tf_op jit(solution)/shard_map/ppermute | solution.py:238
  31.6 29.3 %collective-permute-start.2 = (bf16[2,656,256]{2,1,0:T(8,128)(2,1)}, bf16[2,656,256]{2,1,0:T(8,128)(2,1)}, u32[]{:S(2)}, u32[]{:S(2)}) collective-permute-start(bf16[2,656,256]{2,1,0:T(8,128)(2,1)} %get-tuple-element.19), channel_id=1, source_target_pairs={{0,8},{16,24},{1,9},{17,25},{2,10},{18,26},{3,11},{19,27},{4,12},{... | collective-permute-start | bytes 2015240 | tf_op jit(solution)/shard_map/ppermute | solution.py:237
  48.3 22.3 %collective-permute-start.8 = (bf16[2,1024,256]{2,1,0:T(8,128)(2,1)S(1)}, bf16[2,1024,256]{2,1,0:T(8,128)(2,1)S(1)}, u32[]{:S(2)}, u32[]{:S(2)}) collective-permute-start(bf16[2,1024,256]{2,1,0:T(8,128)(2,1)S(1)} %slant_stack.2), channel_id=1, source_target_pairs={{0,1},{1,2},{2,3},{3,4},{4,5},{5,6},{6,7},{8,9},{9,10},{10,11},{11... | collective-permute-start | bytes 3145736 | tf_op jit(solution)/shard_map/ppermute | solution.py:287
  53.8 16.8 %collective-permute-start.9 = (bf16[2,1024,256]{2,1,0:T(8,128)(2,1)S(1)}, bf16[2,1024,256]{2,1,0:T(8,128)(2,1)S(1)}, u32[]{:S(2)}, u32[]{:S(2)}) collective-permute-start(bf16[2,1024,256]{2,1,0:T(8,128)(2,1)S(1)} %slant_stack.2), channel_id=1, source_target_pairs={{1,0},{2,1},{3,2},{4,3},{5,4},{6,5},{7,6},{9,8},{10,9},{11,10},{12... | collective-permute-start | bytes 3145736 | tf_op jit(solution)/shard_map/ppermute | solution.py:288
  65.0 16.2 %collective-permute-start.7 = (bf16[2,1024,256]{2,1,0:T(8,128)(2,1)S(1)}, bf16[2,1024,256]{2,1,0:T(8,128)(2,1)S(1)}, u32[]{:S(2)}, u32[]{:S(2)}) collective-permute-start(bf16[2,1024,256]{2,1,0:T(8,128)(2,1)S(1)} %slant_stack.3), channel_id=1, source_target_pairs={{1,0},{2,1},{3,2},{4,3},{5,4},{6,5},{7,6},{9,8},{10,9},{11,10},{12... | collective-permute-start | bytes 3145736 | tf_op jit(solution)/shard_map/ppermute | solution.py:288
  66.9 15.4 %collective-permute-start.6 = (bf16[2,1024,256]{2,1,0:T(8,128)(2,1)S(1)}, bf16[2,1024,256]{2,1,0:T(8,128)(2,1)S(1)}, u32[]{:S(2)}, u32[]{:S(2)}) collective-permute-start(bf16[2,1024,256]{2,1,0:T(8,128)(2,1)S(1)} %slant_stack.3), channel_id=1, source_target_pairs={{0,1},{1,2},{2,3},{3,4},{4,5},{5,6},{6,7},{8,9},{9,10},{10,11},{11... | collective-permute-start | bytes 3145736 | tf_op jit(solution)/shard_map/ppermute | solution.py:287

commit v5 on v4

--- a/solution.py
+++ b/solution.py
@@ -13,7 +13,7 @@
 RY = 1
 COLS = 2
 GROUP = 4
-ALIGN = 8
+ALIGN = 2
 
 
 def first_offsets(offset_count):
@@ -64,13 +64,15 @@
         leading_ref[0, place : place + offset_count - start, :] = image_ref[0, row, start:, :]
 
 
-def pack(by_column, upper, lower):
-    columns, depth_cells, offset_count, cross = by_column.shape
+def pack(by_column, upper, lower, first, columns):
+    _, depth_cells, offset_count, cross = by_column.shape
     sizes = [upper[1], lower[1]]
     return pl.pallas_call(
         functools.partial(pack_kernel, upper[0], lower[0]),
         grid=(columns,),
-        in_specs=[pl.BlockSpec((1, depth_cells, offset_count, cross), lambda c: (c, 0, 0, 0))],
+        in_specs=[
+            pl.BlockSpec((1, depth_cells, offset_count, cross), lambda c: (c + first, 0, 0, 0))
+        ],
         out_specs=[pl.BlockSpec((1, n, cross), lambda c: (c, 0, 0)) for n in sizes],
         out_shape=[jax.ShapeDtypeStruct((columns, n, cross), jnp.bfloat16) for n in sizes],
         compiler_params=pltpu.CompilerParams(vmem_limit_bytes=32 * 1024 * 1024),
@@ -211,9 +213,8 @@
     return up, [(j, i) for i, j in up]
 
 
-def halos_of(last, leading, cols):
-    lateral = last.shape[0]
-    chunks = [(last[c : c + cols], leading[c : c + cols]) for c in range(0, lateral, cols)]
+def halos_of(chunks):
+    last, leading = chunks[0]
     if lax.axis_size("depth") != 4 or last.shape[1] < leading.shape[1]:
         up, down = neighbours("depth")
         return [
@@ -253,8 +254,9 @@
     lower = packed_rows(below, offset_count)
     group = GROUP if depth_cells % GROUP == 0 else depth_cells
     by_column = jnp.transpose(offset_image, (2, 1, 0, 3))
-    last, leading = pack(by_column, upper, lower)
-    halos = halos_of(last, leading, cols)
+    halos = halos_of(
+        [pack(by_column, upper, lower, first, cols) for first in range(0, lateral, cols)]
+    )
     matrix = stack_matrix(slant_matrix_of(slant_taper, band_offsets, offset_count), group)
     weights = dip_weights(dip_class, coefficients)
     matrix, weights = lax.optimization_barrier((matrix, weights))

time: 90 us -> 86.1 us (0.957)
  waiting for transfers between devices: 11.8 us -> 7.76 us
  other arithmetic: 6.6 us -> 4.95 us
  Pallas kernels: 20.8 us -> 21.9 us
    ppermute x1, waiting for transfers between devices: 5.94 us -> 1.89 us  [halos_of(): relays[index] = lax.ppermute(crossing, 'depth', [(1, 3), (2, 0)])]
    slice x1 -> x0, other arithmetic: 2.57 us -> none  [halos_of(): last[c:c + cols]]
    reshape x1, local copies, waits for them, and re-layouts: 0.33 us -> 1.45 us  [stack_matrix(): jnp.swapaxes(slant_matrix, 1, 2).reshape(angles, reach * offset_count)]
    slice x1 -> x0, local copies, waits for them, and re-layouts: 1.12 us -> none  [halos_of(): leading[c:c + cols]]
    pallas_call x1 -> x2, Pallas kernels: 0.23 us -> 1.27 us  [pack(): pl.pallas_call(functools.partial(pack_kernel, upper[0], lower[0]), grid=(...]
    select_n x0 -> x1, other arithmetic: none -> 0.99 us  [halos_of(): jnp.where(place == 1, upper, jnp.pad(lower, ((0, 0), (0, pad), (0, 0))))]
    unnamed x6 -> x10, local copies, waits for them, and re-layouts: 3.55 us -> 3.56 us
  transfers between devices with their start and end apart: 10 -> 10, of which waited for: 3 -> 3; matrix products, arithmetic and copies ran while one was open for 15% -> 18% of each run, Pallas kernels for 18% -> 21%
where the time goes in v5:
time: 86.1 us; the launch traced here: 85.5 us
  starting transfers between devices  33.3 us (39%)
  Pallas kernels  21.9 us (25%)
  local copies, waits for them, and re-layouts  14.2 us (16%)
  waiting for transfers between devices  7.76 us (9%)
  other arithmetic  4.95 us (6%)
  matrix products  3.03 us (4%)
    pallas_call x3, Pallas kernels, smooth(): pl.pallas_call(functools.partial(smooth_kernel, sources), grid=(depth_cel...  13.8 us
    ppermute x2, starting transfers between devices, local(): before.append(lax.ppermute(part, 'gx', right))  9.1 us
    ppermute x1, starting transfers between devices, halos_of(): lax.ppermute(upper, 'depth', up)  7.41 us
    pallas_call x2, Pallas kernels, slant_stack(): pl.pallas_call(functools.partial(stack_kernel, upper[0], lower[0], group)...  6.86 us
    ppermute x1, starting transfers between devices, halos_of(): from_above = lax.ppermute(upper, 'depth', [(0, 1), (2, 3)])  5.64 us
    ppermute x2, waiting for transfers between devices, local(): after.append(lax.ppermute(part, 'gx', left))  4.76 us
    ppermute x2, starting transfers between devices, local(): after.append(lax.ppermute(part, 'gx', left))  3.84 us
    unnamed x10, local copies, waits for them, and re-layouts  3.56 us
  transfers between devices with their start and end apart: 10, of which 3 were waited for; matrix products, arithmetic and copies ran while one was open for 18% of the time, Pallas kernels for 21%

profile of v5, /device:TPU:1, one launch (start us, length us, event | category | flops | bytes accessed | tf_op | source)
XLA Modules:
  0.0 85.5 jit_solution(3849172137174325825)
XLA Ops:
  0.0 2.8 %copy.26 = bf16[64,16,4,256]{3,0,1,2:T(8,128)(2,1)S(1)} copy(bf16[64,16,4,256]{3,2,1,0:T(4,128)(2,1)} %param.5) | data formatting | bytes 4194304 | tf_op args[0]
  2.8 0.1 pack.2
  2.9 0.0 copy-start
  2.9 0.0 copy-start.1
  2.9 0.0 copy-start.3
  3.0 0.0 copy-start.2
  3.0 1.0 %pad_select_fusion = bf16[2,608,256]{2,1,0:T(8,128)(2,1)} fusion(bf16[2,608,256]{2,1,0:T(8,128)(2,1)S(1)} %get-tuple-element.21, bf16[2,544,256]{2,1,0:T(8,128)(2,1)S(1)} %get-tuple-element.25, pred[]{:T(512)S(6)} %eq.24), kind=kLoop, calls=%fused_computation.21 | loop fusion | flops 311296 | bytes 1802241 | tf_op jit(solution)/shard_map/jit(_where)/select_n | solution.py:230
  4.0 1.3 %collective-permute-start = (bf16[2,608,256]{2,1,0:T(8,128)(2,1)}, bf16[2,608,256]{2,1,0:T(8,128)(2,1)}, u32[]{:S(2)}, u32[]{:S(2)}) collective-permute-start(bf16[2,608,256]{2,1,0:T(8,128)(2,1)} %pad_select_fusion), channel_id=1, source_target_pairs={{8,24},{16,0},{9,25},{17,1},{10,26},{18,2},{11,27},{19,3},{12,28},... | collective-permute-start | bytes 1867784 | tf_op jit(solution)/shard_map/ppermute | solution.py:231
  5.3 1.1 %pack.3 = (bf16[2,608,256]{2,1,0:T(8,128)(2,1)}, bf16[2,544,256]{2,1,0:T(8,128)(2,1)}) custom-call(bf16[4,16,64,256]{3,2,1,0:T(8,128)(2,1)S(1)} %bitcast.24), custom_call_target="tpu_custom_call" | custom-call | bytes 2359296 | tf_op jit(solution)/shard_map/pack/pallas_call | solution.py:70
  6.4 7.4 %collective-permute-start.3 = (bf16[2,608,256]{2,1,0:T(8,128)(2,1)}, bf16[2,608,256]{2,1,0:T(8,128)(2,1)}, u32[]{:S(2)}, u32[]{:S(2)}) collective-permute-start(bf16[2,608,256]{2,1,0:T(8,128)(2,1)} %get-tuple-element.22), channel_id=1, source_target_pairs={{0,8},{8,16},{16,24},{1,9},{9,17},{17,25},{2,10},{10,18},{18,26},{... | collective-permute-start | bytes 1867784 | tf_op jit(solution)/shard_map/ppermute | solution.py:234
  13.8 1.3 %collective-permute-start.4 = (bf16[2,544,256]{2,1,0:T(8,128)(2,1)}, bf16[2,544,256]{2,1,0:T(8,128)(2,1)}, u32[]{:S(2)}, u32[]{:S(2)}) collective-permute-start(bf16[2,544,256]{2,1,0:T(8,128)(2,1)} %get-tuple-element.23), channel_id=1, source_target_pairs={{8,0},{16,8},{24,16},{9,1},{17,9},{25,17},{10,2},{18,10},{26,18},{... | collective-permute-start | bytes 1671176 | tf_op jit(solution)/shard_map/ppermute | solution.py:234
  15.1 0.0 copy-done.3
  15.1 0.1 add_select_fusion
  15.2 0.0 copy-done.2
  15.2 0.3 fusion.11
  15.6 0.0 copy-done
  15.6 0.0 copy-done.1
  15.6 1.2 %copy.11 = bf16[64,33,64]{2,1,0:T(8,128)(2,1)} copy(bf16[64,33,64]{2,0,1:T(8,128)(2,1)S(1)} %fusion.11) | data formatting | bytes 540672 | tf_op jit(solution)/shard_map/transpose | solution.py:40
  16.8 1.5 %reshape.68 = bf16[64,2112]{1,0:T(8,128)(2,1)S(1)} reshape(bf16[64,33,64]{2,1,0:T(8,128)(2,1)} %copy.11) | data formatting | bytes 540672 | tf_op jit(solution)/shard_map/reshape | solution.py:40
  18.2 0.2 fusion.7.matrix_ref
  18.5 1.0 %fusion.12 = (s32[1,16,4,256]{3,2,1,0:T(4,128)S(1)}, s32[1,16,4,256]{3,2,1,0:T(4,128)S(1)}) fusion(s32[16,4,256]{2,1,0:T(4,128)} %param.6), kind=kLoop, calls=%fused_computation.28 | loop fusion | bytes 196608 | tf_op jit(solution)/shard_map/stack | solution.py:196
  19.5 1.9 %collective-permute-done = bf16[2,608,256]{2,1,0:T(8,128)(2,1)} collective-permute-done((bf16[2,608,256]{2,1,0:T(8,128)(2,1)}, bf16[2,608,256]{2,1,0:T(8,128)(2,1)}, u32[]{:S(2)}, u32[]{:S(2)}) %collective-permute-start) | collective-permute-done | bytes 622624 | tf_op jit(solution)/shard_map/ppermute | solution.py:231
  21.4 3.5 %collective-permute-start.1 = (bf16[2,608,256]{2,1,0:T(8,128)(2,1)}, bf16[2,608,256]{2,1,0:T(8,128)(2,1)}, u32[]{:S(2)}, u32[]{:S(2)}) collective-permute-start(bf16[2,608,256]{2,1,0:T(8,128)(2,1)} %collective-permute-done), channel_id=1, source_target_pairs={{0,8},{24,16},{1,9},{25,17},{2,10},{26,18},{3,11},{27,19},{4,12},{... | collective-permute-start | bytes 1867784 | tf_op jit(solution)/shard_map/ppermute | solution.py:237
  24.9 0.9 pad_add_fusion
  25.8 0.8 copy.12
  26.5 1.3 %collective-permute-start.5 = (bf16[2,544,256]{2,1,0:T(8,128)(2,1)}, bf16[2,544,256]{2,1,0:T(8,128)(2,1)}, u32[]{:S(2)}, u32[]{:S(2)}) collective-permute-start(bf16[2,544,256]{2,1,0:T(8,128)(2,1)} %copy-done.1), channel_id=1, source_target_pairs={{8,0},{24,16},{9,1},{25,17},{10,2},{26,18},{11,3},{27,19},{12,4},{... | collective-permute-start | bytes 1671176 | tf_op jit(solution)/shard_map/ppermute | solution.py:239
  27.8 5.6 %collective-permute-start.2 = (bf16[2,608,256]{2,1,0:T(8,128)(2,1)}, bf16[2,608,256]{2,1,0:T(8,128)(2,1)}, u32[]{:S(2)}, u32[]{:S(2)}) collective-permute-start(bf16[2,608,256]{2,1,0:T(8,128)(2,1)} %copy-done), channel_id=1, source_target_pairs={{0,8},{16,24},{1,9},{17,25},{2,10},{18,26},{3,11},{19,27},{4,12},{... | collective-permute-start | bytes 1867784 | tf_op jit(solution)/shard_map/ppermute | solution.py:238
  33.5 3.0 %convolution_bitcast_fusion = f32[16,4,9,3,256]{4,2,1,0,3:T(8,128)} fusion(s32[3,16,4,256]{3,2,1,0:T(4,128)S(1)} %pad_add_fusion, f32[8,9,3,1,1]{0,2,1,4,3:T(4,128)S(1)} %bitcast.36), kind=kOutput, calls=%fused_computation.13 | convolution fusion | flops 42860544 | bytes 1966944 | tf_op jit(solution)/shard_map/qij,jzxqy->zxijy/dot_general | solution.py:201
  36.5 2.9 %copy.14 = f32[16,4,9,3,256]{4,0,3,2,1:T(8,128)S(1)} copy(f32[16,4,9,3,256]{4,2,1,0,3:T(8,128)} %convolution_bitcast_fusion) | data formatting | bytes 3538944 | tf_op jit(solution)/shard_map/qij,jzxqy->zxijy/transpose | solution.py:201
  39.4 1.0 %copy.18.weight_ref = f32[16,4,27,256]{3,2,1,0:T(8,128)S(1)} copy(f32[16,4,27,256]{3,0,2,1:T(8,128)S(1)} %bitcast.34) | data formatting | bytes 3538944 | tf_op jit(solution)/shard_map/optimization_barrier | solution.py:262
  40.5 0.0 collective-permute-done.4.below_ref
  40.5 0.0 collective-permute-done.3.above_ref
  40.5 4.0 %slant_stack.2 = bf16[2,1024,256]{2,1,0:T(8,128)(2,1)S(1)} custom-call(bf16[256,2304]{1,0:T(8,128)(2,1)S(1)} %fusion.7.matrix_ref, bf16[2,608,256]{2,1,0:T(8,128)(2,1)} %collective-permute-done.3.above_ref, bf16[4,16,64,256]{3,2,1,0:T(8,128)(2,1)S(1)} %bitcast.25, bf16[2,544,256]{2,1,0:T(8,128)(2,1)} %collective-permute-done.4.below_ref), custom_call_target="tpu_custom_call" | custom-call | flops 2415919104 | bytes 4587520 | tf_op jit(solution)/shard_map/slant_stack/pallas_call | solution.py:120
  44.5 5.5 %collective-permute-start.8 = (bf16[2,1024,256]{2,1,0:T(8,128)(2,1)S(1)}, bf16[2,1024,256]{2,1,0:T(8,128)(2,1)S(1)}, u32[]{:S(2)}, u32[]{:S(2)}) collective-permute-start(bf16[2,1024,256]{2,1,0:T(8,128)(2,1)S(1)} %slant_stack.2), channel_id=1, source_target_pairs={{0,1},{1,2},{2,3},{3,4},{4,5},{5,6},{6,7},{8,9},{9,10},{10,11},{11... | collective-permute-start | bytes 3145736 | tf_op jit(solution)/shard_map/ppermute | solution.py:289
  49.9 1.9 %collective-permute-start.9 = (bf16[2,1024,256]{2,1,0:T(8,128)(2,1)S(1)}, bf16[2,1024,256]{2,1,0:T(8,128)(2,1)S(1)}, u32[]{:S(2)}, u32[]{:S(2)}) collective-permute-start(bf16[2,1024,256]{2,1,0:T(8,128)(2,1)S(1)} %slant_stack.2), channel_id=1, source_target_pairs={{1,0},{2,1},{3,2},{4,3},{5,4},{6,5},{7,6},{9,8},{10,9},{11,10},{12... | collective-permute-start | bytes 3145736 | tf_op jit(solution)/shard_map/ppermute | solution.py:290
  51.9 3.8 %smooth.3.refs_3_ = f32[4,16,64,256]{3,2,1,0:T(8,128)S(1)} custom-call(f32[16,4,27,256]{3,2,1,0:T(8,128)S(1)} %copy.18.weight_ref, bf16[2,16,64,256]{3,2,1,0:T(8,128)(2,1)S(1)} %bitcast.28), custom_call_target="tpu_custom_call" | custom-call | flops 419430400 | bytes 8388608 | tf_op jit(solution)/shard_map/smooth/pallas_call | solution.py:174
  55.7 0.0 collective-permute-done.5
  55.7 0.0 collective-permute-done.1
  55.7 1.3 %slice_select_fusion.below_ref = bf16[2,544,256]{2,1,0:T(8,128)(2,1)S(1)} fusion(bf16[2,544,256]{2,1,0:T(8,128)(2,1)} %collective-permute-done.5, bf16[2,608,256]{2,1,0:T(8,128)(2,1)} %collective-permute-done.1, pred[]{:T(512)S(6)} %eq.24), kind=kLoop, calls=%fused_computation.23 | loop fusion | flops 278528 | bytes 1671169 | tf_op jit(solution)/shard_map/jit(_where)/select_n | solution.py:241
  57.0 0.0 collective-permute-done.2
  57.0 1.2 %broadcast_select_fusion.above_ref = bf16[2,608,256]{2,1,0:T(8,128)(2,1)S(1)} fusion(bf16[2,608,256]{2,1,0:T(8,128)(2,1)} %collective-permute-done.1, bf16[2,608,256]{2,1,0:T(8,128)(2,1)} %collective-permute-done.2, pred[]{:T(512)S(6)} %eq.23), kind=kLoop, calls=%fused_computation.22 | loop fusion | flops 311296 | bytes 1867777 | tf_op jit(solution)/shard_map/jit(_where)/select_n | solution.py:240
  58.2 2.9 %slant_stack.3 = bf16[2,1024,256]{2,1,0:T(8,128)(2,1)S(1)} custom-call(bf16[256,2304]{1,0:T(8,128)(2,1)S(1)} %fusion.7.matrix_ref, bf16[2,608,256]{2,1,0:T(8,128)(2,1)S(1)} %broadcast_select_fusion.above_ref, bf16[4,16,64,256]{3,2,1,0:T(8,128)(2,1)S(1)} %bitcast.26, bf16[2,544,256]{2,1,0:T(8,128)(2,1)S(1)} %slice_select_fusion.below_ref), custom_call_target="tpu_custom_call" | custom-call | flops 2415919104 | bytes 4587520 | tf_op jit(solution)/shard_map/slant_stack/pallas_call | solution.py:120
  61.1 1.9 %collective-permute-start.7 = (bf16[2,1024,256]{2,1,0:T(8,128)(2,1)S(1)}, bf16[2,1024,256]{2,1,0:T(8,128)(2,1)S(1)}, u32[]{:S(2)}, u32[]{:S(2)}) collective-permute-start(bf16[2,1024,256]{2,1,0:T(8,128)(2,1)S(1)} %slant_stack.3), channel_id=1, source_target_pairs={{1,0},{2,1},{3,2},{4,3},{5,4},{6,5},{7,6},{9,8},{10,9},{11,10},{12... | collective-permute-start | bytes 3145736 | tf_op jit(solution)/shard_map/ppermute | solution.py:290
  63.0 3.6 %collective-permute-start.6 = (bf16[2,1024,256]{2,1,0:T(8,128)(2,1)S(1)}, bf16[2,1024,256]{2,1,0:T(8,128)(2,1)S(1)}, u32[]{:S(2)}, u32[]{:S(2)}) collective-permute-start(bf16[2,1024,256]{2,1,0:T(8,128)(2,1)S(1)} %slant_stack.3), channel_id=1, source_target_pairs={{0,1},{1,2},{2,3},{3,4},{4,5},{5,6},{6,7},{8,9},{9,10},{10,11},{11... | collective-permute-start | bytes 3145736 | tf_op jit(solution)/shard_map/ppermute | solution.py:289
  66.7 0.0 collective-permute-done.8
  66.7 0.0 collective-permute-done.9
  66.7 5.8 %smooth.4.refs_2_ = f32[4,16,64,256]{3,2,1,0:T(8,128)S(1)} custom-call(f32[16,4,27,256]{3,2,1,0:T(8,128)S(1)} %copy.18.weight_ref, bf16[2,16,64,256]{3,2,1,0:T(8,128)(2,1)S(1)} %bitcast.31, bf16[2,16,64,256]{3,2,1,0:T(8,128)(2,1)S(1)} %bitcast.33, bf16[2,16,64,256]{3,2,1,0:T(8,128)(2,1)S(1)} %bitcast.32, f32[4,16,64,256]{3,2,1,0:T(8,128)S(1)} %smooth.3.refs_3_), custom_call_target="tpu_custom_call" | custom-call | flops 943718400 | bytes 8388608 | tf_op jit(solution)/shard_map/smooth/pallas_call | solution.py:174
  72.5 4.8 %collective-permute-done.7 = bf16[2,1024,256]{2,1,0:T(8,128)(2,1)S(1)} collective-permute-done((bf16[2,1024,256]{2,1,0:T(8,128)(2,1)S(1)}, bf16[2,1024,256]{2,1,0:T(8,128)(2,1)S(1)}, u32[]{:S(2)}, u32[]{:S(2)}) %collective-permute-start.7) | collective-permute-done | bytes 1048608 | tf_op jit(solution)/shard_map/ppermute | solution.py:290
  77.3 1.1 %collective-permute-done.6 = bf16[2,1024,256]{2,1,0:T(8,128)(2,1)S(1)} collective-permute-done((bf16[2,1024,256]{2,1,0:T(8,128)(2,1)S(1)}, bf16[2,1024,256]{2,1,0:T(8,128)(2,1)S(1)}, u32[]{:S(2)}, u32[]{:S(2)}) %collective-permute-start.6) | collective-permute-done | bytes 1048608 | tf_op jit(solution)/shard_map/ppermute | solution.py:289
  78.4 4.1 %smooth.5 = bf16[4,16,64,256]{3,2,1,0:T(8,128)(2,1)S(1)} custom-call(f32[16,4,27,256]{3,2,1,0:T(8,128)S(1)} %copy.18.weight_ref, bf16[2,16,64,256]{3,2,1,0:T(8,128)(2,1)S(1)} %bitcast.30, bf16[2,16,64,256]{3,2,1,0:T(8,128)(2,1)S(1)} %bitcast.29, f32[4,16,64,256]{3,2,1,0:T(8,128)S(1)} %smooth.4.refs_2_), custom_call_target="tpu_custom_call" | custom-call | flops 524288000 | bytes 8388608 | tf_op jit(solution)/shard_map/smooth/pallas_call | solution.py:174
  82.5 2.9 %copy.19 = bf16[64,16,4,256]{3,2,1,0:T(4,128)(2,1)} copy(bf16[64,16,4,256]{3,0,1,2:T(8,128)(2,1)S(1)} %bitcast.27) | data formatting | bytes 4194304 | tf_op jit(solution)/shard_map/transpose | solution.py:294
  (2 shorter events, 0.0 us)
Async XLA Ops:
  2.9 12.6 %copy-start = (bf16[2,608,256]{2,1,0:T(8,128)(2,1)}, bf16[2,608,256]{2,1,0:T(8,128)(2,1)S(1)}, u32[]{:S(2)}) copy-start(bf16[2,608,256]{2,1,0:T(8,128)(2,1)S(1)} %get-tuple-element.21) | copy-start | bytes 1867780
  2.9 12.6 %copy-start.1 = (bf16[2,544,256]{2,1,0:T(8,128)(2,1)}, bf16[2,544,256]{2,1,0:T(8,128)(2,1)S(1)}, u32[]{:S(2)}) copy-start(bf16[2,544,256]{2,1,0:T(8,128)(2,1)S(1)} %get-tuple-element.25) | copy-start | bytes 1671172
  2.9 12.1 %copy-start.3 = (s32[64]{0:T(128)S(1)}, s32[64]{0:T(128)}, u32[]{:S(2)}) copy-start(s32[64]{0:T(128)} %param.8) | copy-start | bytes 772
  3.0 12.2 %copy-start.2 = (bf16[64,64,33]{1,0,2:T(8,128)(2,1)S(1)}, bf16[64,64,33]{1,0,2:T(8,128)(2,1)}, u32[]{:S(2)}) copy-start(bf16[64,64,33]{1,0,2:T(8,128)(2,1)} %param.7) | copy-start | bytes 811012
  4.0 17.4 %collective-permute-start = (bf16[2,608,256]{2,1,0:T(8,128)(2,1)}, bf16[2,608,256]{2,1,0:T(8,128)(2,1)}, u32[]{:S(2)}, u32[]{:S(2)}) collective-permute-start(bf16[2,608,256]{2,1,0:T(8,128)(2,1)} %pad_select_fusion), channel_id=1, source_target_pairs={{8,24},{16,0},{9,25},{17,1},{10,26},{18,2},{11,27},{19,3},{12,28},... | collective-permute-start | bytes 1867784 | tf_op jit(solution)/shard_map/ppermute | solution.py:231
  6.4 34.1 %collective-permute-start.3 = (bf16[2,608,256]{2,1,0:T(8,128)(2,1)}, bf16[2,608,256]{2,1,0:T(8,128)(2,1)}, u32[]{:S(2)}, u32[]{:S(2)}) collective-permute-start(bf16[2,608,256]{2,1,0:T(8,128)(2,1)} %get-tuple-element.22), channel_id=1, source_target_pairs={{0,8},{8,16},{16,24},{1,9},{9,17},{17,25},{2,10},{10,18},{18,26},{... | collective-permute-start | bytes 1867784 | tf_op jit(solution)/shard_map/ppermute | solution.py:234
  13.8 26.7 %collective-permute-start.4 = (bf16[2,544,256]{2,1,0:T(8,128)(2,1)}, bf16[2,544,256]{2,1,0:T(8,128)(2,1)}, u32[]{:S(2)}, u32[]{:S(2)}) collective-permute-start(bf16[2,544,256]{2,1,0:T(8,128)(2,1)} %get-tuple-element.23), channel_id=1, source_target_pairs={{8,0},{16,8},{24,16},{9,1},{17,9},{25,17},{10,2},{18,10},{26,18},{... | collective-permute-start | bytes 1671176 | tf_op jit(solution)/shard_map/ppermute | solution.py:234
  21.4 34.3 %collective-permute-start.1 = (bf16[2,608,256]{2,1,0:T(8,128)(2,1)}, bf16[2,608,256]{2,1,0:T(8,128)(2,1)}, u32[]{:S(2)}, u32[]{:S(2)}) collective-permute-start(bf16[2,608,256]{2,1,0:T(8,128)(2,1)} %collective-permute-done), channel_id=1, source_target_pairs={{0,8},{24,16},{1,9},{25,17},{2,10},{26,18},{3,11},{27,19},{4,12},{... | collective-permute-start | bytes 1867784 | tf_op jit(solution)/shard_map/ppermute | solution.py:237
  26.5 29.2 %collective-permute-start.5 = (bf16[2,544,256]{2,1,0:T(8,128)(2,1)}, bf16[2,544,256]{2,1,0:T(8,128)(2,1)}, u32[]{:S(2)}, u32[]{:S(2)}) collective-permute-start(bf16[2,544,256]{2,1,0:T(8,128)(2,1)} %copy-done.1), channel_id=1, source_target_pairs={{8,0},{24,16},{9,1},{25,17},{10,2},{26,18},{11,3},{27,19},{12,4},{... | collective-permute-start | bytes 1671176 | tf_op jit(solution)/shard_map/ppermute | solution.py:239
  27.8 29.2 %collective-permute-start.2 = (bf16[2,608,256]{2,1,0:T(8,128)(2,1)}, bf16[2,608,256]{2,1,0:T(8,128)(2,1)}, u32[]{:S(2)}, u32[]{:S(2)}) collective-permute-start(bf16[2,608,256]{2,1,0:T(8,128)(2,1)} %copy-done), channel_id=1, source_target_pairs={{0,8},{16,24},{1,9},{17,25},{2,10},{18,26},{3,11},{19,27},{4,12},{... | collective-permute-start | bytes 1867784 | tf_op jit(solution)/shard_map/ppermute | solution.py:238
  44.5 22.2 %collective-permute-start.8 = (bf16[2,1024,256]{2,1,0:T(8,128)(2,1)S(1)}, bf16[2,1024,256]{2,1,0:T(8,128)(2,1)S(1)}, u32[]{:S(2)}, u32[]{:S(2)}) collective-permute-start(bf16[2,1024,256]{2,1,0:T(8,128)(2,1)S(1)} %slant_stack.2), channel_id=1, source_target_pairs={{0,1},{1,2},{2,3},{3,4},{4,5},{5,6},{6,7},{8,9},{9,10},{10,11},{11... | collective-permute-start | bytes 3145736 | tf_op jit(solution)/shard_map/ppermute | solution.py:289
  49.9 16.7 %collective-permute-start.9 = (bf16[2,1024,256]{2,1,0:T(8,128)(2,1)S(1)}, bf16[2,1024,256]{2,1,0:T(8,128)(2,1)S(1)}, u32[]{:S(2)}, u32[]{:S(2)}) collective-permute-start(bf16[2,1024,256]{2,1,0:T(8,128)(2,1)S(1)} %slant_stack.2), channel_id=1, source_target_pairs={{1,0},{2,1},{3,2},{4,3},{5,4},{6,5},{7,6},{9,8},{10,9},{11,10},{12... | collective-permute-start | bytes 3145736 | tf_op jit(solution)/shard_map/ppermute | solution.py:290
  61.1 16.2 %collective-permute-start.7 = (bf16[2,1024,256]{2,1,0:T(8,128)(2,1)S(1)}, bf16[2,1024,256]{2,1,0:T(8,128)(2,1)S(1)}, u32[]{:S(2)}, u32[]{:S(2)}) collective-permute-start(bf16[2,1024,256]{2,1,0:T(8,128)(2,1)S(1)} %slant_stack.3), channel_id=1, source_target_pairs={{1,0},{2,1},{3,2},{4,3},{5,4},{6,5},{7,6},{9,8},{10,9},{11,10},{12... | collective-permute-start | bytes 3145736 | tf_op jit(solution)/shard_map/ppermute | solution.py:290
  63.0 15.4 %collective-permute-start.6 = (bf16[2,1024,256]{2,1,0:T(8,128)(2,1)S(1)}, bf16[2,1024,256]{2,1,0:T(8,128)(2,1)S(1)}, u32[]{:S(2)}, u32[]{:S(2)}) collective-permute-start(bf16[2,1024,256]{2,1,0:T(8,128)(2,1)S(1)} %slant_stack.3), channel_id=1, source_target_pairs={{0,1},{1,2},{2,3},{3,4},{4,5},{5,6},{6,7},{8,9},{9,10},{10,11},{11... | collective-permute-start | bytes 3145736 | tf_op jit(solution)/shard_map/ppermute | solution.py:289

commit v6 on v5

--- a/solution.py
+++ b/solution.py
@@ -259,7 +259,6 @@
     )
     matrix = stack_matrix(slant_matrix_of(slant_taper, band_offsets, offset_count), group)
     weights = dip_weights(dip_class, coefficients)
-    matrix, weights = lax.optimization_barrier((matrix, weights))
     mine, before, after = [], [], []
     count = len(halos)
     chunks = [(p, c) for p in range(3 * count) for c in range(cols)]

time: 86.1 us -> 86.1 us (level)
    optimization_barrier x1 -> x0, local copies, waits for them, and re-layouts: 1.04 us -> none  [local(): matrix, weights = lax.optimization_barrier((matrix, weights))]
    reshape x0 -> x1, local copies, waits for them, and re-layouts: none -> 1.04 us  [dip_weights(): return weights.reshape(weights.shape[:2] + (taps, cross))]
where the time goes in v6:
time: 86.1 us; the launch traced here: 85.5 us
  starting transfers between devices  33.3 us (39%)
  Pallas kernels  21.9 us (25%)
  local copies, waits for them, and re-layouts  14.2 us (16%)
  waiting for transfers between devices  7.76 us (9%)
  other arithmetic  4.95 us (6%)
  matrix products  3.03 us (4%)
    pallas_call x3, Pallas kernels, smooth(): pl.pallas_call(functools.partial(smooth_kernel, sources), grid=(depth_cel...  13.8 us
    ppermute x2, starting transfers between devices, local(): before.append(lax.ppermute(part, 'gx', right))  9.1 us
    ppermute x1, starting transfers between devices, halos_of(): lax.ppermute(upper, 'depth', up)  7.41 us
    pallas_call x2, Pallas kernels, slant_stack(): pl.pallas_call(functools.partial(stack_kernel, upper[0], lower[0], group)...  6.86 us
    ppermute x1, starting transfers between devices, halos_of(): from_above = lax.ppermute(upper, 'depth', [(0, 1), (2, 3)])  5.64 us
    ppermute x2, waiting for transfers between devices, local(): after.append(lax.ppermute(part, 'gx', left))  4.76 us
    ppermute x2, starting transfers between devices, local(): after.append(lax.ppermute(part, 'gx', left))  3.84 us
    unnamed x10, local copies, waits for them, and re-layouts  3.56 us
  transfers between devices with their start and end apart: 10, of which 3 were waited for; matrix products, arithmetic and copies ran while one was open for 18% of the time, Pallas kernels for 21%

profile of v6, /device:TPU:1, one launch (start us, length us, event | category | flops | bytes accessed | tf_op | source)
XLA Modules:
  0.0 85.5 jit_solution(3849172137174325825)
XLA Ops:
  0.0 2.8 %copy.26 = bf16[64,16,4,256]{3,0,1,2:T(8,128)(2,1)S(1)} copy(bf16[64,16,4,256]{3,2,1,0:T(4,128)(2,1)} %param.5) | data formatting | bytes 4194304 | tf_op args[0]
  2.8 0.1 pack.2
  2.9 0.0 copy-start
  2.9 0.0 copy-start.1
  2.9 0.0 copy-start.3
  3.0 0.0 copy-start.2
  3.0 1.0 %pad_select_fusion = bf16[2,608,256]{2,1,0:T(8,128)(2,1)} fusion(bf16[2,608,256]{2,1,0:T(8,128)(2,1)S(1)} %get-tuple-element.17, bf16[2,544,256]{2,1,0:T(8,128)(2,1)S(1)} %get-tuple-element.21, pred[]{:T(512)S(6)} %eq.24), kind=kLoop, calls=%fused_computation.21 | loop fusion | flops 311296 | bytes 1802241 | tf_op jit(solution)/shard_map/jit(_where)/select_n | solution.py:230
  4.0 1.3 %collective-permute-start = (bf16[2,608,256]{2,1,0:T(8,128)(2,1)}, bf16[2,608,256]{2,1,0:T(8,128)(2,1)}, u32[]{:S(2)}, u32[]{:S(2)}) collective-permute-start(bf16[2,608,256]{2,1,0:T(8,128)(2,1)} %pad_select_fusion), channel_id=1, source_target_pairs={{8,24},{16,0},{9,25},{17,1},{10,26},{18,2},{11,27},{19,3},{12,28},... | collective-permute-start | bytes 1867784 | tf_op jit(solution)/shard_map/ppermute | solution.py:231
  5.3 1.1 %pack.3 = (bf16[2,608,256]{2,1,0:T(8,128)(2,1)}, bf16[2,544,256]{2,1,0:T(8,128)(2,1)}) custom-call(bf16[4,16,64,256]{3,2,1,0:T(8,128)(2,1)S(1)} %bitcast.24), custom_call_target="tpu_custom_call" | custom-call | bytes 2359296 | tf_op jit(solution)/shard_map/pack/pallas_call | solution.py:70
  6.4 7.4 %collective-permute-start.3 = (bf16[2,608,256]{2,1,0:T(8,128)(2,1)}, bf16[2,608,256]{2,1,0:T(8,128)(2,1)}, u32[]{:S(2)}, u32[]{:S(2)}) collective-permute-start(bf16[2,608,256]{2,1,0:T(8,128)(2,1)} %get-tuple-element.18), channel_id=1, source_target_pairs={{0,8},{8,16},{16,24},{1,9},{9,17},{17,25},{2,10},{10,18},{18,26},{... | collective-permute-start | bytes 1867784 | tf_op jit(solution)/shard_map/ppermute | solution.py:234
  13.8 1.3 %collective-permute-start.4 = (bf16[2,544,256]{2,1,0:T(8,128)(2,1)}, bf16[2,544,256]{2,1,0:T(8,128)(2,1)}, u32[]{:S(2)}, u32[]{:S(2)}) collective-permute-start(bf16[2,544,256]{2,1,0:T(8,128)(2,1)} %get-tuple-element.19), channel_id=1, source_target_pairs={{8,0},{16,8},{24,16},{9,1},{17,9},{25,17},{10,2},{18,10},{26,18},{... | collective-permute-start | bytes 1671176 | tf_op jit(solution)/shard_map/ppermute | solution.py:234
  15.1 0.0 copy-done.3
  15.1 0.1 add_select_fusion
  15.2 0.0 copy-done.2
  15.2 0.3 fusion.11
  15.6 0.0 copy-done
  15.6 0.0 copy-done.1
  15.6 1.2 %copy.14 = bf16[64,33,64]{2,1,0:T(8,128)(2,1)} copy(bf16[64,33,64]{2,0,1:T(8,128)(2,1)S(1)} %fusion.11) | data formatting | bytes 540672 | tf_op jit(solution)/shard_map/transpose | solution.py:40
  16.8 1.5 %reshape.70 = bf16[64,2112]{1,0:T(8,128)(2,1)S(1)} reshape(bf16[64,33,64]{2,1,0:T(8,128)(2,1)} %copy.14) | data formatting | bytes 540672 | tf_op jit(solution)/shard_map/reshape | solution.py:40
  18.2 0.2 fusion.7.matrix_ref
  18.5 1.0 %fusion.12 = (s32[1,16,4,256]{3,2,1,0:T(4,128)S(1)}, s32[1,16,4,256]{3,2,1,0:T(4,128)S(1)}) fusion(s32[16,4,256]{2,1,0:T(4,128)} %param.6), kind=kLoop, calls=%fused_computation.28 | loop fusion | bytes 196608 | tf_op jit(solution)/shard_map/stack | solution.py:196
  19.5 1.9 %collective-permute-done = bf16[2,608,256]{2,1,0:T(8,128)(2,1)} collective-permute-done((bf16[2,608,256]{2,1,0:T(8,128)(2,1)}, bf16[2,608,256]{2,1,0:T(8,128)(2,1)}, u32[]{:S(2)}, u32[]{:S(2)}) %collective-permute-start) | collective-permute-done | bytes 622624 | tf_op jit(solution)/shard_map/ppermute | solution.py:231
  21.4 3.5 %collective-permute-start.1 = (bf16[2,608,256]{2,1,0:T(8,128)(2,1)}, bf16[2,608,256]{2,1,0:T(8,128)(2,1)}, u32[]{:S(2)}, u32[]{:S(2)}) collective-permute-start(bf16[2,608,256]{2,1,0:T(8,128)(2,1)} %collective-permute-done), channel_id=1, source_target_pairs={{0,8},{24,16},{1,9},{25,17},{2,10},{26,18},{3,11},{27,19},{4,12},{... | collective-permute-start | bytes 1867784 | tf_op jit(solution)/shard_map/ppermute | solution.py:237
  24.9 0.9 pad_add_fusion
  25.8 0.8 copy.11
  26.5 1.3 %collective-permute-start.5 = (bf16[2,544,256]{2,1,0:T(8,128)(2,1)}, bf16[2,544,256]{2,1,0:T(8,128)(2,1)}, u32[]{:S(2)}, u32[]{:S(2)}) collective-permute-start(bf16[2,544,256]{2,1,0:T(8,128)(2,1)} %copy-done.1), channel_id=1, source_target_pairs={{8,0},{24,16},{9,1},{25,17},{10,2},{26,18},{11,3},{27,19},{12,4},{... | collective-permute-start | bytes 1671176 | tf_op jit(solution)/shard_map/ppermute | solution.py:239
  27.8 5.6 %collective-permute-start.2 = (bf16[2,608,256]{2,1,0:T(8,128)(2,1)}, bf16[2,608,256]{2,1,0:T(8,128)(2,1)}, u32[]{:S(2)}, u32[]{:S(2)}) collective-permute-start(bf16[2,608,256]{2,1,0:T(8,128)(2,1)} %copy-done), channel_id=1, source_target_pairs={{0,8},{16,24},{1,9},{17,25},{2,10},{18,26},{3,11},{19,27},{4,12},{... | collective-permute-start | bytes 1867784 | tf_op jit(solution)/shard_map/ppermute | solution.py:238
  33.5 3.0 %convolution_bitcast_fusion = f32[16,4,9,3,256]{4,2,1,0,3:T(8,128)} fusion(s32[3,16,4,256]{3,2,1,0:T(4,128)S(1)} %pad_add_fusion, f32[8,9,3,1,1]{0,2,1,4,3:T(4,128)S(1)} %bitcast.36), kind=kOutput, calls=%fused_computation.13 | convolution fusion | flops 42860544 | bytes 1966944 | tf_op jit(solution)/shard_map/qij,jzxqy->zxijy/dot_general | solution.py:201
  36.5 2.9 %copy.13 = f32[16,4,9,3,256]{4,0,3,2,1:T(8,128)S(1)} copy(f32[16,4,9,3,256]{4,2,1,0,3:T(8,128)} %convolution_bitcast_fusion) | data formatting | bytes 3538944 | tf_op jit(solution)/shard_map/qij,jzxqy->zxijy/transpose | solution.py:201
  39.4 1.0 %copy.18.weight_ref = f32[16,4,27,256]{3,2,1,0:T(8,128)S(1)} copy(f32[16,4,27,256]{3,0,2,1:T(8,128)S(1)} %bitcast.34) | data formatting | bytes 3538944 | tf_op jit(solution)/shard_map/reshape | solution.py:207
  40.5 0.0 collective-permute-done.4.below_ref
  40.5 0.0 collective-permute-done.3.above_ref
  40.5 4.0 %slant_stack.2 = bf16[2,1024,256]{2,1,0:T(8,128)(2,1)S(1)} custom-call(bf16[256,2304]{1,0:T(8,128)(2,1)S(1)} %fusion.7.matrix_ref, bf16[2,608,256]{2,1,0:T(8,128)(2,1)} %collective-permute-done.3.above_ref, bf16[4,16,64,256]{3,2,1,0:T(8,128)(2,1)S(1)} %bitcast.25, bf16[2,544,256]{2,1,0:T(8,128)(2,1)} %collective-permute-done.4.below_ref), custom_call_target="tpu_custom_call" | custom-call | flops 2415919104 | bytes 4587520 | tf_op jit(solution)/shard_map/slant_stack/pallas_call | solution.py:120
  44.5 5.5 %collective-permute-start.8 = (bf16[2,1024,256]{2,1,0:T(8,128)(2,1)S(1)}, bf16[2,1024,256]{2,1,0:T(8,128)(2,1)S(1)}, u32[]{:S(2)}, u32[]{:S(2)}) collective-permute-start(bf16[2,1024,256]{2,1,0:T(8,128)(2,1)S(1)} %slant_stack.2), channel_id=1, source_target_pairs={{0,1},{1,2},{2,3},{3,4},{4,5},{5,6},{6,7},{8,9},{9,10},{10,11},{11... | collective-permute-start | bytes 3145736 | tf_op jit(solution)/shard_map/ppermute | solution.py:288
  49.9 1.9 %collective-permute-start.9 = (bf16[2,1024,256]{2,1,0:T(8,128)(2,1)S(1)}, bf16[2,1024,256]{2,1,0:T(8,128)(2,1)S(1)}, u32[]{:S(2)}, u32[]{:S(2)}) collective-permute-start(bf16[2,1024,256]{2,1,0:T(8,128)(2,1)S(1)} %slant_stack.2), channel_id=1, source_target_pairs={{1,0},{2,1},{3,2},{4,3},{5,4},{6,5},{7,6},{9,8},{10,9},{11,10},{12... | collective-permute-start | bytes 3145736 | tf_op jit(solution)/shard_map/ppermute | solution.py:289
  51.9 3.8 %smooth.3.refs_3_ = f32[4,16,64,256]{3,2,1,0:T(8,128)S(1)} custom-call(f32[16,4,27,256]{3,2,1,0:T(8,128)S(1)} %copy.18.weight_ref, bf16[2,16,64,256]{3,2,1,0:T(8,128)(2,1)S(1)} %bitcast.28), custom_call_target="tpu_custom_call" | custom-call | flops 419430400 | bytes 8388608 | tf_op jit(solution)/shard_map/smooth/pallas_call | solution.py:174
  55.7 0.0 collective-permute-done.5
  55.7 0.0 collective-permute-done.1
  55.7 1.3 %slice_select_fusion.below_ref = bf16[2,544,256]{2,1,0:T(8,128)(2,1)S(1)} fusion(bf16[2,544,256]{2,1,0:T(8,128)(2,1)} %collective-permute-done.5, bf16[2,608,256]{2,1,0:T(8,128)(2,1)} %collective-permute-done.1, pred[]{:T(512)S(6)} %eq.24), kind=kLoop, calls=%fused_computation.23 | loop fusion | flops 278528 | bytes 1671169 | tf_op jit(solution)/shard_map/jit(_where)/select_n | solution.py:241
  57.0 0.0 collective-permute-done.2
  57.0 1.2 %broadcast_select_fusion.above_ref = bf16[2,608,256]{2,1,0:T(8,128)(2,1)S(1)} fusion(bf16[2,608,256]{2,1,0:T(8,128)(2,1)} %collective-permute-done.1, bf16[2,608,256]{2,1,0:T(8,128)(2,1)} %collective-permute-done.2, pred[]{:T(512)S(6)} %eq.23), kind=kLoop, calls=%fused_computation.22 | loop fusion | flops 311296 | bytes 1867777 | tf_op jit(solution)/shard_map/jit(_where)/select_n | solution.py:240
  58.2 2.9 %slant_stack.3 = bf16[2,1024,256]{2,1,0:T(8,128)(2,1)S(1)} custom-call(bf16[256,2304]{1,0:T(8,128)(2,1)S(1)} %fusion.7.matrix_ref, bf16[2,608,256]{2,1,0:T(8,128)(2,1)S(1)} %broadcast_select_fusion.above_ref, bf16[4,16,64,256]{3,2,1,0:T(8,128)(2,1)S(1)} %bitcast.26, bf16[2,544,256]{2,1,0:T(8,128)(2,1)S(1)} %slice_select_fusion.below_ref), custom_call_target="tpu_custom_call" | custom-call | flops 2415919104 | bytes 4587520 | tf_op jit(solution)/shard_map/slant_stack/pallas_call | solution.py:120
  61.1 1.9 %collective-permute-start.7 = (bf16[2,1024,256]{2,1,0:T(8,128)(2,1)S(1)}, bf16[2,1024,256]{2,1,0:T(8,128)(2,1)S(1)}, u32[]{:S(2)}, u32[]{:S(2)}) collective-permute-start(bf16[2,1024,256]{2,1,0:T(8,128)(2,1)S(1)} %slant_stack.3), channel_id=1, source_target_pairs={{1,0},{2,1},{3,2},{4,3},{5,4},{6,5},{7,6},{9,8},{10,9},{11,10},{12... | collective-permute-start | bytes 3145736 | tf_op jit(solution)/shard_map/ppermute | solution.py:289
  63.0 3.6 %collective-permute-start.6 = (bf16[2,1024,256]{2,1,0:T(8,128)(2,1)S(1)}, bf16[2,1024,256]{2,1,0:T(8,128)(2,1)S(1)}, u32[]{:S(2)}, u32[]{:S(2)}) collective-permute-start(bf16[2,1024,256]{2,1,0:T(8,128)(2,1)S(1)} %slant_stack.3), channel_id=1, source_target_pairs={{0,1},{1,2},{2,3},{3,4},{4,5},{5,6},{6,7},{8,9},{9,10},{10,11},{11... | collective-permute-start | bytes 3145736 | tf_op jit(solution)/shard_map/ppermute | solution.py:288
  66.7 0.0 collective-permute-done.8
  66.7 0.0 collective-permute-done.9
  66.7 5.8 %smooth.4.refs_2_ = f32[4,16,64,256]{3,2,1,0:T(8,128)S(1)} custom-call(f32[16,4,27,256]{3,2,1,0:T(8,128)S(1)} %copy.18.weight_ref, bf16[2,16,64,256]{3,2,1,0:T(8,128)(2,1)S(1)} %bitcast.31, bf16[2,16,64,256]{3,2,1,0:T(8,128)(2,1)S(1)} %bitcast.33, bf16[2,16,64,256]{3,2,1,0:T(8,128)(2,1)S(1)} %bitcast.32, f32[4,16,64,256]{3,2,1,0:T(8,128)S(1)} %smooth.3.refs_3_), custom_call_target="tpu_custom_call" | custom-call | flops 943718400 | bytes 8388608 | tf_op jit(solution)/shard_map/smooth/pallas_call | solution.py:174
  72.5 4.8 %collective-permute-done.7 = bf16[2,1024,256]{2,1,0:T(8,128)(2,1)S(1)} collective-permute-done((bf16[2,1024,256]{2,1,0:T(8,128)(2,1)S(1)}, bf16[2,1024,256]{2,1,0:T(8,128)(2,1)S(1)}, u32[]{:S(2)}, u32[]{:S(2)}) %collective-permute-start.7) | collective-permute-done | bytes 1048608 | tf_op jit(solution)/shard_map/ppermute | solution.py:289
  77.3 1.1 %collective-permute-done.6 = bf16[2,1024,256]{2,1,0:T(8,128)(2,1)S(1)} collective-permute-done((bf16[2,1024,256]{2,1,0:T(8,128)(2,1)S(1)}, bf16[2,1024,256]{2,1,0:T(8,128)(2,1)S(1)}, u32[]{:S(2)}, u32[]{:S(2)}) %collective-permute-start.6) | collective-permute-done | bytes 1048608 | tf_op jit(solution)/shard_map/ppermute | solution.py:288
  78.4 4.1 %smooth.5 = bf16[4,16,64,256]{3,2,1,0:T(8,128)(2,1)S(1)} custom-call(f32[16,4,27,256]{3,2,1,0:T(8,128)S(1)} %copy.18.weight_ref, bf16[2,16,64,256]{3,2,1,0:T(8,128)(2,1)S(1)} %bitcast.30, bf16[2,16,64,256]{3,2,1,0:T(8,128)(2,1)S(1)} %bitcast.29, f32[4,16,64,256]{3,2,1,0:T(8,128)S(1)} %smooth.4.refs_2_), custom_call_target="tpu_custom_call" | custom-call | flops 524288000 | bytes 8388608 | tf_op jit(solution)/shard_map/smooth/pallas_call | solution.py:174
  82.5 2.9 %copy.19 = bf16[64,16,4,256]{3,2,1,0:T(4,128)(2,1)} copy(bf16[64,16,4,256]{3,0,1,2:T(8,128)(2,1)S(1)} %bitcast.27) | data formatting | bytes 4194304 | tf_op jit(solution)/shard_map/transpose | solution.py:293
  (2 shorter events, 0.0 us)
Async XLA Ops:
  2.9 12.6 %copy-start = (bf16[2,608,256]{2,1,0:T(8,128)(2,1)}, bf16[2,608,256]{2,1,0:T(8,128)(2,1)S(1)}, u32[]{:S(2)}) copy-start(bf16[2,608,256]{2,1,0:T(8,128)(2,1)S(1)} %get-tuple-element.17) | copy-start | bytes 1867780
  2.9 12.6 %copy-start.1 = (bf16[2,544,256]{2,1,0:T(8,128)(2,1)}, bf16[2,544,256]{2,1,0:T(8,128)(2,1)S(1)}, u32[]{:S(2)}) copy-start(bf16[2,544,256]{2,1,0:T(8,128)(2,1)S(1)} %get-tuple-element.21) | copy-start | bytes 1671172
  2.9 12.1 %copy-start.3 = (s32[64]{0:T(128)S(1)}, s32[64]{0:T(128)}, u32[]{:S(2)}) copy-start(s32[64]{0:T(128)} %param.8) | copy-start | bytes 772
  3.0 12.2 %copy-start.2 = (bf16[64,64,33]{1,0,2:T(8,128)(2,1)S(1)}, bf16[64,64,33]{1,0,2:T(8,128)(2,1)}, u32[]{:S(2)}) copy-start(bf16[64,64,33]{1,0,2:T(8,128)(2,1)} %param.7) | copy-start | bytes 811012
  4.0 17.4 %collective-permute-start = (bf16[2,608,256]{2,1,0:T(8,128)(2,1)}, bf16[2,608,256]{2,1,0:T(8,128)(2,1)}, u32[]{:S(2)}, u32[]{:S(2)}) collective-permute-start(bf16[2,608,256]{2,1,0:T(8,128)(2,1)} %pad_select_fusion), channel_id=1, source_target_pairs={{8,24},{16,0},{9,25},{17,1},{10,26},{18,2},{11,27},{19,3},{12,28},... | collective-permute-start | bytes 1867784 | tf_op jit(solution)/shard_map/ppermute | solution.py:231
  6.4 34.1 %collective-permute-start.3 = (bf16[2,608,256]{2,1,0:T(8,128)(2,1)}, bf16[2,608,256]{2,1,0:T(8,128)(2,1)}, u32[]{:S(2)}, u32[]{:S(2)}) collective-permute-start(bf16[2,608,256]{2,1,0:T(8,128)(2,1)} %get-tuple-element.18), channel_id=1, source_target_pairs={{0,8},{8,16},{16,24},{1,9},{9,17},{17,25},{2,10},{10,18},{18,26},{... | collective-permute-start | bytes 1867784 | tf_op jit(solution)/shard_map/ppermute | solution.py:234
  13.8 26.7 %collective-permute-start.4 = (bf16[2,544,256]{2,1,0:T(8,128)(2,1)}, bf16[2,544,256]{2,1,0:T(8,128)(2,1)}, u32[]{:S(2)}, u32[]{:S(2)}) collective-permute-start(bf16[2,544,256]{2,1,0:T(8,128)(2,1)} %get-tuple-element.19), channel_id=1, source_target_pairs={{8,0},{16,8},{24,16},{9,1},{17,9},{25,17},{10,2},{18,10},{26,18},{... | collective-permute-start | bytes 1671176 | tf_op jit(solution)/shard_map/ppermute | solution.py:234
  21.4 34.3 %collective-permute-start.1 = (bf16[2,608,256]{2,1,0:T(8,128)(2,1)}, bf16[2,608,256]{2,1,0:T(8,128)(2,1)}, u32[]{:S(2)}, u32[]{:S(2)}) collective-permute-start(bf16[2,608,256]{2,1,0:T(8,128)(2,1)} %collective-permute-done), channel_id=1, source_target_pairs={{0,8},{24,16},{1,9},{25,17},{2,10},{26,18},{3,11},{27,19},{4,12},{... | collective-permute-start | bytes 1867784 | tf_op jit(solution)/shard_map/ppermute | solution.py:237
  26.5 29.2 %collective-permute-start.5 = (bf16[2,544,256]{2,1,0:T(8,128)(2,1)}, bf16[2,544,256]{2,1,0:T(8,128)(2,1)}, u32[]{:S(2)}, u32[]{:S(2)}) collective-permute-start(bf16[2,544,256]{2,1,0:T(8,128)(2,1)} %copy-done.1), channel_id=1, source_target_pairs={{8,0},{24,16},{9,1},{25,17},{10,2},{26,18},{11,3},{27,19},{12,4},{... | collective-permute-start | bytes 1671176 | tf_op jit(solution)/shard_map/ppermute | solution.py:239
  27.8 29.2 %collective-permute-start.2 = (bf16[2,608,256]{2,1,0:T(8,128)(2,1)}, bf16[2,608,256]{2,1,0:T(8,128)(2,1)}, u32[]{:S(2)}, u32[]{:S(2)}) collective-permute-start(bf16[2,608,256]{2,1,0:T(8,128)(2,1)} %copy-done), channel_id=1, source_target_pairs={{0,8},{16,24},{1,9},{17,25},{2,10},{18,26},{3,11},{19,27},{4,12},{... | collective-permute-start | bytes 1867784 | tf_op jit(solution)/shard_map/ppermute | solution.py:238
  44.5 22.2 %collective-permute-start.8 = (bf16[2,1024,256]{2,1,0:T(8,128)(2,1)S(1)}, bf16[2,1024,256]{2,1,0:T(8,128)(2,1)S(1)}, u32[]{:S(2)}, u32[]{:S(2)}) collective-permute-start(bf16[2,1024,256]{2,1,0:T(8,128)(2,1)S(1)} %slant_stack.2), channel_id=1, source_target_pairs={{0,1},{1,2},{2,3},{3,4},{4,5},{5,6},{6,7},{8,9},{9,10},{10,11},{11... | collective-permute-start | bytes 3145736 | tf_op jit(solution)/shard_map/ppermute | solution.py:288
  49.9 16.7 %collective-permute-start.9 = (bf16[2,1024,256]{2,1,0:T(8,128)(2,1)S(1)}, bf16[2,1024,256]{2,1,0:T(8,128)(2,1)S(1)}, u32[]{:S(2)}, u32[]{:S(2)}) collective-permute-start(bf16[2,1024,256]{2,1,0:T(8,128)(2,1)S(1)} %slant_stack.2), channel_id=1, source_target_pairs={{1,0},{2,1},{3,2},{4,3},{5,4},{6,5},{7,6},{9,8},{10,9},{11,10},{12... | collective-permute-start | bytes 3145736 | tf_op jit(solution)/shard_map/ppermute | solution.py:289
  61.1 16.2 %collective-permute-start.7 = (bf16[2,1024,256]{2,1,0:T(8,128)(2,1)S(1)}, bf16[2,1024,256]{2,1,0:T(8,128)(2,1)S(1)}, u32[]{:S(2)}, u32[]{:S(2)}) collective-permute-start(bf16[2,1024,256]{2,1,0:T(8,128)(2,1)S(1)} %slant_stack.3), channel_id=1, source_target_pairs={{1,0},{2,1},{3,2},{4,3},{5,4},{6,5},{7,6},{9,8},{10,9},{11,10},{12... | collective-permute-start | bytes 3145736 | tf_op jit(solution)/shard_map/ppermute | solution.py:289
  63.0 15.4 %collective-permute-start.6 = (bf16[2,1024,256]{2,1,0:T(8,128)(2,1)S(1)}, bf16[2,1024,256]{2,1,0:T(8,128)(2,1)S(1)}, u32[]{:S(2)}, u32[]{:S(2)}) collective-permute-start(bf16[2,1024,256]{2,1,0:T(8,128)(2,1)S(1)} %slant_stack.3), channel_id=1, source_target_pairs={{0,1},{1,2},{2,3},{3,4},{4,5},{5,6},{6,7},{8,9},{9,10},{10,11},{11... | collective-permute-start | bytes 3145736 | tf_op jit(solution)/shard_map/ppermute | solution.py:288
